TPU v7x, 32 devices: a whole 2x2x4 slice. The times are simulated.
32 devices in a mesh: tok: 4 (over y, x), cent: 8 (over z, core).
Axes of the slice: x: 2, y: 2, z: 4, core: 2. Of those that a mesh axis runs over, the one named last changes fastest.
Arguments:
- tokens: bfloat16 [8192, 128], P('tok'), may hold values from -80 to 80
- centroids: bfloat16 [262144, 128], P('cent'), may hold values from -0.6 to 0.6
Outputs:
- updated: float32 [262144, 128], P('cent')
- masses: float32 [262144], P('cent')
All inputs are finite; a program needn't handle non-finite values.
Results may differ from a plain program's by a relative error of at most 0.0028.
Values may be sent and summed in bfloat16 or wider, within the bound.
No kernel may reach another device: no remote copies, remote signals or barrier semaphores. Data moves between devices by JAX's collectives and lax.ppermute only.
A program may use at most 128 MiB of HBM per device.

v0:
```python
import jax
import jax.numpy as jnp
from jax import lax
from jax.sharding import PartitionSpec as P

inverse_temp = 2.0
prior_weight = 0.05


def joined(value, axis, combine):
    everything = jax.tree.map(lambda part: lax.all_gather(part, axis), value)
    leading = jax.tree.map(lambda part: part[0], everything)

    def step(k, so_far):
        return combine(so_far, jax.tree.map(lambda part: part[k], everything))

    return lax.fori_loop(1, lax.axis_size(axis), step, leading)


def combine_stats(earlier, later):
    peak = jnp.maximum(earlier[0], later[0])
    return (peak, earlier[1] * jnp.exp(earlier[0] - peak) + later[1] * jnp.exp(later[0] - peak))


def local_stats(tok_block, cent_blocks):

    def first_pass(running, cent_block):
        row_max, row_sum = running
        logits = jnp.dot(tok_block, cent_block.T, preferred_element_type=jnp.float32) * inverse_temp
        new_max = jnp.maximum(row_max, jnp.max(logits, axis=1))
        row_sum = row_sum * jnp.exp(row_max - new_max) + jnp.sum(
            jnp.exp(logits - new_max[:, None]), axis=1
        )
        return ((new_max, row_sum), None)

    rows = tok_block.shape[0]
    begin = (jnp.full((rows,), -1e30, jnp.float32), jnp.zeros((rows,), jnp.float32))
    result, _ = lax.scan(first_pass, begin, cent_blocks)
    return result


def weigh_rows(tok_block, cent_blocks, global_max, global_sum):

    def second_pass(unused, cent_block):
        logits = jnp.dot(tok_block, cent_block.T, preferred_element_type=jnp.float32) * inverse_temp
        weights = (jnp.exp(logits - global_max[:, None]) / global_sum[:, None]).astype(jnp.bfloat16)
        block_sums = jnp.einsum("tc,td->cd", weights, tok_block, preferred_element_type=jnp.float32)
        return (unused, (block_sums, jnp.sum(weights.astype(jnp.float32), axis=0)))

    _, result = lax.scan(second_pass, 0, cent_blocks)
    return result


def local(tokens, centroids):
    tok_count, width = tokens.shape
    cent_count = centroids.shape[0]
    share_rows = cent_count // lax.axis_size("tok")
    own = lax.dynamic_slice_in_dim(centroids, lax.axis_index("tok") * share_rows, share_rows, 0)
    every_tok = lax.all_gather(tokens, "tok", axis=0, tiled=True)
    all_count = every_tok.shape[0]
    block_rows = min(512, all_count)
    cent_rows = min(2048, share_rows)
    tok_blocks = every_tok.reshape(all_count // block_rows, block_rows, width)
    own_blocks = own.reshape(share_rows // cent_rows, cent_rows, width)
    local_max, local_sum = lax.map(lambda blk: local_stats(blk, own_blocks), tok_blocks)
    global_max, global_sum = joined((local_max, local_sum), ("tok", "cent"), combine_stats)

    def grid_step(accum, inputs):
        tok_block, block_max, block_sum = inputs
        block_sums, block_mass = weigh_rows(tok_block, own_blocks, block_max, block_sum)
        return ((accum[0] + block_sums, accum[1] + block_mass), None)

    start = (jnp.zeros(own_blocks.shape, jnp.float32), jnp.zeros(own_blocks.shape[:2], jnp.float32))
    (share_sums, share_mass), _ = lax.scan(grid_step, start, (tok_blocks, global_max, global_sum))
    share_sums = share_sums.reshape(share_rows, width)
    share_mass = share_mass.reshape(share_rows)
    share_new = (share_sums + prior_weight * own.astype(jnp.float32)) / (
        share_mass[:, None] + prior_weight
    )
    updated, masses = (
        lax.all_gather(share_new, "tok", axis=0, tiled=True),
        lax.all_gather(share_mass, "tok", axis=0, tiled=True),
    )
    return (updated, masses)


def solution(mesh):
    placed = (P("tok", None), P("cent", None))
    return jax.shard_map(
        local, mesh=mesh, in_specs=placed, out_specs=(P("cent", None), P("cent")), check_vma=False
    )
```

profile of v0, /device:TPU:0, one launch (start us, length us, event | category | flops | bytes accessed | tf_op | source)
XLA Modules:
  0.0 936.0 jit_solution(2062532660733547284)
XLA Ops:
  11.0 36.8 %all-gather.7.cloned.1.call-done = bf16[8192,128]{1,0:T(8,128)(2,1)} async-done(((bf16[2048,128]{1,0:T(8,128)(2,1)}), bf16[8192,128]{1,0:T(8,128)(2,1)}) %all-gather.7.cloned.1.call-update) | async-done | bytes 2097168 | tf_op jit(solution)/shard_map/all_gather | solution.py:59
  47.9 202.4 %while.76 = (s32[]{:T(128)}, f32[16,512]{1,0:T(8,128)S(1)}, f32[16,512]{1,0:T(8,128)}, bf16[16,512,128]{2,1,0:T(8,128)(2,1)}, bf16[4,2048,128]{2,1,0:T(8,128)(2,1)}, /*index=5*/s32[]{:T(128)}, s32[]{:T(128)}) while((s32[]{:T(128)}, f32[16,512]{1,0:T(8,128)S(1)}, f32[16,512]{1,0:T(8,128)}, bf16[16,512,128]{2,1,0:T(8,128)(2,1)}, ...), condition=%wide.region_5.6_spmd.clone, body=%wide.region_0.5_spmd.sunk.clone | while | flops 273680896 | bytes 9341189 | solution.py:65
  61.5 10.3 %while.75 = (s32[]{:T(128)}, f32[512]{0:T(512)S(1)}, f32[512]{0:T(512)S(1)}, bf16[4,2048,128]{2,1,0:T(8,128)(2,1)}, bf16[512,128]{1,0:T(8,128)(2,1)S(1)}, /*index=5*/s32[]{:T(128)}, s32[]{:T(128)}) while((s32[]{:T(128)}, f32[512]{0:T(512)S(1)}, f32[512]{0:T(512)S(1)}, bf16[4,2048,128]{2,1,0:T(8,128)(2,1)}, ...), condition=%wide.region_4.4_spmd.clone, body=%wide.region_1.3_spmd.clone.sunk | while | flops 273680896 | bytes 9070692 | solution.py:38
  74.1 10.3 %while.75 = (s32[]{:T(128)}, f32[512]{0:T(512)S(1)}, f32[512]{0:T(512)S(1)}, bf16[4,2048,128]{2,1,0:T(8,128)(2,1)}, bf16[512,128]{1,0:T(8,128)(2,1)S(1)}, /*index=5*/s32[]{:T(128)}, s32[]{:T(128)}) while((s32[]{:T(128)}, f32[512]{0:T(512)S(1)}, f32[512]{0:T(512)S(1)}, bf16[4,2048,128]{2,1,0:T(8,128)(2,1)}, ...), condition=%wide.region_4.4_spmd.clone, body=%wide.region_1.3_spmd.clone.sunk | while | flops 273680896 | bytes 9070692 | solution.py:38
  86.8 10.3 %while.75 = (s32[]{:T(128)}, f32[512]{0:T(512)S(1)}, f32[512]{0:T(512)S(1)}, bf16[4,2048,128]{2,1,0:T(8,128)(2,1)}, bf16[512,128]{1,0:T(8,128)(2,1)S(1)}, /*index=5*/s32[]{:T(128)}, s32[]{:T(128)}) while((s32[]{:T(128)}, f32[512]{0:T(512)S(1)}, f32[512]{0:T(512)S(1)}, bf16[4,2048,128]{2,1,0:T(8,128)(2,1)}, ...), condition=%wide.region_4.4_spmd.clone, body=%wide.region_1.3_spmd.clone.sunk | while | flops 273680896 | bytes 9070692 | solution.py:38
  99.4 10.3 %while.75 = (s32[]{:T(128)}, f32[512]{0:T(512)S(1)}, f32[512]{0:T(512)S(1)}, bf16[4,2048,128]{2,1,0:T(8,128)(2,1)}, bf16[512,128]{1,0:T(8,128)(2,1)S(1)}, /*index=5*/s32[]{:T(128)}, s32[]{:T(128)}) while((s32[]{:T(128)}, f32[512]{0:T(512)S(1)}, f32[512]{0:T(512)S(1)}, bf16[4,2048,128]{2,1,0:T(8,128)(2,1)}, ...), condition=%wide.region_4.4_spmd.clone, body=%wide.region_1.3_spmd.clone.sunk | while | flops 273680896 | bytes 9070692 | solution.py:38
  162.6 10.3 %while.75 = (s32[]{:T(128)}, f32[512]{0:T(512)S(1)}, f32[512]{0:T(512)S(1)}, bf16[4,2048,128]{2,1,0:T(8,128)(2,1)}, bf16[512,128]{1,0:T(8,128)(2,1)S(1)}, /*index=5*/s32[]{:T(128)}, s32[]{:T(128)}) while((s32[]{:T(128)}, f32[512]{0:T(512)S(1)}, f32[512]{0:T(512)S(1)}, bf16[4,2048,128]{2,1,0:T(8,128)(2,1)}, ...), condition=%wide.region_4.4_spmd.clone, body=%wide.region_1.3_spmd.clone.sunk | while | flops 273680896 | bytes 9070692 | solution.py:38
  175.3 10.3 %while.75 = (s32[]{:T(128)}, f32[512]{0:T(512)S(1)}, f32[512]{0:T(512)S(1)}, bf16[4,2048,128]{2,1,0:T(8,128)(2,1)}, bf16[512,128]{1,0:T(8,128)(2,1)S(1)}, /*index=5*/s32[]{:T(128)}, s32[]{:T(128)}) while((s32[]{:T(128)}, f32[512]{0:T(512)S(1)}, f32[512]{0:T(512)S(1)}, bf16[4,2048,128]{2,1,0:T(8,128)(2,1)}, ...), condition=%wide.region_4.4_spmd.clone, body=%wide.region_1.3_spmd.clone.sunk | while | flops 273680896 | bytes 9070692 | solution.py:38
  187.9 10.3 %while.75 = (s32[]{:T(128)}, f32[512]{0:T(512)S(1)}, f32[512]{0:T(512)S(1)}, bf16[4,2048,128]{2,1,0:T(8,128)(2,1)}, bf16[512,128]{1,0:T(8,128)(2,1)S(1)}, /*index=5*/s32[]{:T(128)}, s32[]{:T(128)}) while((s32[]{:T(128)}, f32[512]{0:T(512)S(1)}, f32[512]{0:T(512)S(1)}, bf16[4,2048,128]{2,1,0:T(8,128)(2,1)}, ...), condition=%wide.region_4.4_spmd.clone, body=%wide.region_1.3_spmd.clone.sunk | while | flops 273680896 | bytes 9070692 | solution.py:38
  200.6 10.3 %while.75 = (s32[]{:T(128)}, f32[512]{0:T(512)S(1)}, f32[512]{0:T(512)S(1)}, bf16[4,2048,128]{2,1,0:T(8,128)(2,1)}, bf16[512,128]{1,0:T(8,128)(2,1)S(1)}, /*index=5*/s32[]{:T(128)}, s32[]{:T(128)}) while((s32[]{:T(128)}, f32[512]{0:T(512)S(1)}, f32[512]{0:T(512)S(1)}, bf16[4,2048,128]{2,1,0:T(8,128)(2,1)}, ...), condition=%wide.region_4.4_spmd.clone, body=%wide.region_1.3_spmd.clone.sunk | while | flops 273680896 | bytes 9070692 | solution.py:38
  251.7 53.1 %all-gather.11.cloned.1.call-done = f32[512,512]{1,0:T(8,128)} async-done(((f32[16,512]{1,0:T(8,128)}), f32[512,512]{1,0:T(8,128)}) %all-gather.11.cloned.1.call-update) | async-done | bytes 1048592 | tf_op jit(solution)/shard_map/all_gather | solution.py:11
  305.6 55.6 %all-gather.13.cloned.1.call-done = f32[512,512]{1,0:T(8,128)} async-done(((f32[16,512]{1,0:T(8,128)}), f32[512,512]{1,0:T(8,128)}) %all-gather.13.cloned.1.call-update) | async-done | bytes 1048592 | tf_op jit(solution)/shard_map/all_gather | solution.py:11
  362.0 25.9 %while.77 = (s32[]{:T(128)}, f32[16,512]{1,0:T(8,128)S(1)}, f32[16,512]{1,0:T(8,128)S(1)}, f32[32,16,512]{2,1,0:T(8,128)}, f32[32,16,512]{2,1,0:T(8,128)}) while((s32[]{:T(128)}, f32[16,512]{1,0:T(8,128)S(1)}, f32[16,512]{1,0:T(8,128)S(1)}, f32[32,16,512]{2,1,0:T(8,128)}, f32[32,16,512]{2,1,0:T(8,128)}) %tuple.162), condition=%wide.region_7.8_spmd.clone, body=%wide.region_6.7_spmd.sunk.clone | while | flops 49157 | bytes 196707 | solution.py:17
  387.9 368.2 %while.79 = (s32[]{:T(128)}, f32[4,2048,128]{2,1,0:T(8,128)}, f32[4,2048]{1,0:T(4,128)S(1)}, bf16[16,512,128]{2,1,0:T(8,128)(2,1)}, f32[16,512]{1,0:T(8,128)S(1)...) while((s32[]{:T(128)}, f32[4,2048,128]{2,1,0:T(8,128)}, ...), condition=%wide.region_12.13_spmd.clone.clone, body=%wide.region_8.12_spmd.clone.sunk.clone | while | flops 545273856 | bytes 19009856 | solution.py:74
  388.8 16.2 %while.78 = (s32[]{:T(128)}, f32[4,2048,128]{2,1,0:T(8,128)}, f32[4,2048]{1,0:T(4,128)S(1)}, bf16[4,2048,128]{2,1,0:T(8,128)(2,1)}, bf16[512,128]{1,0:T(8,128)(2...) while((s32[]{:T(128)}, f32[4,2048,128]{2,1,0:T(8,128)}, ...), condition=%wide.region_11.11_spmd, body=%wide.region_9.10_spmd.sunk | while | flops 543160320 | bytes 6058097 | solution.py:50
  410.6 16.2 %while.78 = (s32[]{:T(128)}, f32[4,2048,128]{2,1,0:T(8,128)}, f32[4,2048]{1,0:T(4,128)S(1)}, bf16[4,2048,128]{2,1,0:T(8,128)(2,1)}, bf16[512,128]{1,0:T(8,128)(2...) while((s32[]{:T(128)}, f32[4,2048,128]{2,1,0:T(8,128)}, ...), condition=%wide.region_11.11_spmd, body=%wide.region_9.10_spmd.sunk | while | flops 543160320 | bytes 6058097 | solution.py:50
  433.7 16.2 %while.78 = (s32[]{:T(128)}, f32[4,2048,128]{2,1,0:T(8,128)}, f32[4,2048]{1,0:T(4,128)S(1)}, bf16[4,2048,128]{2,1,0:T(8,128)(2,1)}, bf16[512,128]{1,0:T(8,128)(2...) while((s32[]{:T(128)}, f32[4,2048,128]{2,1,0:T(8,128)}, ...), condition=%wide.region_11.11_spmd, body=%wide.region_9.10_spmd.sunk | while | flops 543160320 | bytes 6058097 | solution.py:50
  456.8 16.2 %while.78 = (s32[]{:T(128)}, f32[4,2048,128]{2,1,0:T(8,128)}, f32[4,2048]{1,0:T(4,128)S(1)}, bf16[4,2048,128]{2,1,0:T(8,128)(2,1)}, bf16[512,128]{1,0:T(8,128)(2...) while((s32[]{:T(128)}, f32[4,2048,128]{2,1,0:T(8,128)}, ...), condition=%wide.region_11.11_spmd, body=%wide.region_9.10_spmd.sunk | while | flops 543160320 | bytes 6058097 | solution.py:50
  479.9 16.2 %while.78 = (s32[]{:T(128)}, f32[4,2048,128]{2,1,0:T(8,128)}, f32[4,2048]{1,0:T(4,128)S(1)}, bf16[4,2048,128]{2,1,0:T(8,128)(2,1)}, bf16[512,128]{1,0:T(8,128)(2...) while((s32[]{:T(128)}, f32[4,2048,128]{2,1,0:T(8,128)}, ...), condition=%wide.region_11.11_spmd, body=%wide.region_9.10_spmd.sunk | while | flops 543160320 | bytes 6058097 | solution.py:50
  503.0 16.2 %while.78 = (s32[]{:T(128)}, f32[4,2048,128]{2,1,0:T(8,128)}, f32[4,2048]{1,0:T(4,128)S(1)}, bf16[4,2048,128]{2,1,0:T(8,128)(2,1)}, bf16[512,128]{1,0:T(8,128)(2...) while((s32[]{:T(128)}, f32[4,2048,128]{2,1,0:T(8,128)}, ...), condition=%wide.region_11.11_spmd, body=%wide.region_9.10_spmd.sunk | while | flops 543160320 | bytes 6058097 | solution.py:50
  526.1 16.2 %while.78 = (s32[]{:T(128)}, f32[4,2048,128]{2,1,0:T(8,128)}, f32[4,2048]{1,0:T(4,128)S(1)}, bf16[4,2048,128]{2,1,0:T(8,128)(2,1)}, bf16[512,128]{1,0:T(8,128)(2...) while((s32[]{:T(128)}, f32[4,2048,128]{2,1,0:T(8,128)}, ...), condition=%wide.region_11.11_spmd, body=%wide.region_9.10_spmd.sunk | while | flops 543160320 | bytes 6058097 | solution.py:50
  549.2 16.2 %while.78 = (s32[]{:T(128)}, f32[4,2048,128]{2,1,0:T(8,128)}, f32[4,2048]{1,0:T(4,128)S(1)}, bf16[4,2048,128]{2,1,0:T(8,128)(2,1)}, bf16[512,128]{1,0:T(8,128)(2...) while((s32[]{:T(128)}, f32[4,2048,128]{2,1,0:T(8,128)}, ...), condition=%wide.region_11.11_spmd, body=%wide.region_9.10_spmd.sunk | while | flops 543160320 | bytes 6058097 | solution.py:50
  572.3 16.2 %while.78 = (s32[]{:T(128)}, f32[4,2048,128]{2,1,0:T(8,128)}, f32[4,2048]{1,0:T(4,128)S(1)}, bf16[4,2048,128]{2,1,0:T(8,128)(2,1)}, bf16[512,128]{1,0:T(8,128)(2...) while((s32[]{:T(128)}, f32[4,2048,128]{2,1,0:T(8,128)}, ...), condition=%wide.region_11.11_spmd, body=%wide.region_9.10_spmd.sunk | while | flops 543160320 | bytes 6058097 | solution.py:50
  595.4 16.2 %while.78 = (s32[]{:T(128)}, f32[4,2048,128]{2,1,0:T(8,128)}, f32[4,2048]{1,0:T(4,128)S(1)}, bf16[4,2048,128]{2,1,0:T(8,128)(2,1)}, bf16[512,128]{1,0:T(8,128)(2...) while((s32[]{:T(128)}, f32[4,2048,128]{2,1,0:T(8,128)}, ...), condition=%wide.region_11.11_spmd, body=%wide.region_9.10_spmd.sunk | while | flops 543160320 | bytes 6058097 | solution.py:50
  618.5 16.2 %while.78 = (s32[]{:T(128)}, f32[4,2048,128]{2,1,0:T(8,128)}, f32[4,2048]{1,0:T(4,128)S(1)}, bf16[4,2048,128]{2,1,0:T(8,128)(2,1)}, bf16[512,128]{1,0:T(8,128)(2...) while((s32[]{:T(128)}, f32[4,2048,128]{2,1,0:T(8,128)}, ...), condition=%wide.region_11.11_spmd, body=%wide.region_9.10_spmd.sunk | while | flops 543160320 | bytes 6058097 | solution.py:50
  641.5 16.2 %while.78 = (s32[]{:T(128)}, f32[4,2048,128]{2,1,0:T(8,128)}, f32[4,2048]{1,0:T(4,128)S(1)}, bf16[4,2048,128]{2,1,0:T(8,128)(2,1)}, bf16[512,128]{1,0:T(8,128)(2...) while((s32[]{:T(128)}, f32[4,2048,128]{2,1,0:T(8,128)}, ...), condition=%wide.region_11.11_spmd, body=%wide.region_9.10_spmd.sunk | while | flops 543160320 | bytes 6058097 | solution.py:50
  664.6 16.2 %while.78 = (s32[]{:T(128)}, f32[4,2048,128]{2,1,0:T(8,128)}, f32[4,2048]{1,0:T(4,128)S(1)}, bf16[4,2048,128]{2,1,0:T(8,128)(2,1)}, bf16[512,128]{1,0:T(8,128)(2...) while((s32[]{:T(128)}, f32[4,2048,128]{2,1,0:T(8,128)}, ...), condition=%wide.region_11.11_spmd, body=%wide.region_9.10_spmd.sunk | while | flops 543160320 | bytes 6058097 | solution.py:50
  687.7 16.2 %while.78 = (s32[]{:T(128)}, f32[4,2048,128]{2,1,0:T(8,128)}, f32[4,2048]{1,0:T(4,128)S(1)}, bf16[4,2048,128]{2,1,0:T(8,128)(2,1)}, bf16[512,128]{1,0:T(8,128)(2...) while((s32[]{:T(128)}, f32[4,2048,128]{2,1,0:T(8,128)}, ...), condition=%wide.region_11.11_spmd, body=%wide.region_9.10_spmd.sunk | while | flops 543160320 | bytes 6058097 | solution.py:50
  710.8 16.2 %while.78 = (s32[]{:T(128)}, f32[4,2048,128]{2,1,0:T(8,128)}, f32[4,2048]{1,0:T(4,128)S(1)}, bf16[4,2048,128]{2,1,0:T(8,128)(2,1)}, bf16[512,128]{1,0:T(8,128)(2...) while((s32[]{:T(128)}, f32[4,2048,128]{2,1,0:T(8,128)}, ...), condition=%wide.region_11.11_spmd, body=%wide.region_9.10_spmd.sunk | while | flops 543160320 | bytes 6058097 | solution.py:50
  733.9 16.2 %while.78 = (s32[]{:T(128)}, f32[4,2048,128]{2,1,0:T(8,128)}, f32[4,2048]{1,0:T(4,128)S(1)}, bf16[4,2048,128]{2,1,0:T(8,128)(2,1)}, bf16[512,128]{1,0:T(8,128)(2...) while((s32[]{:T(128)}, f32[4,2048,128]{2,1,0:T(8,128)}, ...), condition=%wide.region_11.11_spmd, body=%wide.region_9.10_spmd.sunk | while | flops 543160320 | bytes 6058097 | solution.py:50
  769.2 148.1 %all-gather.9.cloned.1.call-done = f32[32768,128]{1,0:T(8,128)} async-done(((f32[8192,128]{1,0:T(8,128)}), f32[32768,128]{1,0:T(8,128)}) %all-gather.9.cloned.1.call-update) | async-done | bytes 16777232 | tf_op jit(solution)/shard_map/all_gather | solution.py:81
  917.4 11.4 %copy.57 = f32[32768,128]{1,0:T(8,128)} copy(f32[32768,128]{1,0:T(8,128)} %all-gather.9.cloned.1.call-done) | data formatting | bytes 33554432
  (749 shorter events, 695.2 us)
Async XLA Ops:
  7.2 40.7 %all-gather.7.cloned.1.call-start = ((), (), s32[]{:S(2)}) async-start(), calls=%async_computation | async-start | bytes 2621440 | tf_op jit(solution)/shard_map/all_gather | solution.py:59
  7.9 296.9 %all-gather.11.cloned.1.call-start = ((), (), s32[]{:S(2)}) async-start(), calls=%async_computation.2 | async-start | bytes 1081344 | tf_op jit(solution)/shard_map/all_gather | solution.py:11
  250.3 0.6 copy-start
  250.9 110.3 %all-gather.13.cloned.1.call-start = ((), (), s32[]{:S(2)}) async-start(), calls=%async_computation.3 | async-start | bytes 1081344 | tf_op jit(solution)/shard_map/all_gather | solution.py:11
  251.6 665.7 %all-gather.9.cloned.1.call-start = ((), (), s32[]{:S(2)}) async-start(), calls=%async_computation.1 | async-start | bytes 20971520 | tf_op jit(solution)/shard_map/all_gather | solution.py:81
Sparse Core Ops, SparseCore 0:
  9.8 38.0 all-gather.6
  251.0 53.7 all-gather.10
  308.4 52.7 all-gather.12
  760.9 156.3 all-gather.8
where the time goes:
time: 946 us; the launch traced here: 936 us
  matrix products  363 us (38%)
  waiting for transfers between devices  295 us (31%)
  other arithmetic  173 us (18%)
  local copies, waits for them, and re-layouts  77.7 us (8%)
  between operations  13.8 us (1%)
    all_gather x1, waiting for transfers between devices, local(): lax.all_gather(share_new, 'tok', axis=0, tiled=True)  148 us
    dot_general x64, matrix products, second_pass(): jnp.dot(tok_block, cent_block.T, preferred_element_type=jnp.float32)  139 us
    dot_general x64, matrix products, first_pass(): jnp.dot(tok_block, cent_block.T, preferred_element_type=jnp.float32)  113 us
    dot_general x64, matrix products, second_pass(): jnp.einsum('tc,td->cd', weights, tok_block, preferred_element_type=jnp.fl...  111 us
    all_gather x2, waiting for transfers between devices, joined(): everything = jax.tree.map(lambda part: lax.all_gather(part, axis), value)  109 us
    add x32, other arithmetic, grid_step(): return ((accum[0] + block_sums, accum[1] + block_mass), None)  93.4 us
    reduce_sum x64, other arithmetic, first_pass(): jnp.sum(jnp.exp(logits - new_max[:, None]), axis=1)  48.4 us
    all_gather x1, waiting for transfers between devices, local(): every_tok = lax.all_gather(tokens, 'tok', axis=0, tiled=True)  36.8 us
  transfers between devices with their start and end apart: 4, of which 4 were waited for; matrix products, arithmetic and copies ran while one was open for 0% of the time, Pallas kernels for 0%

commit v1 on v0

v1 whole, which is shorter than its diff:
```python
import functools

import jax
import jax.numpy as jnp
from jax import lax
from jax.experimental import pallas as pl
from jax.experimental.pallas import tpu as pltpu
from jax.sharding import PartitionSpec as P

inverse_temp = 2.0
prior_weight = 0.05
safe_sum = 1e30
vmem_bytes = 56 * 1024 * 1024


def divisor(count, most):
    size = min(count, most)
    while count % size:
        size //= 2
    return size


def dot_nt(a, b):
    return lax.dot_general(a, b, (((1,), (1,)), ((), ())), preferred_element_type=jnp.float32)


def fold_rows(x, combine):
    parts = [x[k * 8 : (k + 1) * 8, :] for k in range(x.shape[0] // 8)]
    while len(parts) > 1:
        half = len(parts) // 2
        parts = [combine(parts[2 * k], parts[2 * k + 1]) for k in range(half)] + parts[2 * half :]
    return parts[0]


def stats_kernel(sub_rows, tok_cols, tok_ref, cent_ref, out_ref, base_ref, shift_ref, sums_ref):
    step = pl.program_id(0)
    tok_count = tok_ref.shape[0]
    tile = divisor(sub_rows, 256)
    subs = cent_ref.shape[0] // sub_rows
    col_blocks = tok_count // tok_cols

    def columns(t):
        return pl.ds(pl.multiple_of(t * tok_cols, tok_cols), tok_cols)

    def scaled_tokens(t):
        return tok_ref[columns(t), :] * jnp.bfloat16(inverse_temp)

    @pl.when(step == 0)
    def _():
        @pl.loop(0, col_blocks)
        def _(t):
            logits = dot_nt(cent_ref[0:128, :], scaled_tokens(t))
            top = jnp.max(fold_rows(logits, jnp.maximum), axis=0, keepdims=True)
            base_ref[:, columns(t)] = top

    @pl.loop(0, col_blocks)
    def _(t):
        rhs = scaled_tokens(t)
        shift = base_ref[:, columns(t)]
        for sub in range(subs):
            total = jnp.zeros((8, tok_cols), jnp.float32)
            for k in range(sub_rows // tile):
                logits = dot_nt(cent_ref[pl.ds(sub * sub_rows + k * tile, tile), :], rhs)
                total = total + fold_rows(jnp.exp(logits - shift), jnp.add)
            sums_ref[step * subs + sub, :, columns(t)] = total
            shift_ref[step * subs + sub, :, columns(t)] = shift

    worst = jnp.max(sums_ref[pl.ds(step * subs, subs), :, :])

    @pl.when(jnp.logical_not(worst < safe_sum))
    def _():
        @pl.loop(0, col_blocks)
        def _(t):
            worst_t = jnp.max(sums_ref[pl.ds(step * subs, subs), :, columns(t)])

            @pl.when(jnp.logical_not(worst_t < safe_sum))
            def _():
                @pl.loop(0, subs)
                def _(sub):
                    worst_s = jnp.max(sums_ref[step * subs + sub, :, columns(t)])

                    @pl.when(jnp.logical_not(worst_s < safe_sum))
                    def _():
                        rhs = scaled_tokens(t)
                        lowest = base_ref[:, columns(t)]

                        def logits_of(k):
                            first = pl.multiple_of(sub * sub_rows + k * tile, tile)
                            return dot_nt(cent_ref[pl.ds(first, tile), :], rhs)

                        def raise_top(k, top):
                            return jnp.maximum(top, fold_rows(logits_of(k), jnp.maximum))

                        top = lax.fori_loop(
                            0, sub_rows // tile, raise_top, jnp.broadcast_to(lowest, (8, tok_cols))
                        )
                        top = jnp.max(top, axis=0, keepdims=True)

                        def add_up(k, total):
                            return total + fold_rows(jnp.exp(logits_of(k) - top), jnp.add)

                        total = lax.fori_loop(
                            0, sub_rows // tile, add_up, jnp.zeros((8, tok_cols), jnp.float32)
                        )
                        sums_ref[step * subs + sub, :, columns(t)] = total
                        shift_ref[step * subs + sub, :, columns(t)] = top

    @pl.when(step == pl.num_programs(0) - 1)
    def _():
        @pl.loop(0, col_blocks)
        def _(t):
            shifts = shift_ref[:, :, columns(t)]
            top = jnp.max(shifts, axis=0)
            scale = jnp.exp(shifts - top[None])
            total = jnp.sum(sums_ref[:, :, columns(t)] * scale, axis=0)
            total = jnp.sum(total, axis=0, keepdims=True)
            out_ref[:, columns(t)] = top + jnp.log(total)


def local_lse(tokens, centroids):
    tok_count, width = tokens.shape
    cent_count = centroids.shape[0]
    block_rows = divisor(cent_count, 4096)
    sub_rows = divisor(block_rows, 1024)
    tok_cols = divisor(tok_count, 512)
    blocks = cent_count // block_rows
    subs = cent_count // sub_rows
    return pl.pallas_call(
        functools.partial(stats_kernel, sub_rows, tok_cols),
        grid=(blocks,),
        in_specs=[
            pl.BlockSpec((tok_count, width), lambda j: (0, 0)),
            pl.BlockSpec((block_rows, width), lambda j: (j, 0)),
        ],
        out_specs=pl.BlockSpec((1, tok_count), lambda j: (0, 0)),
        out_shape=jax.ShapeDtypeStruct((1, tok_count), jnp.float32),
        scratch_shapes=[
            pltpu.VMEM((1, tok_count), jnp.float32),
            pltpu.VMEM((subs, 1, tok_count), jnp.float32),
            pltpu.VMEM((subs, 8, tok_count), jnp.float32),
        ],
        compiler_params=pltpu.CompilerParams(vmem_limit_bytes=vmem_bytes),
        cost_estimate=pl.CostEstimate(
            flops=2 * tok_count * cent_count * width,
            bytes_accessed=(tok_count + cent_count) * width * 2,
            transcendentals=tok_count * cent_count,
        ),
        name="row_stats",
    )(tokens, centroids)


def update_kernel(shards, place_ref, *refs):
    tok_refs, lse_refs = refs[:shards], refs[shards : 2 * shards]
    cent_ref, new_ref, mass_ref, weights_ref, total_ref = refs[2 * shards :]
    rows = cent_ref.shape[0]
    depth, width = tok_refs[0].shape
    tile = divisor(rows, 256)
    piece = divisor(depth, 512)

    def weigh(first, stage):
        cents = cent_ref[pl.ds(first, tile), :] * jnp.bfloat16(inverse_temp)
        for k in range(depth // piece):
            span = pl.ds(k * piece, piece)
            logits = dot_nt(cents, tok_refs[stage][span, :])
            weights = jnp.exp(logits - lse_refs[stage][:, span])
            weights_ref[stage % 2, :, span] = weights.astype(jnp.bfloat16)

    def gather_up(stage):
        toks = tok_refs[stage][...]
        rhs = jnp.concatenate([toks, jnp.ones_like(toks)], axis=1)
        part = jnp.dot(weights_ref[stage % 2], rhs, preferred_element_type=jnp.float32)
        if stage == 0:
            total_ref[...] = part
        else:
            total_ref[...] += part

    diagonal = lax.broadcasted_iota(jnp.int32, (128, 128), 0) == lax.broadcasted_iota(
        jnp.int32, (128, 128), 1
    )

    @pl.loop(0, rows // tile)
    def _(r):
        first = pl.multiple_of(r * tile, tile)
        weigh(first, 0)
        for stage in range(1, shards):
            weigh(first, stage)
            gather_up(stage - 1)
        gather_up(shards - 1)
        sums = total_ref[:, 0:width]
        mass = total_ref[:, width : 2 * width]
        cents = cent_ref[pl.ds(first, tile), :].astype(jnp.float32)
        new = (sums + prior_weight * cents) / (mass + prior_weight)
        new_ref[pl.ds(first, tile), :] = new.astype(new_ref.dtype)
        for k in range(tile // 128):
            square = jnp.where(diagonal, mass[k * 128 : (k + 1) * 128, :], 0.0)
            mass_ref[r * (tile // 128) + k] = jnp.sum(square, axis=0, keepdims=True)


def updated_chunk(place, toks, lses, centroids, rows):
    shards = len(toks)
    depth, width = toks[0].shape
    block_rows = divisor(rows, 1024)
    tile = divisor(block_rows, 256)
    per_chunk = rows // block_rows
    all_count = shards * depth
    whole = lambda j, place: (0, 0)
    return pl.pallas_call(
        functools.partial(update_kernel, shards),
        grid_spec=pltpu.PrefetchScalarGridSpec(
            num_scalar_prefetch=1,
            grid=(per_chunk,),
            in_specs=[pl.BlockSpec((depth, width), whole)] * shards
            + [pl.BlockSpec((1, depth), whole)] * shards
            + [pl.BlockSpec((block_rows, width), lambda j, place: (place[0] * per_chunk + j, 0))],
            out_specs=[
                pl.BlockSpec((block_rows, width), lambda j, place: (j, 0)),
                pl.BlockSpec((block_rows // 128, 1, 128), lambda j, place: (j, 0, 0)),
            ],
            scratch_shapes=[
                pltpu.VMEM((2, tile, depth), jnp.bfloat16),
                pltpu.VMEM((tile, 2 * width), jnp.float32),
            ],
        ),
        out_shape=[
            jax.ShapeDtypeStruct((rows, width), jnp.float32),
            jax.ShapeDtypeStruct((rows // 128, 1, 128), jnp.float32),
        ],
        compiler_params=pltpu.CompilerParams(vmem_limit_bytes=vmem_bytes),
        cost_estimate=pl.CostEstimate(
            flops=6 * all_count * rows * width,
            bytes_accessed=(2 * all_count + 4 * rows) * width,
            transcendentals=all_count * rows,
        ),
        name="new_rows",
    )(place, *toks, *lses, centroids)


def combine_kernel(*refs):
    parts, out_ref = [ref[...] for ref in refs[:-1]], refs[-1]
    top = functools.reduce(jnp.maximum, parts)
    out_ref[...] = top + jnp.log(sum(jnp.exp(part - top) for part in parts))


def combined_lse(parts):
    return pl.pallas_call(
        combine_kernel, out_shape=jax.ShapeDtypeStruct(parts[0].shape, jnp.float32), name="join_stats"
    )(*parts)


def blank(shape):
    return pl.pallas_call(
        lambda out_ref: None,
        out_specs=pl.BlockSpec(memory_space=pl.ANY),
        out_shape=jax.ShapeDtypeStruct(shape, jnp.float32),
        name="blank",
    )()


def from_others(value, axis):
    size = lax.axis_size(axis)
    found = [value]
    for shift in range(1, size):
        found.append(lax.ppermute(value, axis, [(k, (k + shift) % size) for k in range(size)]))
    return found


def spread(value, me, size):
    if size != 4:
        others = from_others(value, "tok")
        return [((me - s) % size, 0, part) for s, part in enumerate(others)]

    def swap(part, mask):
        return lax.ppermute(part, "tok", [(k, k ^ mask) for k in range(4)])

    half = value.shape[0] // 2
    upper, lower = value[:half], value[half:]
    upper1, lower1 = swap(upper, 1), swap(lower, 1)
    upper2, lower2 = swap(upper, 2), swap(lower, 2)
    upper3, lower3 = swap(upper1, 2), swap(lower2, 1)
    return [
        (me, 0, value),
        (me ^ 1, 0, upper1),
        (me ^ 1, half, lower1),
        (me ^ 2, 0, upper2),
        (me ^ 2, half, lower2),
        (me ^ 3, 0, upper3),
        (me ^ 3, half, lower3),
    ]


def local(tokens, centroids):
    tok_size = lax.axis_size("tok")
    me = lax.axis_index("tok")
    cent_count, width = centroids.shape
    share_rows = cent_count // tok_size

    toks = from_others(tokens, "tok")
    own_lse = combined_lse(from_others(local_lse(tokens, centroids), "cent"))
    lses = from_others(own_lse, "tok")

    chunks = 4
    while share_rows % (chunks * 256):
        chunks //= 2
    rows = share_rows // chunks
    updated = blank((cent_count, width))
    masses = []
    for k in range(chunks):
        place = (k * tok_size + me).reshape(1)
        new, mass = updated_chunk(place, toks, lses, centroids, rows)
        for shift, first, part in spread(new.astype(jnp.float16), me, tok_size):
            start = (k * tok_size + shift) * rows + first
            updated = lax.dynamic_update_slice(updated, part.astype(jnp.float32), (start, 0))
        masses.append(mass.reshape(1, 1, rows // 128, 128))
    found = from_others(jnp.concatenate(masses), "tok")
    index = lax.broadcasted_iota(jnp.int32, (1, tok_size, 1, 1), 1)
    source = (me - index) % tok_size
    all_masses = found[0]
    for s in range(1, tok_size):
        all_masses = jnp.where(source == s, found[s], all_masses)
    return updated, all_masses.reshape(cent_count)


def solution(mesh):
    placed = (P("tok", None), P("cent", None))
    return jax.shard_map(
        local, mesh=mesh, in_specs=placed, out_specs=(P("cent", None), P("cent")), check_vma=False
    )
```

time: 946 us -> 266 us (0.28)
  matrix products: 363 us -> 0 us
  waiting for transfers between devices: 295 us -> 37.9 us
  Pallas kernels: 0 us -> 155 us
  other arithmetic: 173 us -> 30.6 us
  local copies, waits for them, and re-layouts: 77.7 us -> 2.7 us
  starting transfers between devices: 0.16 us -> 36.4 us
  between operations: 13.8 us -> 0.98 us
    dot_general x192 -> x0, matrix products: 363 us -> none  [the longest x64 139 us: second_pass(): jnp.dot(tok_block, cent_block.T, preferred_element_type=jnp.float32)]
    all_gather x4 -> x0, waiting for transfers between devices: 294 us -> none  [the longest x1 148 us: local(): lax.all_gather(share_new, 'tok', axis=0, tiled=True)]
    pallas_call x0 -> x7, Pallas kernels: none -> 155 us  [the longest x4 89.1 us: updated_chunk(): pl.pallas_call(functools.partial(update_kernel, shards), grid_spec=pltpu....]
    add x128 -> x0, other arithmetic: 120 us -> none  [the longest x32 93.4 us: grid_step(): return ((accum[0] + block_sums, accum[1] + block_mass), None)]
    reduce_sum x64 -> x0, other arithmetic: 48.4 us -> none  [first_pass(): jnp.sum(jnp.exp(logits - new_max[:, None]), axis=1)]
    ppermute x0 -> x40, waiting for transfers between devices: none -> 37.9 us  [the longest x16 19.9 us: from_others(): lax.ppermute(value, axis, [(k, (k + shift) % size) for k in range(size)])]
    ppermute x0 -> x40, starting transfers between devices: none -> 36.4 us  [the longest x24 23.4 us: swap(): return lax.ppermute(part, 'tok', [(k, k ^ mask) for k in range(4)])]
    dynamic_update_slice x96 -> x0, local copies, waits for them, and re-layouts: 30.8 us -> none  [the longest x32 22.5 us: local(): lax.map(lambda blk: local_stats(blk, own_blocks), tok_blocks)]
  transfers between devices with their start and end apart: 4 -> 40, of which waited for: 4 -> 19; matrix products, arithmetic and copies ran while one was open for 0% -> 8% of each run, Pallas kernels for 0% -> 50%
where the time goes in v1:
time: 266 us; the launch traced here: 263 us
  Pallas kernels  155 us (58%)
  waiting for transfers between devices  37.9 us (14%)
  starting transfers between devices  36.4 us (14%)
  other arithmetic  30.6 us (12%)
  local copies, waits for them, and re-layouts  2.7 us (1%)
    pallas_call x4, Pallas kernels, updated_chunk(): pl.pallas_call(functools.partial(update_kernel, shards), grid_spec=pltpu....  89.1 us
    pallas_call x1, Pallas kernels, local_lse(): pl.pallas_call(functools.partial(stats_kernel, sub_rows, tok_cols), grid=...  64 us
    dynamic_update_slice x28, other arithmetic, local(): lax.dynamic_update_slice(updated, part.astype(jnp.float32), (start, 0))  29.1 us
    ppermute x24, starting transfers between devices, swap(): return lax.ppermute(part, 'tok', [(k, k ^ mask) for k in range(4)])  23.4 us
    ppermute x16, waiting for transfers between devices, from_others(): lax.ppermute(value, axis, [(k, (k + shift) % size) for k in range(size)])  19.9 us
    ppermute x24, waiting for transfers between devices, swap(): return lax.ppermute(part, 'tok', [(k, k ^ mask) for k in range(4)])  18 us
    ppermute x16, starting transfers between devices, from_others(): lax.ppermute(value, axis, [(k, (k + shift) % size) for k in range(size)])  12.9 us
  transfers between devices with their start and end apart: 40, of which 19 were waited for; matrix products, arithmetic and copies ran while one was open for 8% of the time, Pallas kernels for 50%

profile of v1, /device:TPU:0, one launch (start us, length us, event | category | flops | bytes accessed | tf_op | source)
XLA Modules:
  0.0 263.1 jit_solution(2479911296143620852)
XLA Ops:
  0.6 3.0 %collective-permute-start = (bf16[2048,128]{1,0:T(8,128)(2,1)}, bf16[2048,128]{1,0:T(8,128)(2,1)S(1)}, u32[]{:S(2)}, u32[]{:S(2)}) collective-permute-start(bf16[2048,128]{1,0:T(8,128)(2,1)} %refs_0_.7), channel_id=1, source_target_pairs={{0,8},{8,16},{16,24},{24,0},{1,9},{9,17},{17,25},{25,1},{2,10},{10... | collective-permute-start | bytes 1572872 | tf_op jit(solution)/shard_map/ppermute | solution.py:263
  3.6 1.5 collective-permute-start.1
  5.1 1.4 collective-permute-start.2
  6.6 64.0 %row_stats.1.refs_0_ = f32[1,2048]{1,0:T(1,128)} custom-call(bf16[2048,128]{1,0:T(8,128)(2,1)} %refs_0_.7, bf16[32768,128]{1,0:T(8,128)(2,1)} %refs_8_.7), custom_call_target="tpu_custom_call" | custom-call | flops 17179869184 | bytes 8912896 | tf_op jit(solution)/shard_map/row_stats/pallas_call | solution.py:128
  70.6 5.1 %collective-permute-done.3.refs_1_ = f32[1,2048]{1,0:T(1,128)S(1)} collective-permute-done((f32[1,2048]{1,0:T(1,128)}, f32[1,2048]{1,0:T(1,128)S(1)}, u32[]{:S(2)}, u32[]{:S(2)}) %collective-permute-start.3) | collective-permute-done | bytes 8224 | tf_op jit(solution)/shard_map/ppermute | solution.py:263
  76.3 3.6 %collective-permute-done.5.refs_3_ = f32[1,2048]{1,0:T(1,128)S(1)} collective-permute-done((f32[1,2048]{1,0:T(1,128)}, f32[1,2048]{1,0:T(1,128)S(1)}, u32[]{:S(2)}, u32[]{:S(2)}) %collective-permute-start.5) | collective-permute-done | bytes 8224 | tf_op jit(solution)/shard_map/ppermute | solution.py:263
  81.6 1.5 collective-permute-done.7.refs_5_
  83.1 1.8 collective-permute-done.8.refs_6_
  86.1 1.4 join_stats.1.refs_4_
  87.5 1.9 collective-permute-start.11
  89.4 2.9 %collective-permute-done.10.refs_5_ = f32[1,2048]{1,0:T(1,128)S(1)} collective-permute-done((f32[1,2048]{1,0:T(1,128)}, f32[1,2048]{1,0:T(1,128)S(1)}, u32[]{:S(2)}, u32[]{:S(2)}) %collective-permute-start.10) | collective-permute-done | bytes 8224 | tf_op jit(solution)/shard_map/ppermute | solution.py:263
  92.8 3.3 %collective-permute-done.12.refs_7_ = f32[1,2048]{1,0:T(1,128)S(1)} collective-permute-done((f32[1,2048]{1,0:T(1,128)}, f32[1,2048]{1,0:T(1,128)S(1)}, u32[]{:S(2)}, u32[]{:S(2)}) %collective-permute-start.12) | collective-permute-done | bytes 8224 | tf_op jit(solution)/shard_map/ppermute | solution.py:263
  97.3 22.2 %new_rows.4 = (f32[2048,128]{1,0:T(8,128)}, f32[16,1,128]{2,1,0:T(1,128)}) custom-call(s32[1]{0:T(128)} %bitcast.place_ref, bf16[2048,128]{1,0:T(8,128)(2,1)} %refs_0_.7, bf16[2048,128]{1,0:T(8,128)(2,1)} %copy-done.10, bf16[2048,128]{1,0:T(8,128)(2,1)} %copy-done.11, bf16[2048,128]{1,0:T(8,128)(2,1)} %copy-done.12, f32[1,2048]{1,0:T(1,128)} %join_stats.1.refs_4_, ...), custom_call_target="tpu_custom_call" | custom-call | flops 12884901888 | bytes 3145728 | tf_op jit(solution)/shard_map/new_rows/pallas_call | solution.py:207
  119.5 2.3 convert_dynamic-update-slice_fusion.3
  123.9 1.9 collective-permute-start.14
  126.1 22.2 %new_rows.5 = (f32[2048,128]{1,0:T(8,128)}, f32[16,1,128]{2,1,0:T(1,128)}) custom-call(s32[1]{0:T(128)} %bitcast.1.place_ref, bf16[2048,128]{1,0:T(8,128)(2,1)} %refs_0_.7, bf16[2048,128]{1,0:T(8,128)(2,1)} %copy-done.10, bf16[2048,128]{1,0:T(8,128)(2,1)} %copy-done.11, bf16[2048,128]{1,0:T(8,128)(2,1)} %copy-done.12, f32[1,2048]{1,0:T(1,128)} %join_stats.1.refs_4_, ...), custom_call_target="tpu_custom_call" | custom-call | flops 12884901888 | bytes 3145728 | tf_op jit(solution)/shard_map/new_rows/pallas_call | solution.py:207
  148.3 1.9 collective-permute-start.17
  157.4 2.3 convert_dynamic-update-slice_fusion.2
  161.4 1.4 collective-permute-start.19
  162.7 22.2 %new_rows.6 = (f32[2048,128]{1,0:T(8,128)}, f32[16,1,128]{2,1,0:T(1,128)}) custom-call(s32[1]{0:T(128)} %bitcast.2.place_ref, bf16[2048,128]{1,0:T(8,128)(2,1)} %refs_0_.7, bf16[2048,128]{1,0:T(8,128)(2,1)} %copy-done.10, bf16[2048,128]{1,0:T(8,128)(2,1)} %copy-done.11, bf16[2048,128]{1,0:T(8,128)(2,1)} %copy-done.12, f32[1,2048]{1,0:T(1,128)} %join_stats.1.refs_4_, ...), custom_call_target="tpu_custom_call" | custom-call | flops 12884901888 | bytes 3145728 | tf_op jit(solution)/shard_map/new_rows/pallas_call | solution.py:207
  189.3 2.0 collective-permute-done.21
  195.8 2.3 convert_dynamic-update-slice_fusion.1
  198.9 22.5 %new_rows.7 = (f32[2048,128]{1,0:T(8,128)}, f32[16,1,128]{2,1,0:T(1,128)}) custom-call(s32[1]{0:T(128)} %bitcast.3.place_ref, bf16[2048,128]{1,0:T(8,128)(2,1)} %refs_0_.7, bf16[2048,128]{1,0:T(8,128)(2,1)} %copy-done.10, bf16[2048,128]{1,0:T(8,128)(2,1)} %copy-done.11, bf16[2048,128]{1,0:T(8,128)(2,1)} %copy-done.12, f32[1,2048]{1,0:T(1,128)} %join_stats.1.refs_4_, ...), custom_call_target="tpu_custom_call" | custom-call | flops 12884901888 | bytes 3145728 | tf_op jit(solution)/shard_map/new_rows/pallas_call | solution.py:207
  221.4 1.4 collective-permute-start.26
  224.1 2.3 collective-permute-start.37
  231.3 1.5 collective-permute-done.27
  234.0 1.6 collective-permute-done.28
  237.5 2.4 collective-permute-done.29
  240.7 4.1 %collective-permute-done.30 = f16[1024,128]{1,0:T(8,128)(2,1)S(1)} collective-permute-done((f16[1024,128]{1,0:T(8,128)(2,1)S(1)}, f16[1024,128]{1,0:T(8,128)(2,1)S(1)}, u32[]{:S(2)}, u32[]{:S(2)}) %collective-permute-start.30) | collective-permute-done | bytes 262176 | tf_op jit(solution)/shard_map/ppermute | solution.py:273
  245.6 2.3 convert_dynamic-update-slice_fusion
  249.5 2.0 collective-permute-start.32
  253.1 1.4 collective-permute-done.31
  (123 shorter events, 48.3 us)
Async XLA Ops:
  0.6 95.5 %collective-permute-start = (bf16[2048,128]{1,0:T(8,128)(2,1)}, bf16[2048,128]{1,0:T(8,128)(2,1)S(1)}, u32[]{:S(2)}, u32[]{:S(2)}) collective-permute-start(bf16[2048,128]{1,0:T(8,128)(2,1)} %refs_0_.7), channel_id=1, source_target_pairs={{0,8},{8,16},{16,24},{24,0},{1,9},{9,17},{17,25},{25,1},{2,10},{10... | collective-permute-start | bytes 1572872 | tf_op jit(solution)/shard_map/ppermute | solution.py:263
  3.6 92.5 %collective-permute-start.1 = (bf16[2048,128]{1,0:T(8,128)(2,1)}, bf16[2048,128]{1,0:T(8,128)(2,1)S(1)}, u32[]{:S(2)}, u32[]{:S(2)}) collective-permute-start(bf16[2048,128]{1,0:T(8,128)(2,1)} %refs_0_.7), channel_id=1, source_target_pairs={{0,16},{8,24},{16,0},{24,8},{1,17},{9,25},{17,1},{25,9},{2,18},{10... | collective-permute-start | bytes 1572872 | tf_op jit(solution)/shard_map/ppermute | solution.py:263
  5.1 91.0 %collective-permute-start.2 = (bf16[2048,128]{1,0:T(8,128)(2,1)}, bf16[2048,128]{1,0:T(8,128)(2,1)S(1)}, u32[]{:S(2)}, u32[]{:S(2)}) collective-permute-start(bf16[2048,128]{1,0:T(8,128)(2,1)} %refs_0_.7), channel_id=1, source_target_pairs={{0,24},{8,0},{16,8},{24,16},{1,25},{9,1},{17,9},{25,17},{2,26},{10... | collective-permute-start | bytes 1572872 | tf_op jit(solution)/shard_map/ppermute | solution.py:263
  70.6 5.7 %collective-permute-start.4 = (f32[1,2048]{1,0:T(1,128)}, f32[1,2048]{1,0:T(1,128)S(1)}, u32[]{:S(2)}, u32[]{:S(2)}) collective-permute-start(f32[1,2048]{1,0:T(1,128)} %row_stats.1.refs_0_), channel_id=1, source_target_pairs={{0,2},{1,3},{2,4},{3,5},{4,6},{5,7},{6,0},{7,1},{8,10},{9,11},{10,... | collective-permute-start | bytes 24584 | tf_op jit(solution)/shard_map/ppermute | solution.py:263
  87.5 5.3 %collective-permute-start.11 = (f32[1,2048]{1,0:T(1,128)}, f32[1,2048]{1,0:T(1,128)S(1)}, u32[]{:S(2)}, u32[]{:S(2)}) collective-permute-start(f32[1,2048]{1,0:T(1,128)} %join_stats.1.refs_4_), channel_id=1, source_target_pairs={{0,16},{8,24},{16,0},{24,8},{1,17},{9,25},{17,1},{25,9},{2,18},{10... | collective-permute-start | bytes 24584 | tf_op jit(solution)/shard_map/ppermute | solution.py:263
  121.9 26.3 %collective-permute-start.13 = (f16[1024,128]{1,0:T(8,128)(2,1)S(1)}, f16[1024,128]{1,0:T(8,128)(2,1)S(1)}, u32[]{:S(2)}, u32[]{:S(2)}) collective-permute-start(f16[1024,128]{1,0:T(8,128)(2,1)S(1)} %get-tuple-element.33), channel_id=1, source_target_pairs={{0,8},{8,0},{16,24},{24,16},{1,9},{9,1},{17,25},{25,17},{2,10},{10... | collective-permute-start | bytes 786440 | tf_op jit(solution)/shard_map/ppermute | solution.py:273
  123.3 28.6 %collective-permute-start.15 = (f16[1024,128]{1,0:T(8,128)(2,1)S(1)}, f16[1024,128]{1,0:T(8,128)(2,1)S(1)}, u32[]{:S(2)}, u32[]{:S(2)}) collective-permute-start(f16[1024,128]{1,0:T(8,128)(2,1)S(1)} %get-tuple-element.33), channel_id=1, source_target_pairs={{0,16},{8,24},{16,0},{24,8},{1,17},{9,25},{17,1},{25,9},{2,18},{10... | collective-permute-start | bytes 786440 | tf_op jit(solution)/shard_map/ppermute | solution.py:273
  123.9 27.2 %collective-permute-start.14 = (f16[1024,128]{1,0:T(8,128)(2,1)S(1)}, f16[1024,128]{1,0:T(8,128)(2,1)S(1)}, u32[]{:S(2)}, u32[]{:S(2)}) collective-permute-start(f16[1024,128]{1,0:T(8,128)(2,1)S(1)} %get-tuple-element.32), channel_id=1, source_target_pairs={{0,8},{8,0},{16,24},{24,16},{1,9},{9,1},{17,25},{25,17},{2,10},{10... | collective-permute-start | bytes 786440 | tf_op jit(solution)/shard_map/ppermute | solution.py:273
  125.9 24.3 %collective-permute-start.16 = (f16[1024,128]{1,0:T(8,128)(2,1)S(1)}, f16[1024,128]{1,0:T(8,128)(2,1)S(1)}, u32[]{:S(2)}, u32[]{:S(2)}) collective-permute-start(f16[1024,128]{1,0:T(8,128)(2,1)S(1)} %get-tuple-element.32), channel_id=1, source_target_pairs={{0,16},{8,24},{16,0},{24,8},{1,17},{9,25},{17,1},{25,9},{2,18},{10... | collective-permute-start | bytes 786440 | tf_op jit(solution)/shard_map/ppermute | solution.py:273
  148.3 6.4 %collective-permute-start.17 = (f16[1024,128]{1,0:T(8,128)(2,1)S(1)}, f16[1024,128]{1,0:T(8,128)(2,1)S(1)}, u32[]{:S(2)}, u32[]{:S(2)}) collective-permute-start(f16[1024,128]{1,0:T(8,128)(2,1)S(1)} %collective-permute-done.13), channel_id=1, source_target_pairs={{0,16},{8,24},{16,0},{24,8},{1,17},{9,25},{17,1},{25,9},{2,18},{10... | collective-permute-start | bytes 786440 | tf_op jit(solution)/shard_map/ppermute | solution.py:273
  150.2 6.4 %collective-permute-start.18 = (f16[1024,128]{1,0:T(8,128)(2,1)S(1)}, f16[1024,128]{1,0:T(8,128)(2,1)S(1)}, u32[]{:S(2)}, u32[]{:S(2)}) collective-permute-start(f16[1024,128]{1,0:T(8,128)(2,1)S(1)} %collective-permute-done.16), channel_id=1, source_target_pairs={{0,8},{8,0},{16,24},{24,16},{1,9},{9,1},{17,25},{25,17},{2,10},{10... | collective-permute-start | bytes 786440 | tf_op jit(solution)/shard_map/ppermute | solution.py:273
  159.8 28.6 %collective-permute-start.20 = (f16[1024,128]{1,0:T(8,128)(2,1)S(1)}, f16[1024,128]{1,0:T(8,128)(2,1)S(1)}, u32[]{:S(2)}, u32[]{:S(2)}) collective-permute-start(f16[1024,128]{1,0:T(8,128)(2,1)S(1)} %get-tuple-element.30), channel_id=1, source_target_pairs={{0,8},{8,0},{16,24},{24,16},{1,9},{9,1},{17,25},{25,17},{2,10},{10... | collective-permute-start | bytes 786440 | tf_op jit(solution)/shard_map/ppermute | solution.py:273
  160.2 26.8 %collective-permute-start.22 = (f16[1024,128]{1,0:T(8,128)(2,1)S(1)}, f16[1024,128]{1,0:T(8,128)(2,1)S(1)}, u32[]{:S(2)}, u32[]{:S(2)}) collective-permute-start(f16[1024,128]{1,0:T(8,128)(2,1)S(1)} %get-tuple-element.30), channel_id=1, source_target_pairs={{0,16},{8,24},{16,0},{24,8},{1,17},{9,25},{17,1},{25,9},{2,18},{10... | collective-permute-start | bytes 786440 | tf_op jit(solution)/shard_map/ppermute | solution.py:273
  161.4 24.8 %collective-permute-start.19 = (f16[1024,128]{1,0:T(8,128)(2,1)S(1)}, f16[1024,128]{1,0:T(8,128)(2,1)S(1)}, u32[]{:S(2)}, u32[]{:S(2)}) collective-permute-start(f16[1024,128]{1,0:T(8,128)(2,1)S(1)} %get-tuple-element.31), channel_id=1, source_target_pairs={{0,8},{8,0},{16,24},{24,16},{1,9},{9,1},{17,25},{25,17},{2,10},{10... | collective-permute-start | bytes 786440 | tf_op jit(solution)/shard_map/ppermute | solution.py:273
  185.0 6.4 %collective-permute-start.21 = (f16[1024,128]{1,0:T(8,128)(2,1)S(1)}, f16[1024,128]{1,0:T(8,128)(2,1)S(1)}, u32[]{:S(2)}, u32[]{:S(2)}) collective-permute-start(f16[1024,128]{1,0:T(8,128)(2,1)S(1)} %get-tuple-element.31), channel_id=1, source_target_pairs={{0,16},{8,24},{16,0},{24,8},{1,17},{9,25},{17,1},{25,9},{2,18},{10... | collective-permute-start | bytes 786440 | tf_op jit(solution)/shard_map/ppermute | solution.py:273
  186.2 8.0 %collective-permute-start.23 = (f16[1024,128]{1,0:T(8,128)(2,1)S(1)}, f16[1024,128]{1,0:T(8,128)(2,1)S(1)}, u32[]{:S(2)}, u32[]{:S(2)}) collective-permute-start(f16[1024,128]{1,0:T(8,128)(2,1)S(1)} %collective-permute-done.19), channel_id=1, source_target_pairs={{0,16},{8,24},{16,0},{24,8},{1,17},{9,25},{17,1},{25,9},{2,18},{10... | collective-permute-start | bytes 786440 | tf_op jit(solution)/shard_map/ppermute | solution.py:273
  187.0 8.0 %collective-permute-start.24 = (f16[1024,128]{1,0:T(8,128)(2,1)S(1)}, f16[1024,128]{1,0:T(8,128)(2,1)S(1)}, u32[]{:S(2)}, u32[]{:S(2)}) collective-permute-start(f16[1024,128]{1,0:T(8,128)(2,1)S(1)} %collective-permute-done.22), channel_id=1, source_target_pairs={{0,8},{8,0},{16,24},{24,16},{1,9},{9,1},{17,25},{25,17},{2,10},{10... | collective-permute-start | bytes 786440 | tf_op jit(solution)/shard_map/ppermute | solution.py:273
  198.2 29.4 %collective-permute-start.25 = (f16[1024,128]{1,0:T(8,128)(2,1)S(1)}, f16[1024,128]{1,0:T(8,128)(2,1)S(1)}, u32[]{:S(2)}, u32[]{:S(2)}) collective-permute-start(f16[1024,128]{1,0:T(8,128)(2,1)S(1)} %get-tuple-element.29), channel_id=1, source_target_pairs={{0,8},{8,0},{16,24},{24,16},{1,9},{9,1},{17,25},{25,17},{2,10},{10... | collective-permute-start | bytes 786440 | tf_op jit(solution)/shard_map/ppermute | solution.py:273
  221.4 7.9 %collective-permute-start.26 = (f16[1024,128]{1,0:T(8,128)(2,1)S(1)}, f16[1024,128]{1,0:T(8,128)(2,1)S(1)}, u32[]{:S(2)}, u32[]{:S(2)}) collective-permute-start(f16[1024,128]{1,0:T(8,128)(2,1)S(1)} %get-tuple-element.28), channel_id=1, source_target_pairs={{0,8},{8,0},{16,24},{24,16},{1,9},{9,1},{17,25},{25,17},{2,10},{10... | collective-permute-start | bytes 786440 | tf_op jit(solution)/shard_map/ppermute | solution.py:273
  223.5 26.0 %collective-permute-start.39 = (f32[4,1,16,128]{3,2,1,0:T(8,128)S(1)}, f32[4,1,16,128]{3,2,1,0:T(8,128)S(1)}, u32[]{:S(2)}, u32[]{:S(2)}) collective-permute-start(f32[4,1,16,128]{3,2,1,0:T(8,128)S(1)} %get-tuple-element.34), channel_id=1, source_target_pairs={{0,8},{8,16},{16,24},{24,0},{1,9},{9,17},{17,25},{25,1},{2,10},{10... | collective-permute-start | bytes 98312 | tf_op jit(solution)/shard_map/ppermute | solution.py:263
  224.1 27.4 %collective-permute-start.37 = (f32[4,1,16,128]{3,2,1,0:T(8,128)S(1)}, f32[4,1,16,128]{3,2,1,0:T(8,128)S(1)}, u32[]{:S(2)}, u32[]{:S(2)}) collective-permute-start(f32[4,1,16,128]{3,2,1,0:T(8,128)S(1)} %get-tuple-element.34), channel_id=1, source_target_pairs={{0,24},{8,0},{16,8},{24,16},{1,25},{9,1},{17,9},{25,17},{2,26},{10... | collective-permute-start | bytes 98312 | tf_op jit(solution)/shard_map/ppermute | solution.py:263
  226.4 6.4 %collective-permute-start.27 = (f16[1024,128]{1,0:T(8,128)(2,1)S(1)}, f16[1024,128]{1,0:T(8,128)(2,1)S(1)}, u32[]{:S(2)}, u32[]{:S(2)}) collective-permute-start(f16[1024,128]{1,0:T(8,128)(2,1)S(1)} %get-tuple-element.29), channel_id=1, source_target_pairs={{0,16},{8,24},{16,0},{24,8},{1,17},{9,25},{17,1},{25,9},{2,18},{10... | collective-permute-start | bytes 786440 | tf_op jit(solution)/shard_map/ppermute | solution.py:273
  227.6 8.0 %collective-permute-start.28 = (f16[1024,128]{1,0:T(8,128)(2,1)S(1)}, f16[1024,128]{1,0:T(8,128)(2,1)S(1)}, u32[]{:S(2)}, u32[]{:S(2)}) collective-permute-start(f16[1024,128]{1,0:T(8,128)(2,1)S(1)} %get-tuple-element.28), channel_id=1, source_target_pairs={{0,16},{8,24},{16,0},{24,8},{1,17},{9,25},{17,1},{25,9},{2,18},{10... | collective-permute-start | bytes 786440 | tf_op jit(solution)/shard_map/ppermute | solution.py:273
  229.3 22.2 %collective-permute-start.38 = (f32[4,1,16,128]{3,2,1,0:T(8,128)S(1)}, f32[4,1,16,128]{3,2,1,0:T(8,128)S(1)}, u32[]{:S(2)}, u32[]{:S(2)}) collective-permute-start(f32[4,1,16,128]{3,2,1,0:T(8,128)S(1)} %get-tuple-element.34), channel_id=1, source_target_pairs={{0,16},{8,24},{16,0},{24,8},{1,17},{9,25},{17,1},{25,9},{2,18},{10... | collective-permute-start | bytes 98312 | tf_op jit(solution)/shard_map/ppermute | solution.py:263
  232.8 7.1 %collective-permute-start.29 = (f16[1024,128]{1,0:T(8,128)(2,1)S(1)}, f16[1024,128]{1,0:T(8,128)(2,1)S(1)}, u32[]{:S(2)}, u32[]{:S(2)}) collective-permute-start(f16[1024,128]{1,0:T(8,128)(2,1)S(1)} %collective-permute-done.25), channel_id=1, source_target_pairs={{0,16},{8,24},{16,0},{24,8},{1,17},{9,25},{17,1},{25,9},{2,18},{10... | collective-permute-start | bytes 786440 | tf_op jit(solution)/shard_map/ppermute | solution.py:273
  235.6 9.2 %collective-permute-start.30 = (f16[1024,128]{1,0:T(8,128)(2,1)S(1)}, f16[1024,128]{1,0:T(8,128)(2,1)S(1)}, u32[]{:S(2)}, u32[]{:S(2)}) collective-permute-start(f16[1024,128]{1,0:T(8,128)(2,1)S(1)} %collective-permute-done.28), channel_id=1, source_target_pairs={{0,8},{8,0},{16,24},{24,16},{1,9},{9,1},{17,25},{25,17},{2,10},{10... | collective-permute-start | bytes 786440 | tf_op jit(solution)/shard_map/ppermute | solution.py:273
  248.1 6.4 %collective-permute-start.31 = (f16[1024,128]{1,0:T(8,128)(2,1)S(1)}, f16[1024,128]{1,0:T(8,128)(2,1)S(1)}, u32[]{:S(2)}, u32[]{:S(2)}) collective-permute-start(f16[1024,128]{1,0:T(8,128)(2,1)S(1)} %get-tuple-element.27), channel_id=1, source_target_pairs={{0,8},{8,0},{16,24},{24,16},{1,9},{9,1},{17,25},{25,17},{2,10},{10... | collective-permute-start | bytes 786440 | tf_op jit(solution)/shard_map/ppermute | solution.py:273
  248.3 7.4 %collective-permute-start.34 = (f16[1024,128]{1,0:T(8,128)(2,1)S(1)}, f16[1024,128]{1,0:T(8,128)(2,1)S(1)}, u32[]{:S(2)}, u32[]{:S(2)}) collective-permute-start(f16[1024,128]{1,0:T(8,128)(2,1)S(1)} %get-tuple-element.26), channel_id=1, source_target_pairs={{0,16},{8,24},{16,0},{24,8},{1,17},{9,25},{17,1},{25,9},{2,18},{10... | collective-permute-start | bytes 786440 | tf_op jit(solution)/shard_map/ppermute | solution.py:273
  249.5 7.9 %collective-permute-start.32 = (f16[1024,128]{1,0:T(8,128)(2,1)S(1)}, f16[1024,128]{1,0:T(8,128)(2,1)S(1)}, u32[]{:S(2)}, u32[]{:S(2)}) collective-permute-start(f16[1024,128]{1,0:T(8,128)(2,1)S(1)} %get-tuple-element.26), channel_id=1, source_target_pairs={{0,8},{8,0},{16,24},{24,16},{1,9},{9,1},{17,25},{25,17},{2,10},{10... | collective-permute-start | bytes 786440 | tf_op jit(solution)/shard_map/ppermute | solution.py:273
  252.2 6.4 %collective-permute-start.33 = (f16[1024,128]{1,0:T(8,128)(2,1)S(1)}, f16[1024,128]{1,0:T(8,128)(2,1)S(1)}, u32[]{:S(2)}, u32[]{:S(2)}) collective-permute-start(f16[1024,128]{1,0:T(8,128)(2,1)S(1)} %get-tuple-element.27), channel_id=1, source_target_pairs={{0,16},{8,24},{16,0},{24,8},{1,17},{9,25},{17,1},{25,9},{2,18},{10... | collective-permute-start | bytes 786440 | tf_op jit(solution)/shard_map/ppermute | solution.py:273
  254.5 6.9 %collective-permute-start.35 = (f16[1024,128]{1,0:T(8,128)(2,1)S(1)}, f16[1024,128]{1,0:T(8,128)(2,1)S(1)}, u32[]{:S(2)}, u32[]{:S(2)}) collective-permute-start(f16[1024,128]{1,0:T(8,128)(2,1)S(1)} %collective-permute-done.31), channel_id=1, source_target_pairs={{0,16},{8,24},{16,0},{24,8},{1,17},{9,25},{17,1},{25,9},{2,18},{10... | collective-permute-start | bytes 786440 | tf_op jit(solution)/shard_map/ppermute | solution.py:273
  255.7 6.5 %collective-permute-start.36 = (f16[1024,128]{1,0:T(8,128)(2,1)S(1)}, f16[1024,128]{1,0:T(8,128)(2,1)S(1)}, u32[]{:S(2)}, u32[]{:S(2)}) collective-permute-start(f16[1024,128]{1,0:T(8,128)(2,1)S(1)} %collective-permute-done.34), channel_id=1, source_target_pairs={{0,8},{8,0},{16,24},{24,16},{1,9},{9,1},{17,25},{25,17},{2,10},{10... | collective-permute-start | bytes 786440 | tf_op jit(solution)/shard_map/ppermute | solution.py:273
  (24 other events, 143.7 us)

commit v2 on v1

v2 whole, which is shorter than its diff:
```python
import functools

import jax
import jax.numpy as jnp
from jax import lax
from jax.experimental import pallas as pl
from jax.experimental.pallas import tpu as pltpu
from jax.sharding import PartitionSpec as P

inverse_temp = 2.0
prior_weight = 0.05
safe_sum = 1e30
code_scale = 2.0**18
vmem_bytes = 56 * 1024 * 1024


def divisor(count, most):
    size = min(count, most)
    while count % size:
        size //= 2
    return size


def dot_nt(a, b):
    return lax.dot_general(a, b, (((1,), (1,)), ((), ())), preferred_element_type=jnp.float32)


def fold_rows(x, combine):
    parts = [x[k * 8 : (k + 1) * 8, :] for k in range(x.shape[0] // 8)]
    while len(parts) > 1:
        half = len(parts) // 2
        parts = [combine(parts[2 * k], parts[2 * k + 1]) for k in range(half)] + parts[2 * half :]
    return parts[0]


def stats_kernel(sub_rows, tok_cols, tok_ref, cent_ref, out_ref, flip_ref, base_ref, shift_ref, sums_ref):
    step = pl.program_id(0)
    tok_count = tok_ref.shape[0]
    tile = divisor(sub_rows, 1024)
    subs = cent_ref.shape[0] // sub_rows
    col_blocks = tok_count // tok_cols

    def columns(t):
        return pl.ds(pl.multiple_of(t * tok_cols, tok_cols), tok_cols)

    def dot(a, b):
        return jnp.dot(a, b, preferred_element_type=jnp.float32)

    @pl.when(step == 0)
    def _():
        @pl.loop(0, col_blocks)
        def _(t):
            flipped = (tok_ref[columns(t), :] * jnp.bfloat16(inverse_temp)).T
            flip_ref[:, columns(t)] = flipped
            logits = dot(cent_ref[0:128, :], flipped)
            top = jnp.max(fold_rows(logits, jnp.maximum), axis=0, keepdims=True)
            base_ref[:, columns(t)] = top

    @pl.loop(0, col_blocks)
    def _(t):
        rhs = flip_ref[:, columns(t)]
        shift = base_ref[:, columns(t)]
        for sub in range(subs):
            total = jnp.zeros((8, tok_cols), jnp.float32)
            for k in range(sub_rows // tile):
                logits = dot(cent_ref[pl.ds(sub * sub_rows + k * tile, tile), :], rhs)
                total = total + fold_rows(jnp.exp(logits - shift), jnp.add)
            sums_ref[step * subs + sub, :, columns(t)] = total
            shift_ref[step * subs + sub, :, columns(t)] = shift

    worst = jnp.max(sums_ref[pl.ds(step * subs, subs), :, :])

    @pl.when(jnp.logical_not(worst < safe_sum))
    def _():
        @pl.loop(0, col_blocks)
        def _(t):
            worst_t = jnp.max(sums_ref[pl.ds(step * subs, subs), :, columns(t)])

            @pl.when(jnp.logical_not(worst_t < safe_sum))
            def _():
                @pl.loop(0, subs)
                def _(sub):
                    worst_s = jnp.max(sums_ref[step * subs + sub, :, columns(t)])

                    @pl.when(jnp.logical_not(worst_s < safe_sum))
                    def _():
                        rhs = flip_ref[:, columns(t)]
                        lowest = base_ref[:, columns(t)]

                        def logits_of(k):
                            first = pl.multiple_of(sub * sub_rows + k * tile, tile)
                            return dot(cent_ref[pl.ds(first, tile), :], rhs)

                        def raise_top(k, top):
                            return jnp.maximum(top, fold_rows(logits_of(k), jnp.maximum))

                        top = lax.fori_loop(
                            0, sub_rows // tile, raise_top, jnp.broadcast_to(lowest, (8, tok_cols))
                        )
                        top = jnp.max(top, axis=0, keepdims=True)

                        def add_up(k, total):
                            return total + fold_rows(jnp.exp(logits_of(k) - top), jnp.add)

                        total = lax.fori_loop(
                            0, sub_rows // tile, add_up, jnp.zeros((8, tok_cols), jnp.float32)
                        )
                        sums_ref[step * subs + sub, :, columns(t)] = total
                        shift_ref[step * subs + sub, :, columns(t)] = top

    @pl.when(step == pl.num_programs(0) - 1)
    def _():
        @pl.loop(0, col_blocks)
        def _(t):
            shifts = shift_ref[:, :, columns(t)]
            top = jnp.max(shifts, axis=0)
            scale = jnp.exp(shifts - top[None])
            total = jnp.sum(sums_ref[:, :, columns(t)] * scale, axis=0)
            total = jnp.sum(total, axis=0, keepdims=True)
            out_ref[:, columns(t)] = top + jnp.log(total)


def local_lse(tokens, centroids):
    tok_count, width = tokens.shape
    cent_count = centroids.shape[0]
    block_rows = divisor(cent_count, 4096)
    sub_rows = divisor(block_rows, 1024)
    tok_cols = divisor(tok_count, 512)
    blocks = cent_count // block_rows
    subs = cent_count // sub_rows
    return pl.pallas_call(
        functools.partial(stats_kernel, sub_rows, tok_cols),
        grid=(blocks,),
        in_specs=[
            pl.BlockSpec((tok_count, width), lambda j: (0, 0)),
            pl.BlockSpec((block_rows, width), lambda j: (j, 0)),
        ],
        out_specs=pl.BlockSpec((1, tok_count), lambda j: (0, 0)),
        out_shape=jax.ShapeDtypeStruct((1, tok_count), jnp.float32),
        scratch_shapes=[
            pltpu.VMEM((width, tok_count), jnp.bfloat16),
            pltpu.VMEM((1, tok_count), jnp.float32),
            pltpu.VMEM((subs, 1, tok_count), jnp.float32),
            pltpu.VMEM((subs, 8, tok_count), jnp.float32),
        ],
        compiler_params=pltpu.CompilerParams(vmem_limit_bytes=vmem_bytes),
        cost_estimate=pl.CostEstimate(
            flops=2 * tok_count * cent_count * width,
            bytes_accessed=(tok_count + cent_count) * width * 2,
            transcendentals=tok_count * cent_count,
        ),
        name="row_stats",
    )(tokens, centroids)


def encoded(x):
    x = x * code_scale
    square = x * x
    return (square * square * x).astype(jnp.bfloat16)


def decoded(code):
    code = code.astype(jnp.float32)
    size = jnp.exp2(jnp.log2(jnp.abs(code)) * 0.2) * (1.0 / code_scale)
    return jnp.where(code < 0, -size, size)


def update_kernel(shards, place_ref, *refs):
    tok_refs, lse_refs = refs[:shards], refs[shards : 2 * shards]
    cent_ref, new_ref, mass_ref, toks_ref, lses_ref, weights_ref, total_ref, sems = refs[2 * shards :]
    rows, width = cent_ref.shape
    shard_rows = tok_refs[0].shape[0]
    depth = weights_ref.shape[2]
    pieces = shards * shard_rows // depth
    piece = divisor(depth, 512)

    @pl.when(pl.program_id(0) == 0)
    def _():
        copies = []
        for s in range(shards):
            span = pl.ds(s * shard_rows, shard_rows)
            copies.append(pltpu.make_async_copy(tok_refs[s], toks_ref.at[span, :], sems.at[2 * s]))
            copies.append(pltpu.make_async_copy(lse_refs[s], lses_ref.at[:, span], sems.at[2 * s + 1]))
        for copy in copies:
            copy.start()
        for copy in copies:
            copy.wait()

    cents = cent_ref[...] * jnp.bfloat16(inverse_temp)

    def weigh(n):
        for k in range(depth // piece):
            span = pl.ds(pl.multiple_of(n * depth + k * piece, piece), piece)
            logits = dot_nt(cents, toks_ref[span, :])
            weights = jnp.exp(logits - lses_ref[:, span])
            weights_ref[lax.rem(n, 2), :, pl.ds(k * piece, piece)] = weights.astype(jnp.bfloat16)

    def gather_up(n):
        toks = toks_ref[pl.ds(pl.multiple_of(n * depth, depth), depth), :]
        rhs = jnp.concatenate([toks, jnp.ones_like(toks)], axis=1)
        return jnp.dot(weights_ref[lax.rem(n, 2)], rhs, preferred_element_type=jnp.float32)

    weigh(0)
    total_ref[...] = jnp.zeros_like(total_ref)

    @pl.loop(1, pieces)
    def _(n):
        weigh(n)
        total_ref[...] += gather_up(n - 1)

    total = total_ref[...] + gather_up(pieces - 1)
    mass = total[:, width:]
    prior = prior_weight * cent_ref[...].astype(jnp.float32)
    new_ref[...] = encoded((total[:, :width] + prior) / (mass + prior_weight))
    diagonal = lax.broadcasted_iota(jnp.int32, (128, 128), 0) == lax.broadcasted_iota(
        jnp.int32, (128, 128), 1
    )
    for k in range(rows // 128):
        square = jnp.where(diagonal, mass[k * 128 : (k + 1) * 128, :], 0.0)
        mass_ref[k] = jnp.sum(square, axis=0, keepdims=True)


def updated_chunk(block, toks, lses, centroids, rows, block_rows):
    shards = len(toks)
    shard_rows, width = toks[0].shape
    all_count = shards * shard_rows
    depth = divisor(all_count, 1024)
    anywhere = pl.BlockSpec(memory_space=pl.ANY)
    return pl.pallas_call(
        functools.partial(update_kernel, shards),
        grid_spec=pltpu.PrefetchScalarGridSpec(
            num_scalar_prefetch=1,
            grid=(rows // block_rows,),
            in_specs=[anywhere] * (2 * shards)
            + [pl.BlockSpec((block_rows, width), lambda j, place: (place[0] + j, 0))],
            out_specs=[
                pl.BlockSpec((block_rows, width), lambda j, place: (j, 0)),
                pl.BlockSpec((block_rows // 128, 1, 128), lambda j, place: (j, 0, 0)),
            ],
            scratch_shapes=[
                pltpu.VMEM((all_count, width), jnp.bfloat16),
                pltpu.VMEM((1, all_count), jnp.float32),
                pltpu.VMEM((2, block_rows, depth), jnp.bfloat16),
                pltpu.VMEM((block_rows, 2 * width), jnp.float32),
                pltpu.SemaphoreType.DMA((2 * shards,)),
            ],
        ),
        out_shape=[
            jax.ShapeDtypeStruct((rows, width), jnp.bfloat16),
            jax.ShapeDtypeStruct((rows // 128, 1, 128), jnp.float32),
        ],
        compiler_params=pltpu.CompilerParams(vmem_limit_bytes=vmem_bytes),
        cost_estimate=pl.CostEstimate(
            flops=6 * all_count * rows * width,
            bytes_accessed=(2 * all_count + 4 * rows) * width,
            transcendentals=all_count * rows,
        ),
        name="new_rows",
    )(block, *toks, *lses, centroids)


def place_kernel(code_ref, base_ref, out_ref):
    out_ref[...] = decoded(code_ref[...])


def placed_rows(base, codes, first):
    rows, width = codes.shape
    block_rows = divisor(rows, 2048)
    while first % block_rows:
        block_rows //= 2
    offset = first // block_rows
    return pl.pallas_call(
        place_kernel,
        grid=(rows // block_rows,),
        in_specs=[
            pl.BlockSpec((block_rows, width), lambda j: (j, 0)),
            pl.BlockSpec(memory_space=pl.ANY),
        ],
        out_specs=pl.BlockSpec((block_rows, width), lambda j: (offset + j, 0)),
        out_shape=jax.ShapeDtypeStruct(base.shape, base.dtype),
        input_output_aliases={1: 0},
        compiler_params=pltpu.CompilerParams(vmem_limit_bytes=vmem_bytes),
        cost_estimate=pl.CostEstimate(
            flops=10 * rows * width, bytes_accessed=6 * rows * width, transcendentals=2 * rows * width
        ),
        name="placed_rows",
    )(codes, base)


def combine_kernel(*refs):
    parts, out_ref = [ref[...] for ref in refs[:-1]], refs[-1]
    top = functools.reduce(jnp.maximum, parts)
    out_ref[...] = top + jnp.log(sum(jnp.exp(part - top) for part in parts))


def combined_lse(parts):
    return pl.pallas_call(
        combine_kernel, out_shape=jax.ShapeDtypeStruct(parts[0].shape, jnp.float32), name="join_stats"
    )(*parts)


def blank(shape):
    return pl.pallas_call(
        lambda out_ref: None,
        out_specs=pl.BlockSpec(memory_space=pl.ANY),
        out_shape=jax.ShapeDtypeStruct(shape, jnp.float32),
        name="blank",
    )()


def from_others(value, axis):
    size = lax.axis_size(axis)
    found = [value]
    for shift in range(1, size):
        found.append(lax.ppermute(value, axis, [(k, (k + shift) % size) for k in range(size)]))
    return found


def chunk_plan(share_rows, block_rows):
    blocks = share_rows // block_rows
    plan = []
    while blocks > 2:
        plan.append(2)
        blocks -= 2
    return plan + [1] * blocks


def local(tokens, centroids):
    tok_size = lax.axis_size("tok")
    me = lax.axis_index("tok")
    cent_count, width = centroids.shape
    share_rows = cent_count // tok_size

    toks = from_others(tokens, "tok")
    own_lse = combined_lse(from_others(local_lse(tokens, centroids), "cent"))
    lses = from_others(own_lse, "tok")

    block_rows = divisor(share_rows, 1024)
    updated = blank((cent_count, width))
    masses, first = [], 0
    for blocks in chunk_plan(share_rows, block_rows):
        block = first * tok_size + me * blocks
        rows = blocks * block_rows
        codes, mass = updated_chunk(block.reshape(1), toks, lses, centroids, rows, block_rows)
        codes = lax.all_gather(codes, "tok", axis=0, tiled=True)
        updated = placed_rows(updated, codes, first * tok_size * block_rows)
        masses.append(mass.reshape(rows // 128, 128))
        first += blocks
    found = from_others(jnp.concatenate(masses), "tok")
    parts, done = [], 0
    for mass in masses:
        count = mass.shape[0]
        index = lax.broadcasted_iota(jnp.int32, (tok_size, 1, 1), 0)
        source = (me - index) % tok_size
        part = found[0][None, done : done + count]
        for s in range(1, tok_size):
            part = jnp.where(source == s, found[s][None, done : done + count], part)
        parts.append(part.reshape(tok_size * count, 128))
        done += count
    return updated, jnp.concatenate(parts).reshape(cent_count)


def solution(mesh):
    placed = (P("tok", None), P("cent", None))
    return jax.shard_map(
        local, mesh=mesh, in_specs=placed, out_specs=(P("cent", None), P("cent")), check_vma=False
    )
```

time: 266 us -> 299 us (1.12)
  waiting for transfers between devices: 37.9 us -> 74.9 us
  Pallas kernels: 155 us -> 191 us
  other arithmetic: 30.6 us -> 0.28 us
  starting transfers between devices: 36.4 us -> 13.1 us
  between operations: 0.98 us -> 14.1 us
    all_gather x0 -> x5, waiting for transfers between devices: none -> 51.5 us  [local(): codes = lax.all_gather(codes, 'tok', axis=0, tiled=True)]
    dynamic_update_slice x28 -> x0, other arithmetic: 29.1 us -> none  [local(): lax.dynamic_update_slice(updated, part.astype(jnp.float32), (start, 0))]
    pallas_call x4 -> x5, Pallas kernels: 89.1 us -> 115 us  [updated_chunk(): pl.pallas_call(functools.partial(update_kernel, shards), grid_spec=pltpu....]
    ppermute x24 -> x0, starting transfers between devices: 23.4 us -> none  [swap(): return lax.ppermute(part, 'tok', [(k, k ^ mask) for k in range(4)])]
    pallas_call x0 -> x5, Pallas kernels: none -> 19.4 us  [placed_rows(): pl.pallas_call(place_kernel, grid=(rows // block_rows,), in_specs=[pl.Blo...]
    ppermute x24 -> x0, waiting for transfers between devices: 18 us -> none  [swap(): return lax.ppermute(part, 'tok', [(k, k ^ mask) for k in range(4)])]
    pallas_call x1, Pallas kernels: 64 us -> 55.2 us  [local_lse(): pl.pallas_call(functools.partial(stats_kernel, sub_rows, tok_cols), grid=...]
    ppermute x16, waiting for transfers between devices: 19.9 us -> 23.3 us  [from_others(): lax.ppermute(value, axis, [(k, (k + shift) % size) for k in range(size)])]
  transfers between devices with their start and end apart: 40 -> 21, of which waited for: 19 -> 13; matrix products, arithmetic and copies ran while one was open for 8% -> 1% of each run, Pallas kernels for 50% -> 54%
where the time goes in v2:
time: 299 us; the launch traced here: 298 us
  Pallas kernels  191 us (64%)
  waiting for transfers between devices  74.9 us (25%)
  between operations  14.1 us (5%)
  starting transfers between devices  13.1 us (4%)
  local copies, waits for them, and re-layouts  4.82 us (2%)
    pallas_call x5, Pallas kernels, updated_chunk(): pl.pallas_call(functools.partial(update_kernel, shards), grid_spec=pltpu....  115 us
    pallas_call x1, Pallas kernels, local_lse(): pl.pallas_call(functools.partial(stats_kernel, sub_rows, tok_cols), grid=...  55.2 us
    all_gather x5, waiting for transfers between devices, local(): codes = lax.all_gather(codes, 'tok', axis=0, tiled=True)  51.5 us
    ppermute x16, waiting for transfers between devices, from_others(): lax.ppermute(value, axis, [(k, (k + shift) % size) for k in range(size)])  23.3 us
    pallas_call x5, Pallas kernels, placed_rows(): pl.pallas_call(place_kernel, grid=(rows // block_rows,), in_specs=[pl.Blo...  19.4 us
    ppermute x16, starting transfers between devices, from_others(): lax.ppermute(value, axis, [(k, (k + shift) % size) for k in range(size)])  12.8 us
  transfers between devices with their start and end apart: 21, of which 13 were waited for; matrix products, arithmetic and copies ran while one was open for 1% of the time, Pallas kernels for 54%

profile of v2, /device:TPU:0, one launch (start us, length us, event | category | flops | bytes accessed | tf_op | source)
XLA Modules:
  0.0 298.0 jit_solution(972082366458562087)
XLA Ops:
  7.2 3.0 %collective-permute-start = (bf16[2048,128]{1,0:T(8,128)(2,1)}, bf16[2048,128]{1,0:T(8,128)(2,1)S(1)}, u32[]{:S(2)}, u32[]{:S(2)}) collective-permute-start(bf16[2048,128]{1,0:T(8,128)(2,1)} %refs_0_.9), channel_id=1, source_target_pairs={{0,8},{8,16},{16,24},{24,0},{1,9},{9,17},{17,25},{25,1},{2,10},{10... | collective-permute-start | bytes 1572872 | tf_op jit(solution)/shard_map/ppermute | solution.py:315
  10.2 1.5 collective-permute-start.1
  11.7 1.4 collective-permute-start.2
  13.2 55.2 %row_stats.1.refs_0_ = f32[1,2048]{1,0:T(1,128)} custom-call(bf16[2048,128]{1,0:T(8,128)(2,1)} %refs_0_.9, bf16[32768,128]{1,0:T(8,128)(2,1)} %refs_8_.9), custom_call_target="tpu_custom_call" | custom-call | flops 17179869184 | bytes 8912896 | tf_op jit(solution)/shard_map/row_stats/pallas_call | solution.py:131
  68.4 5.1 %collective-permute-done.3.refs_1_ = f32[1,2048]{1,0:T(1,128)S(1)} collective-permute-done((f32[1,2048]{1,0:T(1,128)}, f32[1,2048]{1,0:T(1,128)S(1)}, u32[]{:S(2)}, u32[]{:S(2)}) %collective-permute-start.3) | collective-permute-done | bytes 8224 | tf_op jit(solution)/shard_map/ppermute | solution.py:315
  74.1 3.6 %collective-permute-done.5.refs_3_ = f32[1,2048]{1,0:T(1,128)S(1)} collective-permute-done((f32[1,2048]{1,0:T(1,128)}, f32[1,2048]{1,0:T(1,128)S(1)}, u32[]{:S(2)}, u32[]{:S(2)}) %collective-permute-start.5) | collective-permute-done | bytes 8224 | tf_op jit(solution)/shard_map/ppermute | solution.py:315
  77.6 1.2 collective-permute-done.6.refs_4_
  79.4 1.5 collective-permute-done.7.refs_5_
  80.9 1.8 collective-permute-done.8.refs_6_
  83.9 1.4 join_stats.1.refs_4_
  85.3 1.9 collective-permute-start.11
  87.2 2.9 collective-permute-done.10.refs_5_
  90.5 3.4 %collective-permute-done.12.refs_7_ = f32[1,2048]{1,0:T(1,128)S(1)} collective-permute-done((f32[1,2048]{1,0:T(1,128)}, f32[1,2048]{1,0:T(1,128)S(1)}, u32[]{:S(2)}, u32[]{:S(2)}) %collective-permute-start.12) | collective-permute-done | bytes 8224 | tf_op jit(solution)/shard_map/ppermute | solution.py:315
  95.2 27.7 %new_rows.9 = (bf16[2048,128]{1,0:T(8,128)(2,1)}, f32[16,1,128]{2,1,0:T(1,128)}) custom-call(s32[1]{0:T(128)} %bitcast.4.place_ref, bf16[2048,128]{1,0:T(8,128)(2,1)} %refs_0_.9, bf16[2048,128]{1,0:T(8,128)(2,1)} %copy-done.13, bf16[2048,128]{1,0:T(8,128)(2,1)} %copy-done.14, bf16[2048,128]{1,0:T(8,128)(2,1)} %copy-done.15, f32[1,2048]{1,0:T(1,128)} %join_stats.1.refs_4_, ...), custom_call_target="tpu_custom_call" | custom-call | flops 12884901888 | bytes 3145728 | tf_op jit(solution)/shard_map/new_rows/pallas_call | solution.py:229
  123.0 27.8 %new_rows.8 = (bf16[2048,128]{1,0:T(8,128)(2,1)}, f32[16,1,128]{2,1,0:T(1,128)}) custom-call(s32[1]{0:T(128)} %bitcast.3.place_ref, bf16[2048,128]{1,0:T(8,128)(2,1)} %refs_0_.9, bf16[2048,128]{1,0:T(8,128)(2,1)} %copy-done.13, bf16[2048,128]{1,0:T(8,128)(2,1)} %copy-done.14, bf16[2048,128]{1,0:T(8,128)(2,1)} %copy-done.15, f32[1,2048]{1,0:T(1,128)} %join_stats.1.refs_4_, ...), custom_call_target="tpu_custom_call" | custom-call | flops 12884901888 | bytes 3145728 | tf_op jit(solution)/shard_map/new_rows/pallas_call | solution.py:229
  151.1 27.8 %new_rows.7 = (bf16[2048,128]{1,0:T(8,128)(2,1)}, f32[16,1,128]{2,1,0:T(1,128)}) custom-call(s32[1]{0:T(128)} %bitcast.2.place_ref, bf16[2048,128]{1,0:T(8,128)(2,1)} %refs_0_.9, bf16[2048,128]{1,0:T(8,128)(2,1)} %copy-done.13, bf16[2048,128]{1,0:T(8,128)(2,1)} %copy-done.14, bf16[2048,128]{1,0:T(8,128)(2,1)} %copy-done.15, f32[1,2048]{1,0:T(1,128)} %join_stats.1.refs_4_, ...), custom_call_target="tpu_custom_call" | custom-call | flops 12884901888 | bytes 3145728 | tf_op jit(solution)/shard_map/new_rows/pallas_call | solution.py:229
  179.0 15.9 %new_rows.6 = (bf16[1024,128]{1,0:T(8,128)(2,1)}, f32[8,1,128]{2,1,0:T(1,128)}) custom-call(s32[1]{0:T(128)} %bitcast.1.place_ref, bf16[2048,128]{1,0:T(8,128)(2,1)} %refs_0_.9, bf16[2048,128]{1,0:T(8,128)(2,1)} %copy-done.13, bf16[2048,128]{1,0:T(8,128)(2,1)} %copy-done.14, bf16[2048,128]{1,0:T(8,128)(2,1)} %copy-done.15, f32[1,2048]{1,0:T(1,128)} %join_stats.1.refs_4_, ...), custom_call_target="tpu_custom_call" | custom-call | flops 6442450944 | bytes 2621440 | tf_op jit(solution)/shard_map/new_rows/pallas_call | solution.py:229
  195.7 15.5 %new_rows.5 = (bf16[1024,128]{1,0:T(8,128)(2,1)}, f32[8,1,128]{2,1,0:T(1,128)}) custom-call(s32[1]{0:T(128)} %bitcast.place_ref, bf16[2048,128]{1,0:T(8,128)(2,1)} %refs_0_.9, bf16[2048,128]{1,0:T(8,128)(2,1)} %copy-done.13, bf16[2048,128]{1,0:T(8,128)(2,1)} %copy-done.14, bf16[2048,128]{1,0:T(8,128)(2,1)} %copy-done.15, f32[1,2048]{1,0:T(1,128)} %join_stats.1.refs_4_, ...), custom_call_target="tpu_custom_call" | custom-call | flops 6442450944 | bytes 2621440 | tf_op jit(solution)/shard_map/new_rows/pallas_call | solution.py:229
  211.2 0.7 constant_dynamic-update-slice_fusion
  211.9 1.0 collective-permute-start.13
  213.9 1.5 collective-permute-start.14
  215.4 1.5 collective-permute-start.15
  216.9 0.9 collective-permute-done.14
  217.8 2.4 collective-permute-done.15
  220.6 4.7 %placed_rows.5.base_ref = f32[32768,128]{1,0:T(8,128)} custom-call(bf16[8192,128]{1,0:T(8,128)(2,1)} %all-gather.14.cloned.1.call-done.code_ref, f32[32768,128]{1,0:T(8,128)} %blank.1.base_ref), custom_call_target="tpu_custom_call", output_to_operand_aliasing={{}: (1, {})} | custom-call | flops 10485760 | bytes 6291456 | tf_op jit(solution)/shard_map/placed_rows/pallas_call | solution.py:272
  225.3 4.7 %placed_rows.6.base_ref = f32[32768,128]{1,0:T(8,128)} custom-call(bf16[8192,128]{1,0:T(8,128)(2,1)} %all-gather.12.cloned.1.call-done.code_ref, f32[32768,128]{1,0:T(8,128)} %placed_rows.5.base_ref), custom_call_target="tpu_custom_call", output_to_operand_aliasing={{}: (1, {})} | custom-call | flops 10485760 | bytes 6291456 | tf_op jit(solution)/shard_map/placed_rows/pallas_call | solution.py:272
  230.0 2.1 all-gather.10.cloned.1.call-done.code_ref
  232.1 4.7 %placed_rows.7.base_ref = f32[32768,128]{1,0:T(8,128)} custom-call(bf16[8192,128]{1,0:T(8,128)(2,1)} %all-gather.10.cloned.1.call-done.code_ref, f32[32768,128]{1,0:T(8,128)} %placed_rows.6.base_ref), custom_call_target="tpu_custom_call", output_to_operand_aliasing={{}: (1, {})} | custom-call | flops 10485760 | bytes 6291456 | tf_op jit(solution)/shard_map/placed_rows/pallas_call | solution.py:272
  236.8 23.7 %all-gather.8.cloned.1.call-done.code_ref = bf16[4096,128]{1,0:T(8,128)(2,1)} async-done(((bf16[1024,128]{1,0:T(8,128)(2,1)}), bf16[4096,128]{1,0:T(8,128)(2,1)}) %all-gather.8.cloned.1.call-update) | async-done | bytes 1048592 | tf_op jit(solution)/shard_map/all_gather | solution.py:345
  260.5 2.7 placed_rows.8.base_ref
  263.1 25.7 %all-gather.6.cloned.1.call-done.code_ref = bf16[4096,128]{1,0:T(8,128)(2,1)} async-done(((bf16[1024,128]{1,0:T(8,128)(2,1)}), bf16[4096,128]{1,0:T(8,128)(2,1)}) %all-gather.6.cloned.1.call-update) | async-done | bytes 1048592 | tf_op jit(solution)/shard_map/all_gather | solution.py:345
  288.8 2.7 placed_rows.9
  (97 shorter events, 6.5 us)
Async XLA Ops:
  7.2 213.4 %all-gather.14.cloned.1.call-start = ((), (), s32[]{:S(2)}) async-start(), calls=%async_computation.4 | async-start | bytes 2621440 | tf_op jit(solution)/shard_map/all_gather | solution.py:345
  7.2 86.8 %collective-permute-start = (bf16[2048,128]{1,0:T(8,128)(2,1)}, bf16[2048,128]{1,0:T(8,128)(2,1)S(1)}, u32[]{:S(2)}, u32[]{:S(2)}) collective-permute-start(bf16[2048,128]{1,0:T(8,128)(2,1)} %refs_0_.9), channel_id=1, source_target_pairs={{0,8},{8,16},{16,24},{24,0},{1,9},{9,17},{17,25},{25,1},{2,10},{10... | collective-permute-start | bytes 1572872 | tf_op jit(solution)/shard_map/ppermute | solution.py:315
  10.2 83.8 %collective-permute-start.1 = (bf16[2048,128]{1,0:T(8,128)(2,1)}, bf16[2048,128]{1,0:T(8,128)(2,1)S(1)}, u32[]{:S(2)}, u32[]{:S(2)}) collective-permute-start(bf16[2048,128]{1,0:T(8,128)(2,1)} %refs_0_.9), channel_id=1, source_target_pairs={{0,16},{8,24},{16,0},{24,8},{1,17},{9,25},{17,1},{25,9},{2,18},{10... | collective-permute-start | bytes 1572872 | tf_op jit(solution)/shard_map/ppermute | solution.py:315
  11.7 82.3 %collective-permute-start.2 = (bf16[2048,128]{1,0:T(8,128)(2,1)}, bf16[2048,128]{1,0:T(8,128)(2,1)S(1)}, u32[]{:S(2)}, u32[]{:S(2)}) collective-permute-start(bf16[2048,128]{1,0:T(8,128)(2,1)} %refs_0_.9), channel_id=1, source_target_pairs={{0,24},{8,0},{16,8},{24,16},{1,25},{9,1},{17,9},{25,17},{2,26},{10... | collective-permute-start | bytes 1572872 | tf_op jit(solution)/shard_map/ppermute | solution.py:315
  68.4 5.1 %collective-permute-start.3 = (f32[1,2048]{1,0:T(1,128)}, f32[1,2048]{1,0:T(1,128)S(1)}, u32[]{:S(2)}, u32[]{:S(2)}) collective-permute-start(f32[1,2048]{1,0:T(1,128)} %row_stats.1.refs_0_), channel_id=1, source_target_pairs={{0,1},{1,2},{2,3},{3,4},{4,5},{5,6},{6,7},{7,0},{8,9},{9,10},{10,1... | collective-permute-start | bytes 24584 | tf_op jit(solution)/shard_map/ppermute | solution.py:315
  68.4 5.7 %collective-permute-start.4 = (f32[1,2048]{1,0:T(1,128)}, f32[1,2048]{1,0:T(1,128)S(1)}, u32[]{:S(2)}, u32[]{:S(2)}) collective-permute-start(f32[1,2048]{1,0:T(1,128)} %row_stats.1.refs_0_), channel_id=1, source_target_pairs={{0,2},{1,3},{2,4},{3,5},{4,6},{5,7},{6,0},{7,1},{8,10},{9,11},{10,... | collective-permute-start | bytes 24584 | tf_op jit(solution)/shard_map/ppermute | solution.py:315
  73.4 9.2 %copy-start.5 = (f32[1,2048]{1,0:T(1,128)}, f32[1,2048]{1,0:T(1,128)S(1)}, u32[]{:S(2)}) copy-start(f32[1,2048]{1,0:T(1,128)S(1)} %collective-permute-done.3.refs_1_) | copy-start | bytes 24580
  73.4 4.2 %collective-permute-start.5 = (f32[1,2048]{1,0:T(1,128)}, f32[1,2048]{1,0:T(1,128)S(1)}, u32[]{:S(2)}, u32[]{:S(2)}) collective-permute-start(f32[1,2048]{1,0:T(1,128)} %row_stats.1.refs_0_), channel_id=1, source_target_pairs={{0,3},{1,4},{2,5},{3,6},{4,7},{5,0},{6,1},{7,2},{8,11},{9,12},{10,... | collective-permute-start | bytes 24584 | tf_op jit(solution)/shard_map/ppermute | solution.py:315
  74.1 8.6 %copy-start.6 = (f32[1,2048]{1,0:T(1,128)}, f32[1,2048]{1,0:T(1,128)S(1)}, u32[]{:S(2)}) copy-start(f32[1,2048]{1,0:T(1,128)S(1)} %collective-permute-done.4.refs_2_) | copy-start | bytes 24580
  74.1 4.8 %collective-permute-start.6 = (f32[1,2048]{1,0:T(1,128)}, f32[1,2048]{1,0:T(1,128)S(1)}, u32[]{:S(2)}, u32[]{:S(2)}) collective-permute-start(f32[1,2048]{1,0:T(1,128)} %row_stats.1.refs_0_), channel_id=1, source_target_pairs={{0,4},{1,5},{2,6},{3,7},{4,0},{5,1},{6,2},{7,3},{8,12},{9,13},{10,... | collective-permute-start | bytes 24584 | tf_op jit(solution)/shard_map/ppermute | solution.py:315
  77.6 5.1 %copy-start.7 = (f32[1,2048]{1,0:T(1,128)}, f32[1,2048]{1,0:T(1,128)S(1)}, u32[]{:S(2)}) copy-start(f32[1,2048]{1,0:T(1,128)S(1)} %collective-permute-done.5.refs_3_) | copy-start | bytes 24580
  77.6 3.3 %collective-permute-start.7 = (f32[1,2048]{1,0:T(1,128)}, f32[1,2048]{1,0:T(1,128)S(1)}, u32[]{:S(2)}, u32[]{:S(2)}) collective-permute-start(f32[1,2048]{1,0:T(1,128)} %row_stats.1.refs_0_), channel_id=1, source_target_pairs={{0,5},{1,6},{2,7},{3,0},{4,1},{5,2},{6,3},{7,4},{8,13},{9,14},{10,... | collective-permute-start | bytes 24584 | tf_op jit(solution)/shard_map/ppermute | solution.py:315
  78.8 3.9 %copy-start.8 = (f32[1,2048]{1,0:T(1,128)}, f32[1,2048]{1,0:T(1,128)S(1)}, u32[]{:S(2)}) copy-start(f32[1,2048]{1,0:T(1,128)S(1)} %collective-permute-done.6.refs_4_) | copy-start | bytes 24580
  78.8 3.9 %collective-permute-start.8 = (f32[1,2048]{1,0:T(1,128)}, f32[1,2048]{1,0:T(1,128)S(1)}, u32[]{:S(2)}, u32[]{:S(2)}) collective-permute-start(f32[1,2048]{1,0:T(1,128)} %row_stats.1.refs_0_), channel_id=1, source_target_pairs={{0,6},{1,7},{2,0},{3,1},{4,2},{5,3},{6,4},{7,5},{8,14},{9,15},{10,... | collective-permute-start | bytes 24584 | tf_op jit(solution)/shard_map/ppermute | solution.py:315
  80.9 1.8 collective-permute-start.9
  85.3 4.8 %collective-permute-start.10 = (f32[1,2048]{1,0:T(1,128)}, f32[1,2048]{1,0:T(1,128)S(1)}, u32[]{:S(2)}, u32[]{:S(2)}) collective-permute-start(f32[1,2048]{1,0:T(1,128)} %join_stats.1.refs_4_), channel_id=1, source_target_pairs={{0,8},{8,16},{16,24},{24,0},{1,9},{9,17},{17,25},{25,1},{2,10},{10... | collective-permute-start | bytes 24584 | tf_op jit(solution)/shard_map/ppermute | solution.py:315
  85.3 5.2 %collective-permute-start.11 = (f32[1,2048]{1,0:T(1,128)}, f32[1,2048]{1,0:T(1,128)S(1)}, u32[]{:S(2)}, u32[]{:S(2)}) collective-permute-start(f32[1,2048]{1,0:T(1,128)} %join_stats.1.refs_4_), channel_id=1, source_target_pairs={{0,16},{8,24},{16,0},{24,8},{1,17},{9,25},{17,1},{25,9},{2,18},{10... | collective-permute-start | bytes 24584 | tf_op jit(solution)/shard_map/ppermute | solution.py:315
  90.1 3.9 %copy-start.16 = (f32[1,2048]{1,0:T(1,128)}, f32[1,2048]{1,0:T(1,128)S(1)}, u32[]{:S(2)}) copy-start(f32[1,2048]{1,0:T(1,128)S(1)} %collective-permute-done.10.refs_5_) | copy-start | bytes 24580
  90.1 3.9 %collective-permute-start.12 = (f32[1,2048]{1,0:T(1,128)}, f32[1,2048]{1,0:T(1,128)S(1)}, u32[]{:S(2)}, u32[]{:S(2)}) collective-permute-start(f32[1,2048]{1,0:T(1,128)} %join_stats.1.refs_4_), channel_id=1, source_target_pairs={{0,24},{8,0},{16,8},{24,16},{1,25},{9,1},{17,9},{25,17},{2,26},{10... | collective-permute-start | bytes 24584 | tf_op jit(solution)/shard_map/ppermute | solution.py:315
  123.0 102.3 %all-gather.12.cloned.1.call-start = ((), (), s32[]{:S(2)}) async-start(), calls=%async_computation.3 | async-start | bytes 2621440 | tf_op jit(solution)/shard_map/all_gather | solution.py:345
  150.8 81.3 %all-gather.10.cloned.1.call-start = ((), (), s32[]{:S(2)}) async-start(), calls=%async_computation.2 | async-start | bytes 2621440 | tf_op jit(solution)/shard_map/all_gather | solution.py:345
  178.8 16.1 %copy-start = (f32[16,1,128]{2,1,0:T(1,128)S(1)}, f32[16,1,128]{2,1,0:T(1,128)}, u32[]{:S(2)}) copy-start(f32[16,1,128]{2,1,0:T(1,128)} %get-tuple-element.17) | copy-start | bytes 24580
  178.9 16.1 %copy-start.1 = (f32[16,1,128]{2,1,0:T(1,128)S(1)}, f32[16,1,128]{2,1,0:T(1,128)}, u32[]{:S(2)}) copy-start(f32[16,1,128]{2,1,0:T(1,128)} %get-tuple-element.18) | copy-start | bytes 24580
  178.9 16.1 %copy-start.2 = (f32[16,1,128]{2,1,0:T(1,128)S(1)}, f32[16,1,128]{2,1,0:T(1,128)}, u32[]{:S(2)}) copy-start(f32[16,1,128]{2,1,0:T(1,128)} %get-tuple-element.19) | copy-start | bytes 24580
  178.9 81.6 %all-gather.8.cloned.1.call-start = ((), (), s32[]{:S(2)}) async-start(), calls=%async_computation.1 | async-start | bytes 1310720 | tf_op jit(solution)/shard_map/all_gather | solution.py:345
  194.9 94.0 %all-gather.6.cloned.1.call-start = ((), (), s32[]{:S(2)}) async-start(), calls=%async_computation | async-start | bytes 1310720 | tf_op jit(solution)/shard_map/all_gather | solution.py:345
  195.7 24.7 %copy-start.3 = (f32[8,1,128]{2,1,0:T(1,128)S(1)}, f32[8,1,128]{2,1,0:T(1,128)}, u32[]{:S(2)}) copy-start(f32[8,1,128]{2,1,0:T(1,128)} %get-tuple-element.20) | copy-start | bytes 12292
  211.2 9.3 %copy-start.4 = (f32[8,1,128]{2,1,0:T(1,128)S(1)}, f32[8,1,128]{2,1,0:T(1,128)}, u32[]{:S(2)}) copy-start(f32[8,1,128]{2,1,0:T(1,128)} %get-tuple-element.21) | copy-start | bytes 12292
  211.9 4.9 %collective-permute-start.13 = (f32[64,128]{1,0:T(8,128)S(1)}, f32[64,128]{1,0:T(8,128)S(1)}, u32[]{:S(2)}, u32[]{:S(2)}) collective-permute-start(f32[64,128]{1,0:T(8,128)S(1)} %constant_dynamic-update-slice_fusion), channel_id=1, source_target_pairs={{0,24},{8,0},{16,8},{24,16},{1,25},{9,1},{17,9},{25,17},{2,26},{10... | collective-permute-start | bytes 98312 | tf_op jit(solution)/shard_map/ppermute | solution.py:315
  213.9 3.9 %collective-permute-start.14 = (f32[64,128]{1,0:T(8,128)S(1)}, f32[64,128]{1,0:T(8,128)S(1)}, u32[]{:S(2)}, u32[]{:S(2)}) collective-permute-start(f32[64,128]{1,0:T(8,128)S(1)} %constant_dynamic-update-slice_fusion), channel_id=1, source_target_pairs={{0,16},{8,24},{16,0},{24,8},{1,17},{9,25},{17,1},{25,9},{2,18},{10... | collective-permute-start | bytes 98312 | tf_op jit(solution)/shard_map/ppermute | solution.py:315
  215.4 4.8 %collective-permute-start.15 = (f32[64,128]{1,0:T(8,128)S(1)}, f32[64,128]{1,0:T(8,128)S(1)}, u32[]{:S(2)}, u32[]{:S(2)}) collective-permute-start(f32[64,128]{1,0:T(8,128)S(1)} %constant_dynamic-update-slice_fusion), channel_id=1, source_target_pairs={{0,8},{8,16},{16,24},{24,0},{1,9},{9,17},{17,25},{25,1},{2,10},{10... | collective-permute-start | bytes 98312 | tf_op jit(solution)/shard_map/ppermute | solution.py:315
  220.5 4.8 %copy-start.12 = (f32[256,128]{1,0:T(8,128)}, f32[256,128]{1,0:T(8,128)S(1)}, u32[]{:S(2)}) copy-start(f32[256,128]{1,0:T(8,128)S(1)} %constant_dynamic-update-slice_fusion.5) | copy-start | bytes 393220
  (8 other events, 10.1 us)
Sparse Core Ops, SparseCore 0:
  123.1 34.1 all-gather.13
  159.2 35.3 all-gather.11
  196.4 35.7 all-gather.9
  233.8 26.6 all-gather.7
  262.2 26.6 all-gather.5

commit v3 on v2

v3 whole, which is shorter than its diff:
```python
import functools

import jax
import jax.numpy as jnp
from jax import lax
from jax.experimental import pallas as pl
from jax.experimental.pallas import tpu as pltpu
from jax.sharding import PartitionSpec as P

inverse_temp = 2.0
prior_weight = 0.05
safe_sum = 1e30
code_scale = 2.0**24
group_rows = 128
unit_size = 256
vmem_bytes = 56 * 1024 * 1024


def divisor(count, most):
    size = min(count, most)
    while count % size:
        size //= 2
    return size


def widened(x):
    return jnp.concatenate([x, jnp.zeros_like(x)], axis=1)


def fold_rows(x, combine):
    parts = [x[k * 8 : (k + 1) * 8, :] for k in range(x.shape[0] // 8)]
    while len(parts) > 1:
        half = len(parts) // 2
        parts = [combine(parts[2 * k], parts[2 * k + 1]) for k in range(half)] + parts[2 * half :]
    return parts[0]


def stats_kernel(sub_rows, tok_cols, tok_ref, cent_ref, out_ref, base_ref, shift_ref, sums_ref):
    step = pl.program_id(0)
    tok_count = tok_ref.shape[0]
    subs = cent_ref.shape[0] // sub_rows
    groups = sub_rows // group_rows
    col_blocks = tok_count // tok_cols
    units = tok_cols // unit_size

    def columns(t):
        return pl.ds(pl.multiple_of(t * tok_cols, tok_cols), tok_cols)

    def unit_columns(t, unit):
        return pl.ds(pl.multiple_of(t * tok_cols + unit * unit_size, unit_size), unit_size)

    def main(*accs):
        accs = [accs[unit * groups : (unit + 1) * groups] for unit in range(units)]

        def load_tokens(t):
            for unit in range(units):
                toks = tok_ref[unit_columns(t, unit), :] * jnp.bfloat16(inverse_temp)
                pltpu.matmul_push_rhs(widened(toks), 0, unit, transpose=True)

        def product(first, g, load):
            lhs = widened(cent_ref[pl.ds(first, group_rows), :])
            for unit in range(units):
                pltpu.matmul_acc_lhs(accs[unit][g], lhs, 0 if load else None)

        def logits_at(t, first):
            load_tokens(t)
            product(first, 0, True)
            return [pltpu.matmul_pop(accs[unit][0]) for unit in range(units)]

        @pl.when(step == 0)
        def _():
            @pl.loop(0, col_blocks)
            def _(t):
                for unit, logits in enumerate(logits_at(t, 0)):
                    top = jnp.max(fold_rows(logits, jnp.maximum), axis=0, keepdims=True)
                    base_ref[:, unit_columns(t, unit)] = top

        @pl.loop(0, col_blocks)
        def _(t):
            load_tokens(t)
            shifts = [base_ref[:, unit_columns(t, unit)] for unit in range(units)]
            for g in range(groups):
                product(g * group_rows, g, g == 0)
            for sub in range(subs):
                totals = [jnp.zeros((8, unit_size), jnp.float32)] * units
                for g in range(groups):
                    logits = [pltpu.matmul_pop(accs[unit][g]) for unit in range(units)]
                    if sub + 1 < subs:
                        product((sub + 1) * sub_rows + g * group_rows, g, False)
                    for unit in range(units):
                        scaled = jnp.exp(logits[unit] - shifts[unit])
                        totals[unit] = totals[unit] + fold_rows(scaled, jnp.add)
                for unit in range(units):
                    sums_ref[step * subs + sub, :, unit_columns(t, unit)] = totals[unit]
                    shift_ref[step * subs + sub, :, unit_columns(t, unit)] = shifts[unit]

        def redo(t, sub):
            def first_row(k):
                return pl.multiple_of(sub * sub_rows + k * group_rows, group_rows)

            def raise_tops(k, tops):
                parts = logits_at(t, first_row(k))
                return [jnp.maximum(top, fold_rows(part, jnp.maximum)) for top, part in zip(tops, parts)]

            lowest = [base_ref[:, unit_columns(t, unit)] for unit in range(units)]
            tops = [jnp.broadcast_to(low, (8, unit_size)) for low in lowest]
            tops = lax.fori_loop(0, groups, raise_tops, tops)
            tops = [jnp.max(top, axis=0, keepdims=True) for top in tops]

            def add_up(k, totals):
                parts = logits_at(t, first_row(k))
                return [
                    total + fold_rows(jnp.exp(part - top), jnp.add)
                    for total, part, top in zip(totals, parts, tops)
                ]

            totals = [jnp.zeros((8, unit_size), jnp.float32)] * units
            totals = lax.fori_loop(0, groups, add_up, totals)
            for unit in range(units):
                sums_ref[step * subs + sub, :, unit_columns(t, unit)] = totals[unit]
                shift_ref[step * subs + sub, :, unit_columns(t, unit)] = tops[unit]

        worst = jnp.max(sums_ref[pl.ds(step * subs, subs), :, :])

        @pl.when(jnp.logical_not(worst < safe_sum))
        def _():
            @pl.loop(0, col_blocks)
            def _(t):
                worst_t = jnp.max(sums_ref[pl.ds(step * subs, subs), :, columns(t)])

                @pl.when(jnp.logical_not(worst_t < safe_sum))
                def _():
                    @pl.loop(0, subs)
                    def _(sub):
                        worst_s = jnp.max(sums_ref[step * subs + sub, :, columns(t)])

                        @pl.when(jnp.logical_not(worst_s < safe_sum))
                        def _():
                            redo(t, sub)

    accs = [
        pltpu.ACC(unit)((group_rows, unit_size), jnp.float32) for unit in range(units) for _ in range(groups)
    ]
    pl.run_scoped(main, *accs)

    @pl.when(step == pl.num_programs(0) - 1)
    def _():
        @pl.loop(0, col_blocks)
        def _(t):
            shifts = shift_ref[:, :, columns(t)]
            top = jnp.max(shifts, axis=0)
            scale = jnp.exp(shifts - top[None])
            total = jnp.sum(sums_ref[:, :, columns(t)] * scale, axis=0)
            total = jnp.sum(total, axis=0, keepdims=True)
            out_ref[:, columns(t)] = top + jnp.log(total)


def local_lse(tokens, centroids):
    tok_count, width = tokens.shape
    cent_count = centroids.shape[0]
    block_rows = divisor(cent_count, 4096)
    sub_rows = divisor(block_rows, 1024)
    tok_cols = divisor(tok_count, 512)
    blocks = cent_count // block_rows
    subs = cent_count // sub_rows
    return pl.pallas_call(
        functools.partial(stats_kernel, sub_rows, tok_cols),
        grid=(blocks,),
        in_specs=[
            pl.BlockSpec((tok_count, width), lambda j: (0, 0)),
            pl.BlockSpec((block_rows, width), lambda j: (j, 0)),
        ],
        out_specs=pl.BlockSpec((1, tok_count), lambda j: (0, 0)),
        out_shape=jax.ShapeDtypeStruct((1, tok_count), jnp.float32),
        scratch_shapes=[
            pltpu.VMEM((1, tok_count), jnp.float32),
            pltpu.VMEM((subs, 1, tok_count), jnp.float32),
            pltpu.VMEM((subs, 8, tok_count), jnp.float32),
        ],
        compiler_params=pltpu.CompilerParams(vmem_limit_bytes=vmem_bytes),
        cost_estimate=pl.CostEstimate(
            flops=2 * tok_count * cent_count * width,
            bytes_accessed=(tok_count + cent_count) * width * 2,
            transcendentals=tok_count * cent_count,
        ),
        name="row_stats",
    )(tokens, centroids)


def encoded(x):
    x = x * code_scale
    return (x * jnp.abs(x) * (x * x)).astype(jnp.bfloat16)


def decoded(code):
    code = code.astype(jnp.float32)
    size = lax.rsqrt(lax.rsqrt(jnp.maximum(jnp.abs(code), 1e-37))) * (1.0 / code_scale)
    return jnp.where(code < 0, -size, jnp.where(code > 0, size, 0.0))


def update_kernel(shards, place_ref, *refs):
    tok_refs, lse_refs = refs[:shards], refs[shards : 2 * shards]
    cent_ref, new_ref, mass_ref, toks_ref, lses_ref, sems = refs[2 * shards :]
    rows, width = cent_ref.shape
    shard_rows = tok_refs[0].shape[0]
    groups = rows // group_rows
    pieces = shards * shard_rows // unit_size
    run = divisor(pieces, 4)

    @pl.when(pl.program_id(0) == 0)
    def _():
        copies = []
        for s in range(shards):
            span = pl.ds(s * shard_rows, shard_rows)
            copies.append(pltpu.make_async_copy(tok_refs[s], toks_ref.at[span, :], sems.at[2 * s]))
            copies.append(pltpu.make_async_copy(lse_refs[s], lses_ref.at[:, span], sems.at[2 * s + 1]))
        for copy in copies:
            copy.start()
        for copy in copies:
            copy.wait()

    def rows_of(g):
        return pl.ds(g * group_rows, group_rows)

    def tokens_of(n):
        return toks_ref[pl.ds(pl.multiple_of(n * unit_size, unit_size), unit_size), :]

    def main(*accs):
        logit_accs, sum_accs = accs[:groups], accs[groups:]

        def product(g):
            lhs = widened(cent_ref[rows_of(g), :] * jnp.bfloat16(inverse_temp))
            pltpu.matmul_acc_lhs(logit_accs[g], lhs, 0 if g == 0 else None)

        def load_logit_tokens(n):
            pltpu.matmul_push_rhs(widened(tokens_of(n)), 0, 0, transpose=True)

        def step(n, last):
            toks = tokens_of(n)
            pltpu.matmul_push_rhs(jnp.concatenate([toks, jnp.ones_like(toks)], axis=1), 0, 1)
            if not last:
                load_logit_tokens(n + 1)
            lse = lses_ref[:, pl.ds(pl.multiple_of(n * unit_size, unit_size), unit_size)]
            for g in range(groups):
                logits = pltpu.matmul_pop(logit_accs[g])
                if not last:
                    product(g)
                weights = jnp.exp(logits - lse).astype(jnp.bfloat16)
                pltpu.matmul_acc_lhs(sum_accs[g], weights, 0 if g == 0 else None)

        load_logit_tokens(0)
        for g in range(groups):
            product(g)

        @pl.loop(0, pieces // run - 1)
        def _(n):
            for k in range(run):
                step(n * run + k, False)

        for k in range(run):
            step(pieces - run + k, k == run - 1)

        diagonal = lax.broadcasted_iota(jnp.int32, (128, 128), 0) == lax.broadcasted_iota(
            jnp.int32, (128, 128), 1
        )
        for g in range(groups):
            total = pltpu.matmul_pop(sum_accs[g])
            mass = total[:, width:]
            prior = prior_weight * cent_ref[rows_of(g), :].astype(jnp.float32)
            new_ref[rows_of(g), :] = encoded((total[:, :width] + prior) / (mass + prior_weight))
            mass_ref[g] = jnp.sum(jnp.where(diagonal, mass, 0.0), axis=0, keepdims=True)

    accs = [pltpu.ACC(unit)((group_rows, 2 * width), jnp.float32) for unit in range(2) for _ in range(groups)]
    pl.run_scoped(main, *accs)


def updated_chunk(block, toks, lses, centroids, rows, block_rows):
    shards = len(toks)
    shard_rows, width = toks[0].shape
    all_count = shards * shard_rows
    anywhere = pl.BlockSpec(memory_space=pl.ANY)
    return pl.pallas_call(
        functools.partial(update_kernel, shards),
        grid_spec=pltpu.PrefetchScalarGridSpec(
            num_scalar_prefetch=1,
            grid=(rows // block_rows,),
            in_specs=[anywhere] * (2 * shards)
            + [pl.BlockSpec((block_rows, width), lambda j, place: (place[0] + j, 0))],
            out_specs=[
                pl.BlockSpec((block_rows, width), lambda j, place: (j, 0)),
                pl.BlockSpec((block_rows // 128, 1, 128), lambda j, place: (j, 0, 0)),
            ],
            scratch_shapes=[
                pltpu.VMEM((all_count, width), jnp.bfloat16),
                pltpu.VMEM((1, all_count), jnp.float32),
                pltpu.SemaphoreType.DMA((2 * shards,)),
            ],
        ),
        out_shape=[
            jax.ShapeDtypeStruct((rows, width), jnp.bfloat16),
            jax.ShapeDtypeStruct((rows // 128, 1, 128), jnp.float32),
        ],
        compiler_params=pltpu.CompilerParams(vmem_limit_bytes=vmem_bytes),
        cost_estimate=pl.CostEstimate(
            flops=6 * all_count * rows * width,
            bytes_accessed=(2 * all_count + 4 * rows) * width,
            transcendentals=all_count * rows,
        ),
        name="new_rows",
    )(block, *toks, *lses, centroids)


def place_kernel(place_ref, *refs):
    code_refs, out_ref = refs[:-2], refs[-1]
    for s, code_ref in enumerate(code_refs):

        @pl.when(pl.program_id(0) == s)
        def _():
            out_ref[...] = decoded(code_ref[...])


def placed_rows(base, codes, places, block_rows):
    rows, width = codes[0].shape
    blocks = rows // block_rows

    def spec(s):
        def index(q, j, place):
            return jnp.where(q == s, j, jnp.where(q < s, 0, blocks - 1)), 0

        return pl.BlockSpec((block_rows, width), index)

    return pl.pallas_call(
        place_kernel,
        grid_spec=pltpu.PrefetchScalarGridSpec(
            num_scalar_prefetch=1,
            grid=(len(codes), blocks),
            in_specs=[spec(s) for s in range(len(codes))] + [pl.BlockSpec(memory_space=pl.ANY)],
            out_specs=pl.BlockSpec((block_rows, width), lambda q, j, place: (place[q] + j, 0)),
        ),
        out_shape=jax.ShapeDtypeStruct(base.shape, base.dtype),
        input_output_aliases={1 + len(codes): 0},
        compiler_params=pltpu.CompilerParams(vmem_limit_bytes=vmem_bytes),
        cost_estimate=pl.CostEstimate(
            flops=10 * rows * width, bytes_accessed=6 * rows * width, transcendentals=2 * rows * width
        ),
        name="placed_rows",
    )(places, *codes, base)


def combine_kernel(*refs):
    parts, out_ref = [ref[...] for ref in refs[:-1]], refs[-1]
    top = functools.reduce(jnp.maximum, parts)
    out_ref[...] = top + jnp.log(sum(jnp.exp(part - top) for part in parts))


def combined_lse(parts):
    return pl.pallas_call(
        combine_kernel, out_shape=jax.ShapeDtypeStruct(parts[0].shape, jnp.float32), name="join_stats"
    )(*parts)


def blank(shape):
    return pl.pallas_call(
        lambda out_ref: None,
        out_specs=pl.BlockSpec(memory_space=pl.ANY),
        out_shape=jax.ShapeDtypeStruct(shape, jnp.float32),
        name="blank",
    )()


def from_others(value, axis):
    size = lax.axis_size(axis)
    found = [value]
    for s in range(1, size):
        pairs = [(partner(k, s, size), k) for k in range(size)]
        found.append(lax.ppermute(value, axis, pairs))
    return found


def partner(me, s, size):
    return me ^ s if size & (size - 1) == 0 else (me - s) % size


def chunk_plan(blocks):
    plan = []
    while blocks:
        plan.append(max(1, (3 * blocks + 3) // 8))
        blocks -= plan[-1]
    return plan


def local(tokens, centroids):
    tok_size = lax.axis_size("tok")
    me = lax.axis_index("tok")
    cent_count, width = centroids.shape
    share_rows = cent_count // tok_size

    toks = from_others(tokens, "tok")
    own_lse = combined_lse(from_others(local_lse(tokens, centroids), "cent"))
    lses = from_others(own_lse, "tok")

    block_rows = divisor(share_rows, 1024)
    updated = blank((cent_count, width))
    masses, first = [], 0
    sources = jnp.stack([partner(me, s, tok_size) for s in range(tok_size)]).astype(jnp.int32)
    for blocks in chunk_plan(share_rows // block_rows):
        block = first * tok_size + me * blocks
        rows = blocks * block_rows
        codes, mass = updated_chunk(block.reshape(1), toks, lses, centroids, rows, block_rows)
        starts = first * tok_size + sources * blocks
        updated = placed_rows(updated, from_others(codes, "tok"), starts, block_rows)
        masses.append(mass.reshape(rows // 128, 128))
        first += blocks
    found = from_others(jnp.concatenate(masses), "tok")
    parts, done = [], 0
    for mass in masses:
        count = mass.shape[0]
        index = lax.broadcasted_iota(jnp.int32, (tok_size, 1, 1), 0)
        source = partner(me, index, tok_size)
        part = found[0][None, done : done + count]
        for s in range(1, tok_size):
            part = jnp.where(source == s, found[s][None, done : done + count], part)
        parts.append(part.reshape(tok_size * count, 128))
        done += count
    return updated, jnp.concatenate(parts).reshape(cent_count)


def solution(mesh):
    placed = (P("tok", None), P("cent", None))
    return jax.shard_map(
        local, mesh=mesh, in_specs=placed, out_specs=(P("cent", None), P("cent")), check_vma=False
    )
```

time: 299 us -> 358 us (1.20)
  starting transfers between devices: 13.1 us -> 42.6 us
  Pallas kernels: 191 us -> 206 us
  local copies, waits for them, and re-layouts: 4.82 us -> 18.6 us
  between operations: 14.1 us -> 1.1 us
  waiting for transfers between devices: 74.9 us -> 87.3 us
    ppermute x16 -> x31, waiting for transfers between devices: 23.3 us -> 87.3 us  [from_others(): found.append(lax.ppermute(value, axis, pairs))]
    all_gather x5 -> x0, waiting for transfers between devices: 51.5 us -> none  [local(): codes = lax.all_gather(codes, 'tok', axis=0, tiled=True)]
    ppermute x16 -> x31, starting transfers between devices: 12.8 us -> 42.6 us  [from_others(): found.append(lax.ppermute(value, axis, pairs))]
    pallas_call x1, Pallas kernels: 55.2 us -> 78.4 us  [local_lse(): pl.pallas_call(functools.partial(stats_kernel, sub_rows, tok_cols), grid=...]
    pallas_call x5, Pallas kernels: 115 us -> 96 us  [updated_chunk(): pl.pallas_call(functools.partial(update_kernel, shards), grid_spec=pltpu....]
    pallas_call x5, Pallas kernels: 19.4 us -> 30.1 us  [placed_rows(): pl.pallas_call(place_kernel, grid_spec=pltpu.PrefetchScalarGridSpec(num_s...]
    broadcast_in_dim x12 -> x18, local copies, waits for them, and re-layouts: 0.97 us -> 10.9 us  [local(): part = jnp.where(source == s, found[s][None, done:done + count], part)]
    unnamed x45 -> x80, local copies, waits for them, and re-layouts: 3.08 us -> 6.89 us
  transfers between devices with their start and end apart: 21 -> 31, of which waited for: 13 -> 9; matrix products, arithmetic and copies ran while one was open for 1% -> 4% of each run, Pallas kernels for 54% -> 29%
where the time goes in v3:
time: 358 us; the launch traced here: 359 us
  Pallas kernels  206 us (58%)
  waiting for transfers between devices  87.3 us (24%)
  starting transfers between devices  42.6 us (12%)
  local copies, waits for them, and re-layouts  18.6 us (5%)
    pallas_call x5, Pallas kernels, updated_chunk(): pl.pallas_call(functools.partial(update_kernel, shards), grid_spec=pltpu....  96 us
    ppermute x31, waiting for transfers between devices, from_others(): found.append(lax.ppermute(value, axis, pairs))  87.3 us
    pallas_call x1, Pallas kernels, local_lse(): pl.pallas_call(functools.partial(stats_kernel, sub_rows, tok_cols), grid=...  78.4 us
    ppermute x31, starting transfers between devices, from_others(): found.append(lax.ppermute(value, axis, pairs))  42.6 us
    pallas_call x5, Pallas kernels, placed_rows(): pl.pallas_call(place_kernel, grid_spec=pltpu.PrefetchScalarGridSpec(num_s...  30.1 us
    broadcast_in_dim x18, local copies, waits for them, and re-layouts, local(): part = jnp.where(source == s, found[s][None, done:done + count], part)  10.9 us
  transfers between devices with their start and end apart: 31, of which 9 were waited for; matrix products, arithmetic and copies ran while one was open for 4% of the time, Pallas kernels for 29%

profile of v3, /device:TPU:0, one launch (start us, length us, event | category | flops | bytes accessed | tf_op | source)
XLA Modules:
  0.0 358.6 jit_solution(8580718975840388448)
XLA Ops:
  0.6 3.0 collective-permute-start
  3.6 1.5 collective-permute-start.1
  5.2 78.4 %row_stats.1.refs_0_ = f32[1,2048]{1,0:T(1,128)} custom-call(bf16[2048,128]{1,0:T(8,128)(2,1)} %refs_0_.9, bf16[32768,128]{1,0:T(8,128)(2,1)} %refs_8_.9), custom_call_target="tpu_custom_call" | custom-call | flops 17179869184 | bytes 8912896 | tf_op jit(solution)/shard_map/row_stats/pallas_call | solution.py:166
  85.4 2.0 collective-permute-done.4.refs_2_
  89.0 3.1 collective-permute-done.6.refs_4_
  93.6 4.2 %collective-permute-done.8.refs_6_ = f32[1,2048]{1,0:T(1,128)S(1)} collective-permute-done((f32[1,2048]{1,0:T(1,128)}, f32[1,2048]{1,0:T(1,128)S(1)}, u32[]{:S(2)}, u32[]{:S(2)}) %collective-permute-start.8) | collective-permute-done | bytes 8224 | tf_op jit(solution)/shard_map/ppermute | solution.py:376
  100.5 9.5 %collective-permute-start.11 = (f32[1,2048]{1,0:T(1,128)}, f32[1,2048]{1,0:T(1,128)S(1)}, u32[]{:S(2)}, u32[]{:S(2)}) collective-permute-start(f32[1,2048]{1,0:T(1,128)} %join_stats.1.refs_4_), channel_id=1, source_target_pairs={{16,0},{24,8},{0,16},{8,24},{17,1},{25,9},{1,17},{9,25},{18,2},{26... | collective-permute-start | bytes 24584 | tf_op jit(solution)/shard_map/ppermute | solution.py:376
  110.0 3.3 collective-permute-start.12
  113.3 1.8 collective-permute-done.12.refs_7_
  116.3 33.1 %new_rows.9 = (bf16[3072,128]{1,0:T(8,128)(2,1)}, f32[24,1,128]{2,1,0:T(1,128)}) custom-call(s32[1]{0:T(128)} %bitcast.8.place_ref, bf16[2048,128]{1,0:T(8,128)(2,1)} %refs_0_.9, bf16[2048,128]{1,0:T(8,128)(2,1)} %copy-done.32, bf16[2048,128]{1,0:T(8,128)(2,1)} %copy-done.33, bf16[2048,128]{1,0:T(8,128)(2,1)} %copy-done.34, f32[1,2048]{1,0:T(1,128)} %join_stats.1.refs_4_, ...), custom_call_target="tpu_custom_call" | custom-call | flops 19327352832 | bytes 3670016 | tf_op jit(solution)/shard_map/new_rows/pallas_call | solution.py:282
  150.1 23.2 %new_rows.8 = (bf16[2048,128]{1,0:T(8,128)(2,1)}, f32[16,1,128]{2,1,0:T(1,128)}) custom-call(s32[1]{0:T(128)} %bitcast.7.place_ref, bf16[2048,128]{1,0:T(8,128)(2,1)} %refs_0_.9, bf16[2048,128]{1,0:T(8,128)(2,1)} %copy-done.32, bf16[2048,128]{1,0:T(8,128)(2,1)} %copy-done.33, bf16[2048,128]{1,0:T(8,128)(2,1)} %copy-done.34, f32[1,2048]{1,0:T(1,128)} %join_stats.1.refs_4_, ...), custom_call_target="tpu_custom_call" | custom-call | flops 12884901888 | bytes 3145728 | tf_op jit(solution)/shard_map/new_rows/pallas_call | solution.py:282
  174.0 13.2 %new_rows.7 = (bf16[1024,128]{1,0:T(8,128)(2,1)}, f32[8,1,128]{2,1,0:T(1,128)}) custom-call(s32[1]{0:T(128)} %bitcast.6.place_ref, bf16[2048,128]{1,0:T(8,128)(2,1)} %refs_0_.9, bf16[2048,128]{1,0:T(8,128)(2,1)} %copy-done.32, bf16[2048,128]{1,0:T(8,128)(2,1)} %copy-done.33, bf16[2048,128]{1,0:T(8,128)(2,1)} %copy-done.34, f32[1,2048]{1,0:T(1,128)} %join_stats.1.refs_4_, ...), custom_call_target="tpu_custom_call" | custom-call | flops 6442450944 | bytes 2621440 | tf_op jit(solution)/shard_map/new_rows/pallas_call | solution.py:282
  187.9 13.3 %new_rows.6 = (bf16[1024,128]{1,0:T(8,128)(2,1)}, f32[8,1,128]{2,1,0:T(1,128)}) custom-call(s32[1]{0:T(128)} %bitcast.5.place_ref, bf16[2048,128]{1,0:T(8,128)(2,1)} %refs_0_.9, bf16[2048,128]{1,0:T(8,128)(2,1)} %copy-done.32, bf16[2048,128]{1,0:T(8,128)(2,1)} %copy-done.33, bf16[2048,128]{1,0:T(8,128)(2,1)} %copy-done.34, f32[1,2048]{1,0:T(1,128)} %join_stats.1.refs_4_, ...), custom_call_target="tpu_custom_call" | custom-call | flops 6442450944 | bytes 2621440 | tf_op jit(solution)/shard_map/new_rows/pallas_call | solution.py:282
  202.0 13.3 %new_rows.5 = (bf16[1024,128]{1,0:T(8,128)(2,1)}, f32[8,1,128]{2,1,0:T(1,128)}) custom-call(s32[1]{0:T(128)} %bitcast.4.place_ref, bf16[2048,128]{1,0:T(8,128)(2,1)} %refs_0_.9, bf16[2048,128]{1,0:T(8,128)(2,1)} %copy-done.32, bf16[2048,128]{1,0:T(8,128)(2,1)} %copy-done.33, bf16[2048,128]{1,0:T(8,128)(2,1)} %copy-done.34, f32[1,2048]{1,0:T(1,128)} %join_stats.1.refs_4_, ...), custom_call_target="tpu_custom_call" | custom-call | flops 6442450944 | bytes 2621440 | tf_op jit(solution)/shard_map/new_rows/pallas_call | solution.py:282
  216.1 2.9 collective-permute-start.28
  220.2 1.5 collective-permute-start.19
  221.7 2.0 collective-permute-start.20
  223.7 1.5 collective-permute-start.22
  226.4 17.8 %collective-permute-done.30 = f32[64,128]{1,0:T(8,128)S(1)} collective-permute-done((f32[64,128]{1,0:T(8,128)S(1)}, f32[64,128]{1,0:T(8,128)S(1)}, u32[]{:S(2)}, u32[]{:S(2)}) %collective-permute-start.30) | collective-permute-done | bytes 32800 | tf_op jit(solution)/shard_map/ppermute | solution.py:376
  244.2 1.5 collective-permute-start.16
  257.3 1.5 collective-permute-start.26
  258.8 1.5 collective-permute-start.27
  260.3 1.9 collective-permute-start.23
  264.1 55.8 %collective-permute-done.23.refs_2_ = bf16[2048,128]{1,0:T(8,128)(2,1)S(1)} collective-permute-done((bf16[2048,128]{1,0:T(8,128)(2,1)S(1)}, bf16[2048,128]{1,0:T(8,128)(2,1)S(1)}, u32[]{:S(2)}, u32[]{:S(2)}) %collective-permute-start.23) | collective-permute-done | bytes 524320 | tf_op jit(solution)/shard_map/ppermute | solution.py:376
  319.9 1.5 collective-permute-start.17
  323.5 1.5 collective-permute-start.14
  325.0 1.5 collective-permute-start.15
  326.7 10.2 %placed_rows.5.refs_4_ = f32[32768,128]{1,0:T(8,128)} custom-call(s32[4]{0:T(128)} %get-tuple-element.22.place_ref, bf16[3072,128]{1,0:T(8,128)(2,1)} %get-tuple-element.16.refs_0_, bf16[3072,128]{1,0:T(8,128)(2,1)} %copy-done.1, bf16[3072,128]{1,0:T(8,128)(2,1)} %copy-done.2, bf16[3072,128]{1,0:T(8,128)(2,1)} %copy-done.3, ...), custom_call_target="tpu_custom_call", output_to_operand_aliasing={{}: (5, {})} | custom-call | flops 3932160 | bytes 2359296 | tf_op jit(solution)/shard_map/placed_rows/pallas_call | solution.py:332
  336.9 7.6 %placed_rows.6.refs_4_ = f32[32768,128]{1,0:T(8,128)} custom-call(s32[4]{0:T(128)} %get-tuple-element.33.place_ref, bf16[2048,128]{1,0:T(8,128)(2,1)} %get-tuple-element.15.refs_0_, bf16[2048,128]{1,0:T(8,128)(2,1)} %copy-done.5, bf16[2048,128]{1,0:T(8,128)(2,1)} %copy-done.6, bf16[2048,128]{1,0:T(8,128)(2,1)} %copy-done.7, ...), custom_call_target="tpu_custom_call", output_to_operand_aliasing={{}: (5, {})} | custom-call | flops 2621440 | bytes 1572864 | tf_op jit(solution)/shard_map/placed_rows/pallas_call | solution.py:332
  344.5 4.1 %placed_rows.7.refs_4_ = f32[32768,128]{1,0:T(8,128)} custom-call(s32[4]{0:T(128)} %get-tuple-element.34.place_ref, bf16[1024,128]{1,0:T(8,128)(2,1)} %get-tuple-element.14.refs_0_, bf16[1024,128]{1,0:T(8,128)(2,1)} %copy-done.11, bf16[1024,128]{1,0:T(8,128)(2,1)} %copy-done.12, bf16[1024,128]{1,0:T(8,128)(2,1)} %copy-done.13, ...), custom_call_target="tpu_custom_call", output_to_operand_aliasing={{}: (5, {})} | custom-call | flops 1310720 | bytes 786432 | tf_op jit(solution)/shard_map/placed_rows/pallas_call | solution.py:332
  349.5 4.1 %placed_rows.8.refs_4_ = f32[32768,128]{1,0:T(8,128)} custom-call(s32[4]{0:T(128)} %get-tuple-element.35.place_ref, bf16[1024,128]{1,0:T(8,128)(2,1)} %get-tuple-element.13.refs_0_, bf16[1024,128]{1,0:T(8,128)(2,1)} %collective-permute-done.16.refs_1_, bf16[1024,128]{1,0:T(8,128)(2,1)} %copy-done.15, ...), custom_call_target="tpu_custom_call", output_to_operand_aliasing={{}: (5, {})} | custom-call | flops 1310720 | bytes 786432 | tf_op jit(solution)/shard_map/placed_rows/pallas_call | solution.py:332
  354.5 4.1 %placed_rows.9 = f32[32768,128]{1,0:T(8,128)} custom-call(s32[4]{0:T(128)} %get-tuple-element.36.place_ref, bf16[1024,128]{1,0:T(8,128)(2,1)} %get-tuple-element.12.refs_0_, bf16[1024,128]{1,0:T(8,128)(2,1)} %copy-done.14, bf16[1024,128]{1,0:T(8,128)(2,1)} %copy-done.16, bf16[1024,128]{1,0:T(8,128)(2,1)} %copy-done.18, ...), custom_call_target="tpu_custom_call", output_to_operand_aliasing={{}: (5, {})} | custom-call | flops 1310720 | bytes 786432 | tf_op jit(solution)/shard_map/placed_rows/pallas_call | solution.py:332
  (160 shorter events, 32.0 us)
Async XLA Ops:
  0.6 114.5 %collective-permute-start = (bf16[2048,128]{1,0:T(8,128)(2,1)}, bf16[2048,128]{1,0:T(8,128)(2,1)S(1)}, u32[]{:S(2)}, u32[]{:S(2)}) collective-permute-start(bf16[2048,128]{1,0:T(8,128)(2,1)} %refs_0_.9), channel_id=1, source_target_pairs={{8,0},{0,8},{24,16},{16,24},{9,1},{1,9},{25,17},{17,25},{10,2},{2,... | collective-permute-start | bytes 1572872 | tf_op jit(solution)/shard_map/ppermute | solution.py:376
  3.6 111.5 %collective-permute-start.1 = (bf16[2048,128]{1,0:T(8,128)(2,1)}, bf16[2048,128]{1,0:T(8,128)(2,1)S(1)}, u32[]{:S(2)}, u32[]{:S(2)}) collective-permute-start(bf16[2048,128]{1,0:T(8,128)(2,1)} %refs_0_.9), channel_id=1, source_target_pairs={{16,0},{24,8},{0,16},{8,24},{17,1},{25,9},{1,17},{9,25},{18,2},{26... | collective-permute-start | bytes 1572872 | tf_op jit(solution)/shard_map/ppermute | solution.py:376
  5.2 110.0 %collective-permute-start.2 = (bf16[2048,128]{1,0:T(8,128)(2,1)}, bf16[2048,128]{1,0:T(8,128)(2,1)S(1)}, u32[]{:S(2)}, u32[]{:S(2)}) collective-permute-start(bf16[2048,128]{1,0:T(8,128)(2,1)} %refs_0_.9), channel_id=1, source_target_pairs={{24,0},{16,8},{8,16},{0,24},{25,1},{17,9},{9,17},{1,25},{26,2},{18... | collective-permute-start | bytes 1572872 | tf_op jit(solution)/shard_map/ppermute | solution.py:376
  83.5 1.4 collective-permute-start.3
  83.5 3.9 %collective-permute-start.4 = (f32[1,2048]{1,0:T(1,128)}, f32[1,2048]{1,0:T(1,128)S(1)}, u32[]{:S(2)}, u32[]{:S(2)}) collective-permute-start(f32[1,2048]{1,0:T(1,128)} %row_stats.1.refs_0_), channel_id=1, source_target_pairs={{2,0},{3,1},{0,2},{1,3},{6,4},{7,5},{4,6},{5,7},{10,8},{11,9},{8,1... | collective-permute-start | bytes 24584 | tf_op jit(solution)/shard_map/ppermute | solution.py:376
  84.9 3.3 collective-permute-start.5
  87.4 4.8 %collective-permute-start.6 = (f32[1,2048]{1,0:T(1,128)}, f32[1,2048]{1,0:T(1,128)S(1)}, u32[]{:S(2)}, u32[]{:S(2)}) collective-permute-start(f32[1,2048]{1,0:T(1,128)} %row_stats.1.refs_0_), channel_id=1, source_target_pairs={{4,0},{5,1},{6,2},{7,3},{0,4},{1,5},{2,6},{3,7},{12,8},{13,9},{14,... | collective-permute-start | bytes 24584 | tf_op jit(solution)/shard_map/ppermute | solution.py:376
  88.2 4.2 %collective-permute-start.7 = (f32[1,2048]{1,0:T(1,128)}, f32[1,2048]{1,0:T(1,128)S(1)}, u32[]{:S(2)}, u32[]{:S(2)}) collective-permute-start(f32[1,2048]{1,0:T(1,128)} %row_stats.1.refs_0_), channel_id=1, source_target_pairs={{5,0},{4,1},{7,2},{6,3},{1,4},{0,5},{3,6},{2,7},{13,8},{12,9},{15,... | collective-permute-start | bytes 24584 | tf_op jit(solution)/shard_map/ppermute | solution.py:376
  92.2 5.7 %collective-permute-start.8 = (f32[1,2048]{1,0:T(1,128)}, f32[1,2048]{1,0:T(1,128)S(1)}, u32[]{:S(2)}, u32[]{:S(2)}) collective-permute-start(f32[1,2048]{1,0:T(1,128)} %row_stats.1.refs_0_), channel_id=1, source_target_pairs={{6,0},{7,1},{4,2},{5,3},{2,4},{3,5},{0,6},{1,7},{14,8},{15,9},{12,... | collective-permute-start | bytes 24584 | tf_op jit(solution)/shard_map/ppermute | solution.py:376
  92.4 5.4 %collective-permute-start.9 = (f32[1,2048]{1,0:T(1,128)}, f32[1,2048]{1,0:T(1,128)S(1)}, u32[]{:S(2)}, u32[]{:S(2)}) collective-permute-start(f32[1,2048]{1,0:T(1,128)} %row_stats.1.refs_0_), channel_id=1, source_target_pairs={{7,0},{6,1},{5,2},{4,3},{3,4},{2,5},{1,6},{0,7},{15,8},{14,9},{13,... | collective-permute-start | bytes 24584 | tf_op jit(solution)/shard_map/ppermute | solution.py:376
  100.5 9.6 %collective-permute-start.10 = (f32[1,2048]{1,0:T(1,128)}, f32[1,2048]{1,0:T(1,128)S(1)}, u32[]{:S(2)}, u32[]{:S(2)}) collective-permute-start(f32[1,2048]{1,0:T(1,128)} %join_stats.1.refs_4_), channel_id=1, source_target_pairs={{8,0},{0,8},{24,16},{16,24},{9,1},{1,9},{25,17},{17,25},{10,2},{2,... | collective-permute-start | bytes 24584 | tf_op jit(solution)/shard_map/ppermute | solution.py:376
  100.5 12.8 %collective-permute-start.11 = (f32[1,2048]{1,0:T(1,128)}, f32[1,2048]{1,0:T(1,128)S(1)}, u32[]{:S(2)}, u32[]{:S(2)}) collective-permute-start(f32[1,2048]{1,0:T(1,128)} %join_stats.1.refs_4_), channel_id=1, source_target_pairs={{16,0},{24,8},{0,16},{8,24},{17,1},{25,9},{1,17},{9,25},{18,2},{26... | collective-permute-start | bytes 24584 | tf_op jit(solution)/shard_map/ppermute | solution.py:376
  110.0 5.1 %collective-permute-start.12 = (f32[1,2048]{1,0:T(1,128)}, f32[1,2048]{1,0:T(1,128)S(1)}, u32[]{:S(2)}, u32[]{:S(2)}) collective-permute-start(f32[1,2048]{1,0:T(1,128)} %join_stats.1.refs_4_), channel_id=1, source_target_pairs={{24,0},{16,8},{8,16},{0,24},{25,1},{17,9},{9,17},{1,25},{26,2},{18... | collective-permute-start | bytes 24584 | tf_op jit(solution)/shard_map/ppermute | solution.py:376
  202.0 124.5 %copy-start.23 = (f32[8,1,128]{2,1,0:T(1,128)S(1)}, f32[8,1,128]{2,1,0:T(1,128)}, u32[]{:S(2)}) copy-start(f32[8,1,128]{2,1,0:T(1,128)} %get-tuple-element.20) | copy-start | bytes 12292
  216.1 7.6 %collective-permute-start.28 = (f32[64,128]{1,0:T(8,128)S(1)}, f32[64,128]{1,0:T(8,128)S(1)}, u32[]{:S(2)}, u32[]{:S(2)}) collective-permute-start(f32[64,128]{1,0:T(8,128)S(1)} %constant_dynamic-update-slice_fusion), channel_id=1, source_target_pairs={{24,0},{16,8},{8,16},{0,24},{25,1},{17,9},{9,17},{1,25},{26,2},{18... | collective-permute-start | bytes 98312 | tf_op jit(solution)/shard_map/ppermute | solution.py:376
  219.6 6.1 %collective-permute-start.29 = (f32[64,128]{1,0:T(8,128)S(1)}, f32[64,128]{1,0:T(8,128)S(1)}, u32[]{:S(2)}, u32[]{:S(2)}) collective-permute-start(f32[64,128]{1,0:T(8,128)S(1)} %constant_dynamic-update-slice_fusion), channel_id=1, source_target_pairs={{16,0},{24,8},{0,16},{8,24},{17,1},{25,9},{1,17},{9,25},{18,2},{26... | collective-permute-start | bytes 98312 | tf_op jit(solution)/shard_map/ppermute | solution.py:376
  220.2 36.4 %collective-permute-start.19 = (bf16[1024,128]{1,0:T(8,128)(2,1)S(1)}, bf16[1024,128]{1,0:T(8,128)(2,1)S(1)}, u32[]{:S(2)}, u32[]{:S(2)}) collective-permute-start(bf16[1024,128]{1,0:T(8,128)(2,1)S(1)} %copy-done.10), channel_id=1, source_target_pairs={{8,0},{0,8},{24,16},{16,24},{9,1},{1,9},{25,17},{17,25},{10,2},{2,... | collective-permute-start | bytes 786440 | tf_op jit(solution)/shard_map/ppermute | solution.py:376
  221.7 35.6 %collective-permute-start.20 = (bf16[1024,128]{1,0:T(8,128)(2,1)S(1)}, bf16[1024,128]{1,0:T(8,128)(2,1)S(1)}, u32[]{:S(2)}, u32[]{:S(2)}) collective-permute-start(bf16[1024,128]{1,0:T(8,128)(2,1)S(1)} %copy-done.10), channel_id=1, source_target_pairs={{16,0},{24,8},{0,16},{8,24},{17,1},{25,9},{1,17},{9,25},{18,2},{26... | collective-permute-start | bytes 786440 | tf_op jit(solution)/shard_map/ppermute | solution.py:376
  223.7 35.1 %collective-permute-start.21 = (bf16[1024,128]{1,0:T(8,128)(2,1)S(1)}, bf16[1024,128]{1,0:T(8,128)(2,1)S(1)}, u32[]{:S(2)}, u32[]{:S(2)}) collective-permute-start(bf16[1024,128]{1,0:T(8,128)(2,1)S(1)} %copy-done.10), channel_id=1, source_target_pairs={{24,0},{16,8},{8,16},{0,24},{25,1},{17,9},{9,17},{1,25},{26,2},{18... | collective-permute-start | bytes 786440 | tf_op jit(solution)/shard_map/ppermute | solution.py:376
  223.7 38.5 %collective-permute-start.22 = (bf16[2048,128]{1,0:T(8,128)(2,1)S(1)}, bf16[2048,128]{1,0:T(8,128)(2,1)S(1)}, u32[]{:S(2)}, u32[]{:S(2)}) collective-permute-start(bf16[2048,128]{1,0:T(8,128)(2,1)S(1)} %copy-done.4), channel_id=1, source_target_pairs={{8,0},{0,8},{24,16},{16,24},{9,1},{1,9},{25,17},{17,25},{10,2},{2,... | collective-permute-start | bytes 1572872 | tf_op jit(solution)/shard_map/ppermute | solution.py:376
  225.8 18.5 %collective-permute-start.30 = (f32[64,128]{1,0:T(8,128)S(1)}, f32[64,128]{1,0:T(8,128)S(1)}, u32[]{:S(2)}, u32[]{:S(2)}) collective-permute-start(f32[64,128]{1,0:T(8,128)S(1)} %constant_dynamic-update-slice_fusion), channel_id=1, source_target_pairs={{8,0},{0,8},{24,16},{16,24},{9,1},{1,9},{25,17},{17,25},{10,2},{2,... | collective-permute-start | bytes 98312 | tf_op jit(solution)/shard_map/ppermute | solution.py:376
  244.2 16.0 %collective-permute-start.16 = (bf16[1024,128]{1,0:T(8,128)(2,1)S(1)}, bf16[1024,128]{1,0:T(8,128)(2,1)}, u32[]{:S(2)}, u32[]{:S(2)}) collective-permute-start(bf16[1024,128]{1,0:T(8,128)(2,1)S(1)} %copy-done.9), channel_id=1, source_target_pairs={{8,0},{0,8},{24,16},{16,24},{9,1},{1,9},{25,17},{17,25},{10,2},{2,... | collective-permute-start | bytes 786440 | tf_op jit(solution)/shard_map/ppermute | solution.py:376
  256.6 66.3 %collective-permute-start.25 = (bf16[3072,128]{1,0:T(8,128)(2,1)S(1)}, bf16[3072,128]{1,0:T(8,128)(2,1)S(1)}, u32[]{:S(2)}, u32[]{:S(2)}) collective-permute-start(bf16[3072,128]{1,0:T(8,128)(2,1)S(1)} %copy-done), channel_id=1, source_target_pairs={{8,0},{0,8},{24,16},{16,24},{9,1},{1,9},{25,17},{17,25},{10,2},{2,... | collective-permute-start | bytes 2359304 | tf_op jit(solution)/shard_map/ppermute | solution.py:376
  257.3 66.2 %collective-permute-start.26 = (bf16[3072,128]{1,0:T(8,128)(2,1)S(1)}, bf16[3072,128]{1,0:T(8,128)(2,1)S(1)}, u32[]{:S(2)}, u32[]{:S(2)}) collective-permute-start(bf16[3072,128]{1,0:T(8,128)(2,1)S(1)} %copy-done), channel_id=1, source_target_pairs={{16,0},{24,8},{0,16},{8,24},{17,1},{25,9},{1,17},{9,25},{18,2},{26... | collective-permute-start | bytes 2359304 | tf_op jit(solution)/shard_map/ppermute | solution.py:376
  258.8 66.2 %collective-permute-start.27 = (bf16[3072,128]{1,0:T(8,128)(2,1)S(1)}, bf16[3072,128]{1,0:T(8,128)(2,1)S(1)}, u32[]{:S(2)}, u32[]{:S(2)}) collective-permute-start(bf16[3072,128]{1,0:T(8,128)(2,1)S(1)} %copy-done), channel_id=1, source_target_pairs={{24,0},{16,8},{8,16},{0,24},{25,1},{17,9},{9,17},{1,25},{26,2},{18... | collective-permute-start | bytes 2359304 | tf_op jit(solution)/shard_map/ppermute | solution.py:376
  260.3 59.6 %collective-permute-start.23 = (bf16[2048,128]{1,0:T(8,128)(2,1)S(1)}, bf16[2048,128]{1,0:T(8,128)(2,1)S(1)}, u32[]{:S(2)}, u32[]{:S(2)}) collective-permute-start(bf16[2048,128]{1,0:T(8,128)(2,1)S(1)} %copy-done.4), channel_id=1, source_target_pairs={{16,0},{24,8},{0,16},{8,24},{17,1},{25,9},{1,17},{9,25},{18,2},{26... | collective-permute-start | bytes 1572872 | tf_op jit(solution)/shard_map/ppermute | solution.py:376
  262.2 59.2 %collective-permute-start.24 = (bf16[2048,128]{1,0:T(8,128)(2,1)S(1)}, bf16[2048,128]{1,0:T(8,128)(2,1)S(1)}, u32[]{:S(2)}, u32[]{:S(2)}) collective-permute-start(bf16[2048,128]{1,0:T(8,128)(2,1)S(1)} %copy-done.4), channel_id=1, source_target_pairs={{24,0},{16,8},{8,16},{0,24},{25,1},{17,9},{9,17},{1,25},{26,2},{18... | collective-permute-start | bytes 1572872 | tf_op jit(solution)/shard_map/ppermute | solution.py:376
  319.9 28.7 %collective-permute-start.17 = (bf16[1024,128]{1,0:T(8,128)(2,1)S(1)}, bf16[1024,128]{1,0:T(8,128)(2,1)S(1)}, u32[]{:S(2)}, u32[]{:S(2)}) collective-permute-start(bf16[1024,128]{1,0:T(8,128)(2,1)S(1)} %copy-done.9), channel_id=1, source_target_pairs={{16,0},{24,8},{0,16},{8,24},{17,1},{25,9},{1,17},{9,25},{18,2},{26... | collective-permute-start | bytes 786440 | tf_op jit(solution)/shard_map/ppermute | solution.py:376
  321.5 27.2 %collective-permute-start.18 = (bf16[1024,128]{1,0:T(8,128)(2,1)S(1)}, bf16[1024,128]{1,0:T(8,128)(2,1)S(1)}, u32[]{:S(2)}, u32[]{:S(2)}) collective-permute-start(bf16[1024,128]{1,0:T(8,128)(2,1)S(1)} %copy-done.9), channel_id=1, source_target_pairs={{24,0},{16,8},{8,16},{0,24},{25,1},{17,9},{9,17},{1,25},{26,2},{18... | collective-permute-start | bytes 786440 | tf_op jit(solution)/shard_map/ppermute | solution.py:376
  322.9 30.6 %collective-permute-start.13 = (bf16[1024,128]{1,0:T(8,128)(2,1)S(1)}, bf16[1024,128]{1,0:T(8,128)(2,1)S(1)}, u32[]{:S(2)}, u32[]{:S(2)}) collective-permute-start(bf16[1024,128]{1,0:T(8,128)(2,1)S(1)} %copy-done.8), channel_id=1, source_target_pairs={{8,0},{0,8},{24,16},{16,24},{9,1},{1,9},{25,17},{17,25},{10,2},{2,... | collective-permute-start | bytes 786440 | tf_op jit(solution)/shard_map/ppermute | solution.py:376
  323.5 30.1 %collective-permute-start.14 = (bf16[1024,128]{1,0:T(8,128)(2,1)S(1)}, bf16[1024,128]{1,0:T(8,128)(2,1)S(1)}, u32[]{:S(2)}, u32[]{:S(2)}) collective-permute-start(bf16[1024,128]{1,0:T(8,128)(2,1)S(1)} %copy-done.8), channel_id=1, source_target_pairs={{16,0},{24,8},{0,16},{8,24},{17,1},{25,9},{1,17},{9,25},{18,2},{26... | collective-permute-start | bytes 786440 | tf_op jit(solution)/shard_map/ppermute | solution.py:376
  325.0 28.6 %collective-permute-start.15 = (bf16[1024,128]{1,0:T(8,128)(2,1)S(1)}, bf16[1024,128]{1,0:T(8,128)(2,1)S(1)}, u32[]{:S(2)}, u32[]{:S(2)}) collective-permute-start(bf16[1024,128]{1,0:T(8,128)(2,1)S(1)} %copy-done.8), channel_id=1, source_target_pairs={{24,0},{16,8},{8,16},{0,24},{25,1},{17,9},{9,17},{1,25},{26,2},{18... | collective-permute-start | bytes 786440 | tf_op jit(solution)/shard_map/ppermute | solution.py:376
  (37 other events, 980.6 us)

commit v4 on v1

v4 whole, which is shorter than its diff:
```python
import functools

import jax
import jax.numpy as jnp
from jax import lax
from jax.experimental import pallas as pl
from jax.experimental.pallas import tpu as pltpu
from jax.sharding import PartitionSpec as P

inverse_temp = 2.0
prior_weight = 0.05
safe_sum = 1e30
code_scale = 2.0**24
slice_rows = 64
vmem_bytes = 56 * 1024 * 1024


def divisor(count, most):
    size = min(count, most)
    while count % size:
        size //= 2
    return size


def dot_nt(a, b):
    return lax.dot_general(a, b, (((1,), (1,)), ((), ())), preferred_element_type=jnp.float32)


def fold_rows(x, combine):
    parts = [x[k * 8 : (k + 1) * 8, :] for k in range(x.shape[0] // 8)]
    while len(parts) > 1:
        half = len(parts) // 2
        parts = [combine(parts[2 * k], parts[2 * k + 1]) for k in range(half)] + parts[2 * half :]
    return parts[0]


def stats_kernel(sub_rows, tok_cols, tok_ref, cent_ref, out_ref, flip_ref, base_ref, shift_ref, sums_ref):
    step = pl.program_id(0)
    tok_count = tok_ref.shape[0]
    tile = divisor(sub_rows, 1024)
    subs = cent_ref.shape[0] // sub_rows
    col_blocks = tok_count // tok_cols

    def columns(t):
        return pl.ds(pl.multiple_of(t * tok_cols, tok_cols), tok_cols)

    def dot(a, b):
        return jnp.dot(a, b, preferred_element_type=jnp.float32)

    @pl.when(step == 0)
    def _():
        @pl.loop(0, col_blocks)
        def _(t):
            flipped = (tok_ref[columns(t), :] * jnp.bfloat16(inverse_temp)).T
            flip_ref[:, columns(t)] = flipped
            logits = dot(cent_ref[0:128, :], flipped)
            top = jnp.max(fold_rows(logits, jnp.maximum), axis=0, keepdims=True)
            base_ref[:, columns(t)] = top

    @pl.loop(0, col_blocks)
    def _(t):
        rhs = flip_ref[:, columns(t)]
        shift = base_ref[:, columns(t)]
        for sub in range(subs):
            total = jnp.zeros((8, tok_cols), jnp.float32)
            for k in range(sub_rows // tile):
                logits = dot(cent_ref[pl.ds(sub * sub_rows + k * tile, tile), :], rhs)
                for first in range(0, tile, slice_rows):
                    scaled = jnp.exp(logits[first : first + slice_rows] - shift)
                    total = total + fold_rows(scaled, jnp.add)
            sums_ref[step * subs + sub, :, columns(t)] = total
            shift_ref[step * subs + sub, :, columns(t)] = shift

    worst = jnp.max(sums_ref[pl.ds(step * subs, subs), :, :])

    @pl.when(jnp.logical_not(worst < safe_sum))
    def _():
        @pl.loop(0, col_blocks)
        def _(t):
            worst_t = jnp.max(sums_ref[pl.ds(step * subs, subs), :, columns(t)])

            @pl.when(jnp.logical_not(worst_t < safe_sum))
            def _():
                @pl.loop(0, subs)
                def _(sub):
                    worst_s = jnp.max(sums_ref[step * subs + sub, :, columns(t)])

                    @pl.when(jnp.logical_not(worst_s < safe_sum))
                    def _():
                        rhs = flip_ref[:, columns(t)]
                        lowest = base_ref[:, columns(t)]

                        def logits_of(k):
                            first = pl.multiple_of(sub * sub_rows + k * tile, tile)
                            return dot(cent_ref[pl.ds(first, tile), :], rhs)

                        def raise_top(k, top):
                            return jnp.maximum(top, fold_rows(logits_of(k), jnp.maximum))

                        top = lax.fori_loop(
                            0, sub_rows // tile, raise_top, jnp.broadcast_to(lowest, (8, tok_cols))
                        )
                        top = jnp.max(top, axis=0, keepdims=True)

                        def add_up(k, total):
                            return total + fold_rows(jnp.exp(logits_of(k) - top), jnp.add)

                        total = lax.fori_loop(
                            0, sub_rows // tile, add_up, jnp.zeros((8, tok_cols), jnp.float32)
                        )
                        sums_ref[step * subs + sub, :, columns(t)] = total
                        shift_ref[step * subs + sub, :, columns(t)] = top

    @pl.when(step == pl.num_programs(0) - 1)
    def _():
        @pl.loop(0, col_blocks)
        def _(t):
            shifts = shift_ref[:, :, columns(t)]
            top = jnp.max(shifts, axis=0)
            scale = jnp.exp(shifts - top[None])
            total = jnp.sum(sums_ref[:, :, columns(t)] * scale, axis=0)
            total = jnp.sum(total, axis=0, keepdims=True)
            out_ref[:, columns(t)] = top + jnp.log(total)


def local_lse(tokens, centroids):
    tok_count, width = tokens.shape
    cent_count = centroids.shape[0]
    block_rows = divisor(cent_count, 4096)
    sub_rows = divisor(block_rows, 1024)
    tok_cols = divisor(tok_count, 512)
    blocks = cent_count // block_rows
    subs = cent_count // sub_rows
    return pl.pallas_call(
        functools.partial(stats_kernel, sub_rows, tok_cols),
        grid=(blocks,),
        in_specs=[
            pl.BlockSpec((tok_count, width), lambda j: (0, 0)),
            pl.BlockSpec((block_rows, width), lambda j: (j, 0)),
        ],
        out_specs=pl.BlockSpec((1, tok_count), lambda j: (0, 0)),
        out_shape=jax.ShapeDtypeStruct((1, tok_count), jnp.float32),
        scratch_shapes=[
            pltpu.VMEM((width, tok_count), jnp.bfloat16),
            pltpu.VMEM((1, tok_count), jnp.float32),
            pltpu.VMEM((subs, 1, tok_count), jnp.float32),
            pltpu.VMEM((subs, 8, tok_count), jnp.float32),
        ],
        compiler_params=pltpu.CompilerParams(vmem_limit_bytes=vmem_bytes),
        cost_estimate=pl.CostEstimate(
            flops=2 * tok_count * cent_count * width,
            bytes_accessed=(tok_count + cent_count) * width * 2,
            transcendentals=tok_count * cent_count,
        ),
        name="row_stats",
    )(tokens, centroids)


def encoded(x):
    x = x * code_scale
    return (x * jnp.abs(x) * (x * x)).astype(jnp.bfloat16)


def decoded(code):
    code = code.astype(jnp.float32)
    size = lax.rsqrt(lax.rsqrt(jnp.maximum(jnp.abs(code), 1e-37))) * (1.0 / code_scale)
    return jnp.where(code < 0, -size, jnp.where(code > 0, size, 0.0))


def split_exactly(x):
    high = x.astype(jnp.bfloat16).astype(jnp.float32)
    middle = (x - high).astype(jnp.bfloat16).astype(jnp.float32)
    return high, middle, x - high - middle


class Placing:
    def __init__(self, block_rows, starts_ref, code_refs, outs, scratch):
        self.block_rows, self.starts_ref, self.code_refs = block_rows, starts_ref, code_refs
        self.updated_ref, self.masses_ref = outs
        self.codes, self.values, self.masses, self.sems = scratch

    @staticmethod
    def scratch(sources, blocks, block_rows, width):
        return [
            pltpu.VMEM((sources, blocks * coded_rows(block_rows), width), jnp.bfloat16),
            pltpu.VMEM((sources, blocks * block_rows, width), jnp.float32),
            pltpu.VMEM((sources, blocks * block_rows // 128, 128), jnp.float32),
            pltpu.SemaphoreType.DMA((3, sources)),
        ]

    def copies_in(self):
        return [
            pltpu.make_async_copy(ref, self.codes.at[s], self.sems.at[0, s])
            for s, ref in enumerate(self.code_refs)
        ]

    def copies_out(self):
        found = []
        for s in range(len(self.code_refs)):
            rows, mass_rows = self.values.shape[1], self.masses.shape[1]
            start = self.starts_ref[s]
            span = pl.ds(pl.multiple_of(start * self.block_rows, self.block_rows), rows)
            found.append(
                pltpu.make_async_copy(self.values.at[s], self.updated_ref.at[span, :], self.sems.at[1, s])
            )
            per_block = self.block_rows // 128
            span = pl.ds(pl.multiple_of(start * per_block, per_block), mass_rows)
            found.append(
                pltpu.make_async_copy(self.masses.at[s], self.masses_ref.at[span, :], self.sems.at[2, s])
            )
        return found

    def fetch(self):
        for copy in self.copies_in():
            copy.start()

    def place(self):
        block_rows, per_block = self.block_rows, self.block_rows // 128
        full = coded_rows(block_rows)
        tile = divisor(block_rows, 256)
        for copy in self.copies_in():
            copy.wait()

        @pl.loop(0, len(self.code_refs))
        def _(s):
            for b in range(self.values.shape[1] // block_rows):

                @pl.loop(0, block_rows // tile)
                def _(k):
                    source = pl.ds(pl.multiple_of(b * full + k * tile, 16), tile)
                    target = pl.ds(pl.multiple_of(b * block_rows + k * tile, tile), tile)
                    self.values[s, target, :] = decoded(self.codes[s, source, :])

                terms = self.codes[s, b * full + block_rows : (b + 1) * full, :].astype(jnp.float32)
                mass = terms[:per_block] + terms[per_block : 2 * per_block]
                mass = mass + terms[2 * per_block : 3 * per_block]
                self.masses[s, b * per_block : (b + 1) * per_block, :] = mass

        for copy in self.copies_out():
            copy.start()

    def finish(self):
        for copy in self.copies_out():
            copy.wait()


def coded_rows(block_rows):
    return block_rows + block_rows // 32


def update_kernel(sources, block_rows, *refs):
    place_ref, tok_ref, lse_ref, cent_ref = refs[:4]
    code_refs, refs = refs[4 : 4 + sources], refs[4 + sources :]
    if sources:
        code_ref, updated_ref, masses_ref = refs[2:5]
        scratch = refs[5:]
        placing = Placing(block_rows, place_ref.at[pl.ds(1, sources)], code_refs, (updated_ref, masses_ref), scratch[3:])
    else:
        code_ref, scratch, placing = refs[0], refs[1:], None
    weights_ref, total_ref, mass_ref = scratch[:3]
    step, steps = pl.program_id(0), pl.num_programs(0)
    width = tok_ref.shape[1]
    _, tile, depth = weights_ref.shape
    piece = divisor(depth, 512)
    stages = tok_ref.shape[0] // depth
    tiles = block_rows // tile

    if placing:
        pl.when(step == 0)(placing.fetch)

    def weigh(first, stage):
        cents = cent_ref[pl.ds(first, tile), :] * jnp.bfloat16(inverse_temp)
        for k in range(depth // piece):
            span = pl.ds(stage * depth + k * piece, piece)
            logits = dot_nt(cents, tok_ref[span, :])
            lse = lse_ref[:, span]
            for r in range(0, tile, slice_rows):
                weights = jnp.exp(logits[r : r + slice_rows] - lse).astype(jnp.bfloat16)
                weights_ref[stage % 2, r : r + slice_rows, pl.ds(k * piece, piece)] = weights

    def gather_up(stage):
        toks = tok_ref[pl.ds(stage * depth, depth), :]
        rhs = jnp.concatenate([toks, jnp.ones_like(toks)], axis=1)
        part = jnp.dot(weights_ref[stage % 2], rhs, preferred_element_type=jnp.float32)
        if stage == 0:
            total_ref[...] = part
        else:
            total_ref[...] += part

    diagonal = lax.broadcasted_iota(jnp.int32, (128, 128), 0) == lax.broadcasted_iota(
        jnp.int32, (128, 128), 1
    )

    def run(r):
        first = pl.multiple_of(r * tile, tile)
        weigh(first, 0)
        for stage in range(1, stages):
            weigh(first, stage)
            gather_up(stage - 1)
        gather_up(stages - 1)
        mass = total_ref[:, width : 2 * width]
        prior = prior_weight * cent_ref[pl.ds(first, tile), :].astype(jnp.float32)
        new = (total_ref[:, 0:width] + prior) / (mass + prior_weight)
        code_ref[pl.ds(first, tile), :] = encoded(new)
        for k in range(tile // 128):
            square = jnp.where(diagonal, mass[k * 128 : (k + 1) * 128, :], 0.0)
            mass_ref[pl.ds(r * (tile // 128) + k, 1), :] = jnp.sum(square, axis=0, keepdims=True)

    pl.loop(0, tiles // 2)(run)
    if placing:
        pl.when(step == 0)(placing.place)
    pl.loop(tiles // 2, tiles)(run)

    terms = split_exactly(mass_ref[...])
    terms = jnp.concatenate([*terms, jnp.zeros_like(terms[0])], axis=0)
    code_ref[block_rows : block_rows + terms.shape[0], :] = terms.astype(jnp.bfloat16)
    if placing:
        pl.when(step == steps - 1)(placing.finish)


def updated_chunk(block, every_tok, lse, centroids, blocks, block_rows, received=None):
    all_count, width = every_tok.shape
    depth = divisor(all_count, 2048)
    tile = divisor(block_rows, 512)
    rows = blocks * block_rows
    full = coded_rows(block_rows)
    anywhere = pl.BlockSpec(memory_space=pl.ANY)
    whole = lambda j, place: (0, 0)
    place, operands = block.reshape(1), [every_tok, lse, centroids]
    in_specs = [
        pl.BlockSpec((all_count, width), whole),
        pl.BlockSpec((1, all_count), whole),
        pl.BlockSpec((block_rows, width), lambda j, place: (place[0] + j, 0)),
    ]
    out_specs = [pl.BlockSpec((full, width), lambda j, place: (j, 0))]
    out_shape = [jax.ShapeDtypeStruct((blocks * full, width), jnp.bfloat16)]
    scratch_shapes = [
        pltpu.VMEM((2, tile, depth), jnp.bfloat16),
        pltpu.VMEM((tile, 2 * width), jnp.float32),
        pltpu.VMEM((block_rows // 128, 128), jnp.float32),
    ]
    aliases, sources = {}, 0
    if received:
        codes, starts, outs = received
        sources = len(codes)
        place = jnp.concatenate([place, starts])
        operands += [*codes, *outs]
        in_specs += [anywhere] * (sources + 2)
        out_specs += [anywhere] * 2
        out_shape += [jax.ShapeDtypeStruct(out.shape, out.dtype) for out in outs]
        aliases = {4 + sources: 1, 5 + sources: 2}
        scratch_shapes += Placing.scratch(sources, codes[0].shape[0] // full, block_rows, width)
    return pl.pallas_call(
        functools.partial(update_kernel, sources, block_rows),
        grid_spec=pltpu.PrefetchScalarGridSpec(
            num_scalar_prefetch=1,
            grid=(blocks,),
            in_specs=in_specs,
            out_specs=out_specs,
            scratch_shapes=scratch_shapes,
        ),
        out_shape=out_shape,
        input_output_aliases=aliases,
        compiler_params=pltpu.CompilerParams(vmem_limit_bytes=vmem_bytes),
        cost_estimate=pl.CostEstimate(
            flops=6 * all_count * rows * width,
            bytes_accessed=(2 * all_count + 4 * rows) * width,
            transcendentals=all_count * rows,
        ),
        name="new_rows",
    )(place.astype(jnp.int32), *operands)


def place_kernel(sources, block_rows, starts_ref, *refs):
    code_refs, outs, scratch = refs[:sources], refs[sources + 2 : sources + 4], refs[sources + 4 :]
    placing = Placing(block_rows, starts_ref, code_refs, outs, scratch)
    placing.fetch()
    placing.place()
    placing.finish()


def placed(received, block_rows):
    codes, starts, outs = received
    sources, width = len(codes), codes[0].shape[1]
    anywhere = pl.BlockSpec(memory_space=pl.ANY)
    return pl.pallas_call(
        functools.partial(place_kernel, sources, block_rows),
        grid_spec=pltpu.PrefetchScalarGridSpec(
            num_scalar_prefetch=1,
            grid=(1,),
            in_specs=[anywhere] * (sources + 2),
            out_specs=[anywhere] * 2,
            scratch_shapes=Placing.scratch(
                sources, codes[0].shape[0] // coded_rows(block_rows), block_rows, width
            ),
        ),
        out_shape=[jax.ShapeDtypeStruct(out.shape, out.dtype) for out in outs],
        input_output_aliases={1 + sources: 0, 2 + sources: 1},
        compiler_params=pltpu.CompilerParams(vmem_limit_bytes=vmem_bytes),
        name="placed_rows",
    )(starts.astype(jnp.int32), *codes, *outs)


def combine_kernel(groups, parts_ref, out_ref):
    per_group = parts_ref.shape[0] // groups
    count = parts_ref.shape[2]
    for t in range(groups):
        parts = [parts_ref[t * per_group + k] for k in range(per_group)]
        top = functools.reduce(jnp.maximum, parts)
        total = functools.reduce(jnp.add, [jnp.exp(part - top) for part in parts])
        out_ref[:, t * count : (t + 1) * count] = top + jnp.log(total)


def combined_lse(parts, groups):
    return pl.pallas_call(
        functools.partial(combine_kernel, groups),
        out_shape=jax.ShapeDtypeStruct((1, groups * parts.shape[2]), jnp.float32),
        name="join_stats",
    )(parts)


def blank(shape):
    return pl.pallas_call(
        lambda out_ref: None,
        out_specs=pl.BlockSpec(memory_space=pl.ANY),
        out_shape=jax.ShapeDtypeStruct(shape, jnp.float32),
        name="blank",
    )()


def from_others(value, axis):
    size = lax.axis_size(axis)
    found = [value]
    for s in range(1, size):
        pairs = [(partner(k, s, size), k) for k in range(size)]
        found.append(lax.ppermute(value, axis, pairs))
    return found


def partner(me, s, size):
    return me ^ s if size & (size - 1) == 0 else (me - s) % size


def chunk_plan(blocks):
    plan = []
    while blocks:
        plan.append(max(1, (3 * blocks + 4) // 8))
        blocks -= plan[-1]
    return plan


def local(tokens, centroids):
    tok_size, cent_size = lax.axis_size("tok"), lax.axis_size("cent")
    me = lax.axis_index("tok")
    cent_count, width = centroids.shape
    share_rows = cent_count // tok_size

    every_tok = lax.all_gather(tokens, "tok", axis=0, tiled=True)
    own_lse = local_lse(tokens, centroids)
    copies = jnp.broadcast_to(own_lse[None], (tok_size * cent_size, *own_lse.shape))
    parts = lax.all_to_all(copies, ("tok", "cent"), 0, 0, tiled=True)
    lse = combined_lse(parts, tok_size)

    block_rows = divisor(share_rows, 1024)
    sources = jnp.stack([partner(me, s, tok_size) for s in range(tok_size)])
    outs = blank((cent_count, width)), blank((cent_count // 128, 128))
    waiting, first = [], 0
    for blocks in chunk_plan(share_rows // block_rows):
        block = first * tok_size + me * blocks
        if len(waiting) == 2:
            codes, *outs = updated_chunk(
                block, every_tok, lse, centroids, blocks, block_rows, (*waiting.pop(0), outs)
            )
        else:
            (codes,) = updated_chunk(block, every_tok, lse, centroids, blocks, block_rows)
        waiting.append((from_others(codes, "tok"), first * tok_size + sources * blocks))
        first += blocks
    for received in waiting:
        outs = placed((*received, outs), block_rows)
    return outs[0], outs[1].reshape(cent_count)


def solution(mesh):
    placed_as = (P("tok", None), P("cent", None))
    return jax.shard_map(
        local, mesh=mesh, in_specs=placed_as, out_specs=(P("cent", None), P("cent")), check_vma=False
    )
```

time: 266 us -> 237 us (0.89)
  other arithmetic: 30.6 us -> 3.01 us
  between operations: 0.98 us -> 14.4 us
  starting transfers between devices: 36.4 us -> 23 us
  waiting for transfers between devices: 37.9 us -> 26.8 us
  local copies, waits for them, and re-layouts: 2.7 us -> 7.35 us
  Pallas kernels: 155 us -> 159 us
    dynamic_update_slice x28 -> x0, other arithmetic: 29.1 us -> none  [local(): lax.dynamic_update_slice(updated, part.astype(jnp.float32), (start, 0))]
    ppermute x40 -> x15, waiting for transfers between devices: 37.9 us -> 18.8 us  [from_others(): found.append(lax.ppermute(value, axis, pairs))]
    ppermute x40 -> x15, starting transfers between devices: 36.4 us -> 17.7 us  [from_others(): found.append(lax.ppermute(value, axis, pairs))]
    pallas_call x5 -> x8, Pallas kernels: 90.5 us -> 105 us  [the longest x5 94.6 us: updated_chunk(): pl.pallas_call(functools.partial(update_kernel, sources, block_rows), gri...]
    pallas_call x1, Pallas kernels: 64 us -> 54.6 us  [local_lse(): pl.pallas_call(functools.partial(stats_kernel, sub_rows, tok_cols), grid=...]
    all_to_all x0 -> x1, waiting for transfers between devices: none -> 7.32 us  [local(): parts = lax.all_to_all(copies, ('tok', 'cent'), 0, 0, tiled=True)]
    all_to_all x0 -> x1, starting transfers between devices: none -> 5.28 us  [local(): parts = lax.all_to_all(copies, ('tok', 'cent'), 0, 0, tiled=True)]
    unnamed x32, local copies, waits for them, and re-layouts: 2.28 us -> 5.82 us
  transfers between devices with their start and end apart: 40 -> 17, of which waited for: 19 -> 5; matrix products, arithmetic and copies ran while one was open for 8% -> 2% of each run, Pallas kernels for 50% -> 54%
where the time goes in v4:
time: 237 us; the launch traced here: 234 us
  Pallas kernels  159 us (67%)
  waiting for transfers between devices  26.8 us (11%)
  starting transfers between devices  23 us (10%)
  between operations  14.4 us (6%)
  local copies, waits for them, and re-layouts  7.35 us (3%)
  other arithmetic  3.01 us (1%)
    pallas_call x5, Pallas kernels, updated_chunk(): pl.pallas_call(functools.partial(update_kernel, sources, block_rows), gri...  94.6 us
    pallas_call x1, Pallas kernels, local_lse(): pl.pallas_call(functools.partial(stats_kernel, sub_rows, tok_cols), grid=...  54.6 us
    ppermute x15, waiting for transfers between devices, from_others(): found.append(lax.ppermute(value, axis, pairs))  18.8 us
    ppermute x15, starting transfers between devices, from_others(): found.append(lax.ppermute(value, axis, pairs))  17.7 us
    pallas_call x2, Pallas kernels, placed(): pl.pallas_call(functools.partial(place_kernel, sources, block_rows), grid...  8.52 us
    all_to_all x1, waiting for transfers between devices, local(): parts = lax.all_to_all(copies, ('tok', 'cent'), 0, 0, tiled=True)  7.32 us
    unnamed x32, local copies, waits for them, and re-layouts  5.82 us
    all_to_all x1, starting transfers between devices, local(): parts = lax.all_to_all(copies, ('tok', 'cent'), 0, 0, tiled=True)  5.28 us
  transfers between devices with their start and end apart: 17, of which 5 were waited for; matrix products, arithmetic and copies ran while one was open for 2% of the time, Pallas kernels for 54%

profile of v4, /device:TPU:0, one launch (start us, length us, event | category | flops | bytes accessed | tf_op | source)
XLA Modules:
  0.0 233.8 jit_solution(2267853812192597523)
XLA Ops:
  7.9 54.6 %row_stats.1 = f32[1,2048]{1,0:T(1,128)} custom-call(bf16[2048,128]{1,0:T(8,128)(2,1)} %tok_ref.1, bf16[32768,128]{1,0:T(8,128)(2,1)} %refs_3_.9), custom_call_target="tpu_custom_call" | custom-call | flops 17179869184 | bytes 8912896 | tf_op jit(solution)/shard_map/row_stats/pallas_call | solution.py:134
  62.5 1.5 broadcast_in_dim.9
  64.0 5.3 %all-to-all-start = ((f32[32,1,2048]{2,1,0:T(1,128)}), f32[32,1,2048]{2,1,0:T(1,128)S(1)}, u32[]{:S(2)}, u32[]{:S(2)}) async-start(f32[32,1,2048]{2,1,0:T(1,128)} %broadcast_in_dim.9), calls=%async_computation | async-start | bytes 524288 | tf_op jit(solution)/shard_map/all_to_all | solution.py:461
  72.3 7.3 %all-to-all-done.parts_ref = f32[32,1,2048]{2,1,0:T(1,128)S(1)} async-done(((f32[32,1,2048]{2,1,0:T(1,128)}), f32[32,1,2048]{2,1,0:T(1,128)S(1)}, u32[]{:S(2)}, u32[]{:S(2)}) %all-to-all-start) | async-done | bytes 262176 | tf_op jit(solution)/shard_map/all_to_all | solution.py:461
  79.7 0.7 copy-done
  80.3 1.6 join_stats.1.refs_2_
  82.0 29.7 %new_rows.5.refs_4_ = bf16[3168,128]{1,0:T(8,128)(2,1)} custom-call(s32[1]{0:T(128)} %bitcast.7.refs_0_, bf16[8192,128]{1,0:T(8,128)(2,1)} %all-gather.2.cloned.1.call-done.refs_1_, f32[1,8192]{1,0:T(1,128)} %join_stats.1.refs_2_, bf16[32768,128]{1,0:T(8,128)(2,1)} %refs_3_.9), custom_call_target="tpu_custom_call" | custom-call | flops 19327352832 | bytes 3670016 | tf_op jit(solution)/shard_map/new_rows/pallas_call | solution.py:353
  112.2 0.8 collective-permute-start.1
  113.0 2.2 collective-permute-start.2
  115.2 20.7 %new_rows.7.refs_4_ = bf16[2112,128]{1,0:T(8,128)(2,1)} custom-call(s32[1]{0:T(128)} %bitcast.9.refs_0_, bf16[8192,128]{1,0:T(8,128)(2,1)} %all-gather.2.cloned.1.call-done.refs_1_, f32[1,8192]{1,0:T(1,128)} %join_stats.1.refs_2_, bf16[32768,128]{1,0:T(8,128)(2,1)} %refs_3_.9), custom_call_target="tpu_custom_call" | custom-call | flops 12884901888 | bytes 3145728 | tf_op jit(solution)/shard_map/new_rows/pallas_call | solution.py:353
  136.4 0.8 collective-permute-start.7
  137.2 2.2 collective-permute-start.8
  139.4 10.9 %collective-permute-done.1.refs_6_ = bf16[3168,128]{1,0:T(8,128)(2,1)S(1)} collective-permute-done((bf16[3168,128]{1,0:T(8,128)(2,1)}, bf16[3168,128]{1,0:T(8,128)(2,1)S(1)}, u32[]{:S(2)}, u32[]{:S(2)}) %collective-permute-start.1) | collective-permute-done | bytes 811040 | tf_op jit(solution)/shard_map/ppermute | solution.py:436
  150.3 0.9 copy-done.2
  151.2 0.9 copy-done.3
  152.1 15.7 %new_rows.6 = (bf16[1056,128]{1,0:T(8,128)(2,1)}, f32[32768,128]{1,0:T(8,128)}, f32[256,128]{1,0:T(8,128)}) custom-call(s32[5]{0:T(128)} %pad_add_fusion.2.refs_0_, bf16[8192,128]{1,0:T(8,128)(2,1)} %all-gather.2.cloned.1.call-done.refs_1_, f32[1,8192]{1,0:T(1,128)} %join_stats.1.refs_2_, ...), custom_call_target="tpu_custom_call", output_to_operand_aliasing={{1}: (8, {}), {2}: (9, {})} | custom-call | flops 6442450944 | bytes 2621440 | tf_op jit(solution)/shard_map/new_rows/pallas_call | solution.py:353
  167.8 1.9 collective-permute-start.3
  170.0 1.4 collective-permute-start.5
  171.4 2.1 collective-permute-done.7.refs_6_
  173.5 0.8 copy-done.5
  174.5 14.9 %new_rows.8 = (bf16[1056,128]{1,0:T(8,128)(2,1)}, f32[32768,128]{1,0:T(8,128)}, f32[256,128]{1,0:T(8,128)}) custom-call(s32[5]{0:T(128)} %pad_add_fusion.3.refs_0_, bf16[8192,128]{1,0:T(8,128)(2,1)} %all-gather.2.cloned.1.call-done.refs_1_, f32[1,8192]{1,0:T(1,128)} %join_stats.1.refs_2_, ...), custom_call_target="tpu_custom_call", output_to_operand_aliasing={{1}: (8, {}), {2}: (9, {})} | custom-call | flops 6442450944 | bytes 2621440 | tf_op jit(solution)/shard_map/new_rows/pallas_call | solution.py:353
  189.4 1.9 collective-permute-start.12
  191.5 1.4 collective-permute-start.14
  192.9 0.7 copy-done.14
  193.7 13.6 %new_rows.9 = (bf16[1056,128]{1,0:T(8,128)(2,1)}, f32[32768,128]{1,0:T(8,128)}, f32[256,128]{1,0:T(8,128)}) custom-call(s32[5]{0:T(128)} %pad_add_fusion.1.refs_0_, bf16[8192,128]{1,0:T(8,128)(2,1)} %all-gather.2.cloned.1.call-done.refs_1_, f32[1,8192]{1,0:T(1,128)} %join_stats.1.refs_2_, ...), custom_call_target="tpu_custom_call", output_to_operand_aliasing={{1}: (8, {}), {2}: (9, {})} | custom-call | flops 6442450944 | bytes 2621440 | tf_op jit(solution)/shard_map/new_rows/pallas_call | solution.py:353
  207.4 1.3 collective-permute-start.10
  208.6 2.1 collective-permute-start.11
  211.7 4.3 %placed_rows.2 = (f32[32768,128]{1,0:T(8,128)}, f32[256,128]{1,0:T(8,128)}) custom-call(s32[4]{0:T(128)} %get-tuple-element.28.starts_ref, bf16[1056,128]{1,0:T(8,128)(2,1)} %get-tuple-element.21.refs_0_, bf16[1056,128]{1,0:T(8,128)(2,1)} %copy-done.7, bf16[1056,128]{1,0:T(8,128)(2,1)} %copy-done.8, ...), custom_call_target="tpu_custom_call", output_to_operand_aliasing={{0}: (5, {}), {1}: (6, {})} | custom-call | tf_op jit(solution)/shard_map/placed_rows/pallas_call | solution.py:386
  216.0 4.6 %collective-permute-done.10.refs_2_ = bf16[1056,128]{1,0:T(8,128)(2,1)S(1)} collective-permute-done((bf16[1056,128]{1,0:T(8,128)(2,1)}, bf16[1056,128]{1,0:T(8,128)(2,1)S(1)}, u32[]{:S(2)}, u32[]{:S(2)}) %collective-permute-start.10) | collective-permute-done | bytes 270368 | tf_op jit(solution)/shard_map/ppermute | solution.py:436
  220.6 1.2 collective-permute-done.9.refs_1_
  221.8 0.7 copy-done.12
  222.5 4.3 %placed_rows.3 = (f32[32768,128]{1,0:T(8,128)}, f32[256,128]{1,0:T(8,128)}) custom-call(s32[4]{0:T(128)} %get-tuple-element.33.starts_ref, bf16[1056,128]{1,0:T(8,128)(2,1)} %get-tuple-element.20.refs_0_, bf16[1056,128]{1,0:T(8,128)(2,1)} %copy-done.12, bf16[1056,128]{1,0:T(8,128)(2,1)} %copy-done.10, ...), custom_call_target="tpu_custom_call", output_to_operand_aliasing={{0}: (5, {}), {1}: (6, {})} | custom-call | tf_op jit(solution)/shard_map/placed_rows/pallas_call | solution.py:386
  (52 shorter events, 6.6 us)
Async XLA Ops:
  7.2 74.8 %all-gather.2.cloned.1.call-start = ((), (), s32[]{:S(2)}) async-start(), calls=%async_computation.1 | async-start | bytes 2621440 | tf_op jit(solution)/shard_map/all_gather | solution.py:458
  64.0 15.7 %all-to-all-start = ((f32[32,1,2048]{2,1,0:T(1,128)}), f32[32,1,2048]{2,1,0:T(1,128)S(1)}, u32[]{:S(2)}, u32[]{:S(2)}) async-start(f32[32,1,2048]{2,1,0:T(1,128)} %broadcast_in_dim.9), calls=%async_computation | async-start | bytes 524288 | tf_op jit(solution)/shard_map/all_to_all | solution.py:461
  111.7 25.6 %collective-permute-start = (bf16[3168,128]{1,0:T(8,128)(2,1)}, bf16[3168,128]{1,0:T(8,128)(2,1)S(1)}, u32[]{:S(2)}, u32[]{:S(2)}) collective-permute-start(bf16[3168,128]{1,0:T(8,128)(2,1)} %new_rows.5.refs_4_), channel_id=1, source_target_pairs={{8,0},{0,8},{24,16},{16,24},{9,1},{1,9},{25,17},{17,25},{10,2},{2,... | collective-permute-start | bytes 2433032 | tf_op jit(solution)/shard_map/ppermute | solution.py:436
  112.2 38.1 %collective-permute-start.1 = (bf16[3168,128]{1,0:T(8,128)(2,1)}, bf16[3168,128]{1,0:T(8,128)(2,1)S(1)}, u32[]{:S(2)}, u32[]{:S(2)}) collective-permute-start(bf16[3168,128]{1,0:T(8,128)(2,1)} %new_rows.5.refs_4_), channel_id=1, source_target_pairs={{16,0},{24,8},{0,16},{8,24},{17,1},{25,9},{1,17},{9,25},{18,2},{26... | collective-permute-start | bytes 2433032 | tf_op jit(solution)/shard_map/ppermute | solution.py:436
  113.0 37.3 %collective-permute-start.2 = (bf16[3168,128]{1,0:T(8,128)(2,1)}, bf16[3168,128]{1,0:T(8,128)(2,1)S(1)}, u32[]{:S(2)}, u32[]{:S(2)}) collective-permute-start(bf16[3168,128]{1,0:T(8,128)(2,1)} %new_rows.5.refs_4_), channel_id=1, source_target_pairs={{24,0},{16,8},{8,16},{0,24},{25,1},{17,9},{9,17},{1,25},{26,2},{18... | collective-permute-start | bytes 2433032 | tf_op jit(solution)/shard_map/ppermute | solution.py:436
  135.9 34.1 %collective-permute-start.6 = (bf16[2112,128]{1,0:T(8,128)(2,1)}, bf16[2112,128]{1,0:T(8,128)(2,1)S(1)}, u32[]{:S(2)}, u32[]{:S(2)}) collective-permute-start(bf16[2112,128]{1,0:T(8,128)(2,1)} %new_rows.7.refs_4_), channel_id=1, source_target_pairs={{8,0},{0,8},{24,16},{16,24},{9,1},{1,9},{25,17},{17,25},{10,2},{2,... | collective-permute-start | bytes 1622024 | tf_op jit(solution)/shard_map/ppermute | solution.py:436
  136.4 37.1 %collective-permute-start.7 = (bf16[2112,128]{1,0:T(8,128)(2,1)}, bf16[2112,128]{1,0:T(8,128)(2,1)S(1)}, u32[]{:S(2)}, u32[]{:S(2)}) collective-permute-start(bf16[2112,128]{1,0:T(8,128)(2,1)} %new_rows.7.refs_4_), channel_id=1, source_target_pairs={{16,0},{24,8},{0,16},{8,24},{17,1},{25,9},{1,17},{9,25},{18,2},{26... | collective-permute-start | bytes 1622024 | tf_op jit(solution)/shard_map/ppermute | solution.py:436
  137.2 13.1 %copy-start.1 = (bf16[3168,128]{1,0:T(8,128)(2,1)}, bf16[3168,128]{1,0:T(8,128)(2,1)S(1)}, u32[]{:S(2)}) copy-start(bf16[3168,128]{1,0:T(8,128)(2,1)S(1)} %collective-permute-done.refs_5_) | copy-start | bytes 2433028
  137.2 36.2 %collective-permute-start.8 = (bf16[2112,128]{1,0:T(8,128)(2,1)}, bf16[2112,128]{1,0:T(8,128)(2,1)S(1)}, u32[]{:S(2)}, u32[]{:S(2)}) collective-permute-start(bf16[2112,128]{1,0:T(8,128)(2,1)} %new_rows.7.refs_4_), channel_id=1, source_target_pairs={{24,0},{16,8},{8,16},{0,24},{25,1},{17,9},{9,17},{1,25},{26,2},{18... | collective-permute-start | bytes 1622024 | tf_op jit(solution)/shard_map/ppermute | solution.py:436
  150.3 0.9 copy-start.2
  151.2 0.9 copy-start.3
  167.8 23.6 %collective-permute-start.3 = (bf16[1056,128]{1,0:T(8,128)(2,1)}, bf16[1056,128]{1,0:T(8,128)(2,1)S(1)}, u32[]{:S(2)}, u32[]{:S(2)}) collective-permute-start(bf16[1056,128]{1,0:T(8,128)(2,1)} %get-tuple-element.15.refs_4_), channel_id=1, source_target_pairs={{8,0},{0,8},{24,16},{16,24},{9,1},{1,9},{25,17},{17,25},{10,2},{2,... | collective-permute-start | bytes 811016 | tf_op jit(solution)/shard_map/ppermute | solution.py:436
  169.7 23.2 %collective-permute-start.4 = (bf16[1056,128]{1,0:T(8,128)(2,1)}, bf16[1056,128]{1,0:T(8,128)(2,1)S(1)}, u32[]{:S(2)}, u32[]{:S(2)}) collective-permute-start(bf16[1056,128]{1,0:T(8,128)(2,1)} %get-tuple-element.15.refs_4_), channel_id=1, source_target_pairs={{16,0},{24,8},{0,16},{8,24},{17,1},{25,9},{1,17},{9,25},{18,2},{26... | collective-permute-start | bytes 811016 | tf_op jit(solution)/shard_map/ppermute | solution.py:436
  170.0 3.5 %copy-start.4 = (bf16[2112,128]{1,0:T(8,128)(2,1)}, bf16[2112,128]{1,0:T(8,128)(2,1)S(1)}, u32[]{:S(2)}) copy-start(bf16[2112,128]{1,0:T(8,128)(2,1)S(1)} %collective-permute-done.6.refs_5_) | copy-start | bytes 1622020
  170.0 22.9 %collective-permute-start.5 = (bf16[1056,128]{1,0:T(8,128)(2,1)}, bf16[1056,128]{1,0:T(8,128)(2,1)S(1)}, u32[]{:S(2)}, u32[]{:S(2)}) collective-permute-start(bf16[1056,128]{1,0:T(8,128)(2,1)} %get-tuple-element.15.refs_4_), channel_id=1, source_target_pairs={{24,0},{16,8},{8,16},{0,24},{25,1},{17,9},{9,17},{1,25},{26,2},{18... | collective-permute-start | bytes 811016 | tf_op jit(solution)/shard_map/ppermute | solution.py:436
  173.5 0.8 copy-start.5
  173.5 1.0 copy-start.6
  189.4 21.3 %collective-permute-start.12 = (bf16[1056,128]{1,0:T(8,128)(2,1)}, bf16[1056,128]{1,0:T(8,128)(2,1)S(1)}, u32[]{:S(2)}, u32[]{:S(2)}) collective-permute-start(bf16[1056,128]{1,0:T(8,128)(2,1)} %get-tuple-element.21.refs_0_), channel_id=1, source_target_pairs={{8,0},{0,8},{24,16},{16,24},{9,1},{1,9},{25,17},{17,25},{10,2},{2,... | collective-permute-start | bytes 811016 | tf_op jit(solution)/shard_map/ppermute | solution.py:436
  191.2 19.7 %collective-permute-start.13 = (bf16[1056,128]{1,0:T(8,128)(2,1)}, bf16[1056,128]{1,0:T(8,128)(2,1)S(1)}, u32[]{:S(2)}, u32[]{:S(2)}) collective-permute-start(bf16[1056,128]{1,0:T(8,128)(2,1)} %get-tuple-element.21.refs_0_), channel_id=1, source_target_pairs={{16,0},{24,8},{0,16},{8,24},{17,1},{25,9},{1,17},{9,25},{18,2},{26... | collective-permute-start | bytes 811016 | tf_op jit(solution)/shard_map/ppermute | solution.py:436
  191.5 1.5 copy-start.13
  191.5 19.4 %collective-permute-start.14 = (bf16[1056,128]{1,0:T(8,128)(2,1)}, bf16[1056,128]{1,0:T(8,128)(2,1)S(1)}, u32[]{:S(2)}, u32[]{:S(2)}) collective-permute-start(bf16[1056,128]{1,0:T(8,128)(2,1)} %get-tuple-element.21.refs_0_), channel_id=1, source_target_pairs={{24,0},{16,8},{8,16},{0,24},{25,1},{17,9},{9,17},{1,25},{26,2},{18... | collective-permute-start | bytes 811016 | tf_op jit(solution)/shard_map/ppermute | solution.py:436
  192.9 0.7 copy-start.14
  192.9 0.8 copy-start.15
  207.4 13.2 %collective-permute-start.10 = (bf16[1056,128]{1,0:T(8,128)(2,1)}, bf16[1056,128]{1,0:T(8,128)(2,1)S(1)}, u32[]{:S(2)}, u32[]{:S(2)}) collective-permute-start(bf16[1056,128]{1,0:T(8,128)(2,1)} %get-tuple-element.20.refs_0_), channel_id=1, source_target_pairs={{16,0},{24,8},{0,16},{8,24},{17,1},{25,9},{1,17},{9,25},{18,2},{26... | collective-permute-start | bytes 811016 | tf_op jit(solution)/shard_map/ppermute | solution.py:436
  208.6 12.0 %collective-permute-start.11 = (bf16[1056,128]{1,0:T(8,128)(2,1)}, bf16[1056,128]{1,0:T(8,128)(2,1)S(1)}, u32[]{:S(2)}, u32[]{:S(2)}) collective-permute-start(bf16[1056,128]{1,0:T(8,128)(2,1)} %get-tuple-element.20.refs_0_), channel_id=1, source_target_pairs={{24,0},{16,8},{8,16},{0,24},{25,1},{17,9},{9,17},{1,25},{26,2},{18... | collective-permute-start | bytes 811016 | tf_op jit(solution)/shard_map/ppermute | solution.py:436
  210.7 0.7 copy-start.7
  210.7 11.1 %collective-permute-start.9 = (bf16[1056,128]{1,0:T(8,128)(2,1)}, bf16[1056,128]{1,0:T(8,128)(2,1)S(1)}, u32[]{:S(2)}, u32[]{:S(2)}) collective-permute-start(bf16[1056,128]{1,0:T(8,128)(2,1)} %get-tuple-element.20.refs_0_), channel_id=1, source_target_pairs={{8,0},{0,8},{24,16},{16,24},{9,1},{1,9},{25,17},{17,25},{10,2},{2,... | collective-permute-start | bytes 811016 | tf_op jit(solution)/shard_map/ppermute | solution.py:436
  210.9 0.7 copy-start.8
  210.9 0.8 copy-start.9
  220.6 1.2 copy-start.10
  220.6 1.2 copy-start.11
  221.8 0.7 copy-start.12
  (1 other events, 0.7 us)
Sparse Core Ops, SparseCore 0:
  9.8 38.0 all-gather.1
